TPU v7x, 128 devices: a whole 4x4x4 slice. The times are simulated.
128 devices in a mesh: feed: 8 (over y, core), freq: 16 (over x, z).
Axes of the slice: x: 4, y: 4, z: 4, core: 2. Of those that a mesh axis runs over, the one named last changes fastest.
Arguments:
- volts: bfloat16 [2048, 393216], P('feed', 'freq'), may hold values from -6 to 6
- beam_weights: bfloat16 [2, 1024, 2048], P(None, None, 'feed'), may hold values from -0.125 to 0.125
- allocation: int32 [16, 3], replicated, may hold values from -1 to 31, as said below
- beam_order: int32 [1024], replicated, may hold values from 0 to 1023, each once
Outputs:
- visibility: float32 [48, 2, 2048, 2048], P('freq', None, 'feed')
- beam_power: float32 [1024, 48], P('feed', 'freq')
Inputs may be any that keep to these rules, and one draw needn't show every extreme that they name: `allocation`: row j lists owner j's channels in slots 0 up to its count and -1 in the slots after; every channel of 0 to 31 appears exactly once; every owner holds 1 to 3 channels and some owner holds 3. `beam_order`: each beam appears once.
All inputs are finite; a program needn't handle non-finite values.
Results may differ from a plain program's by a relative error of at most 0.0038.
Values may be sent and summed in bfloat16 or wider, within the bound.
No kernel may reach another device: no remote copies, remote signals or barrier semaphores. Data moves between devices by JAX's collectives and lax.ppermute only.
A program may use at most 128 MiB of HBM per device.

v0:
```python
import math

import jax
import jax.numpy as jnp
from jax import lax
from jax.sharding import PartitionSpec as P

NFFT = 2048
TAPS = 4


def from_behind(x, axis, by):
    devices = lax.axis_size(axis)
    pairs = [(i, i + by) for i in range(devices) if 0 <= i + by < devices]
    return lax.ppermute(x, axis, pairs)


def window_taps():
    length = TAPS * NFFT
    positions = jnp.arange(length, dtype=jnp.float32)
    centred = (positions - 0.5 * length + 0.5) / NFFT
    hann_taper = 0.5 - 0.5 * jnp.cos(2.0 * math.pi * (positions + 0.5) / length)
    coeffs = jnp.sinc(centred) * hann_taper
    coeffs = coeffs * jnp.sqrt(NFFT / jnp.sum(coeffs * coeffs))
    return coeffs.reshape(TAPS, NFFT)


def dft_rows(channels):
    bin_index = jnp.arange(channels, dtype=jnp.int32)
    sample_index = jnp.arange(NFFT, dtype=jnp.int32)
    angles = (bin_index[:, None] * sample_index[None, :] % NFFT).astype(jnp.float32) * (
        2.0 * math.pi / NFFT
    )
    rows_both = jnp.stack([jnp.cos(angles), -jnp.sin(angles)], axis=1) / math.sqrt(NFFT)
    return rows_both.reshape(2 * channels, NFFT)


def complex_stack(weight_pair):
    return jnp.stack(
        [jnp.stack([weight_pair[0], -weight_pair[1]]), jnp.stack([weight_pair[1], weight_pair[0]])]
    )


def pairing(own_rows):
    turned = jnp.stack([own_rows[:, 1], -own_rows[:, 0]], axis=1)
    return jnp.stack([own_rows, turned])


def accumulate(paired, columns):
    product = jnp.einsum("psctf,sctg->spfg", paired, columns, preferred_element_type=jnp.float32)
    return (product,)


def tap_sum(framed, coeffs, frames_dev):
    summed = jnp.zeros((framed.shape[0], frames_dev, NFFT), jnp.float32)
    for tap_index in range(TAPS):
        summed = summed + coeffs[tap_index] * framed[:, tap_index : tap_index + frames_dev].astype(
            jnp.float32
        )
    return summed


def shards(volts, beam_weights, allocation, beam_order):
    feeds_dev = volts.shape[0]
    frames_dev = volts.shape[1] // NFFT
    owners = lax.axis_size("freq")
    total_frames = frames_dev * owners
    slots_dev = allocation.shape[1]
    channels = (slots_dev - 1) * allocation.shape[0]
    coeffs = window_taps()
    transform = dft_rows(channels)
    own_frames = volts.reshape(feeds_dev, frames_dev, NFFT)
    history = from_behind(volts[:, volts.shape[1] - (TAPS - 1) * NFFT :], "freq", 1)
    framed = jnp.concatenate([history.reshape(feeds_dev, TAPS - 1, NFFT), own_frames], axis=1)
    summed = tap_sum(framed, coeffs, frames_dev)
    result = lax.dot_general(
        transform,
        summed,
        (((1,), (2,)), ((), ())),
        precision=lax.Precision.HIGHEST,
        preferred_element_type=jnp.float32,
    )
    spectra = (
        result.reshape(channels, 2, feeds_dev, frames_dev)
        .transpose(0, 1, 3, 2)
        .astype(jnp.bfloat16)
    )
    slot_list = allocation.reshape(-1)
    selector = slot_list[:, None] == jnp.arange(channels, dtype=jnp.int32)[None, :]
    weights_ord = jnp.take(beam_weights, beam_order, axis=1)
    beam_share = weights_ord.shape[1] // lax.axis_size("feed")
    stacked = complex_stack(weights_ord)
    voltage = jnp.einsum("ocbf,kctf->bokt", stacked, spectra, preferred_element_type=jnp.float32)
    summed_beams = lax.psum_scatter(
        voltage.reshape(lax.axis_size("feed") * beam_share, -1).astype(jnp.bfloat16),
        "feed",
        scatter_dimension=0,
        tiled=True,
    ).astype(jnp.float32)
    voltage = summed_beams.reshape(beam_share, 2, channels, frames_dev)
    beam_energy = jnp.sum(voltage * voltage, axis=(1, 3)) / total_frames
    slotted = jnp.dot(
        beam_energy,
        selector.astype(jnp.float32).T,
        precision=lax.Precision.HIGHEST,
        preferred_element_type=jnp.float32,
    )
    beam_out = lax.psum_scatter(slotted, "freq", scatter_dimension=1, tiled=True)
    outgoing = jnp.einsum(
        "qk,kctf->qctf", selector.astype(jnp.bfloat16), spectra, preferred_element_type=jnp.float32
    ).astype(jnp.bfloat16)
    own_rows = lax.all_to_all(outgoing, "freq", split_axis=0, concat_axis=2, tiled=True)
    totals = accumulate(pairing(own_rows), lax.all_gather(own_rows, "feed", axis=3, tiled=True))
    visibility = totals[0] / total_frames
    return (visibility, beam_out)


def solution(mesh):
    in_specs = (P("feed", "freq"), P(None, None, "feed"), P(), P())
    out_specs = (P("freq", None, "feed", None), P("feed", "freq"))
    return jax.shard_map(shards, mesh=mesh, in_specs=in_specs, out_specs=out_specs, check_vma=False)
```

profile of v0, /device:TPU:0, one launch (start us, length us, event | category | flops | bytes accessed | tf_op | source)
XLA Modules:
  0.0 262.3 jit_solution(11414782384417409893)
XLA Ops:
  7.2 16.7 %copy.42 = bf16[256,24576]{0,1:T(8,128)(2,1)} copy(bf16[256,24576]{1,0:T(8,128)(2,1)} %param.4) | data formatting | bytes 25165824 | tf_op args[0]
  23.9 3.7 %slice.57 = bf16[256,6144]{0,1:T(8,128)(2,1)} slice(bf16[256,24576]{0,1:T(8,128)(2,1)} %copy.42), slice={[0:256], [18432:24576]} | slice | bytes 6291456 | tf_op jit(solution)/shard_map/slice | solution.py:73
  27.6 5.6 %collective-permute-start = (bf16[256,6144]{0,1:T(8,128)(2,1)}, bf16[256,6144]{0,1:T(8,128)(2,1)}, u32[]{:S(2)}, u32[]{:S(2)}) collective-permute-start(bf16[256,6144]{0,1:T(8,128)(2,1)} %slice.57), channel_id=1, source_target_pairs={{0,1},{1,2},{2,3},{3,4},{4,5},{5,6},{6,7},{7,8},{8,9},{9,10},{10,1... | collective-permute-start | bytes 9437192 | tf_op jit(solution)/shard_map/ppermute | solution.py:15
  33.2 0.8 multiply_reduce_fusion
  34.7 5.3 %gather_fusion = bf16[1024,2,256]{2,0,1:T(8,128)(2,1)S(1)} fusion(bf16[2,1024,256]{2,1,0:T(8,128)(2,1)S(1)} %copy-done, s32[1024]{0:T(1024)S(1)} %fusion.83), kind=kCustom, calls=%fused_computation | custom fusion | bytes 2101248 | tf_op jit(solution)/shard_map/jit(_take)/gather | solution.py:90
  40.8 1.0 sine_negate_fusion
  41.8 57.4 %collective-permute-done = bf16[256,6144]{0,1:T(8,128)(2,1)} collective-permute-done((bf16[256,6144]{0,1:T(8,128)(2,1)}, bf16[256,6144]{0,1:T(8,128)(2,1)}, u32[]{:S(2)}, u32[]{:S(2)}) %collective-permute-start) | collective-permute-done | bytes 3145760 | tf_op jit(solution)/shard_map/ppermute | solution.py:15
  99.2 28.9 %fusion.27 = bf16[32,2,256,12]{2,0,3,1:T(8,128)(2,1)S(1)} fusion(bf16[256,12,2048]{0,2,1:T(8,128)(2,1)} %bitcast.66, bf16[256,3,2048]{0,2,1:T(8,128)(2,1)} %bitcast.4, f32[2048]{0:T(1024)S(1)} %get-tuple-element.10, f32[2048]{0:T(1024)S(1)} %get-tuple-element.11, f32[2048]{0:T(1024)S(1)} %get-tuple-element.12, f32[2048]{0:T(1024)S(1)} %get-tuple-element.9, ...), kind=kOutput, calls=%fused_computation.35 | convolution fusion | flops 4958126080 | bytes 16678912 | tf_op jit(solution)/shard_map/dot_general | solution.py:76
  128.1 1.0 fusion.26
  129.1 0.9 copy.53
  130.0 1.3 convert_element_type.66
  131.3 2.6 copy.64
  134.2 0.4 convolution_convert_fusion
  134.6 0.6 copy.45
  135.2 19.6 %all_to_all.18 = bf16[48,2,12,256]{3,1,2,0:T(2,128)(2,1)S(1)} all-to-all(bf16[48,2,12,256]{3,1,2,0:T(2,128)(2,1)S(1)} %copy.45), channel_id=1, replica_groups=mesh['feed'=8,'freq'=16] {'freq'}, dimensions={0} | all-to-all | bytes 1179648 | tf_op jit(solution)/shard_map/all_to_all | solution.py:112
  154.8 0.4 copy.46
  155.2 0.9 copy.48
  156.1 0.6 dynamic-slice
  157.4 1.1 fusion.90
  158.6 11.3 %reduce-scatter.4.cloned.1.call-done = bf16[128,768]{1,0:T(8,128)(2,1)} async-done(((bf16[1024,768]{1,0:T(8,128)(2,1)}), bf16[128,768]{1,0:T(8,128)(2,1)}) %reduce-scatter.4.cloned.1.call-update) | async-done | bytes 196624
  169.9 1.1 copy.65
  171.4 74.5 %all-reduce = f32[128,48]{0,1:T(8,128)S(1)} all-reduce(f32[128,48]{0,1:T(8,128)S(1)} %fusion.76), channel_id=3, replica_groups=mesh['feed'=8,'freq'=16] {'freq'}, use_global_device_ids=true, to_apply=%region_3.4.clone | all-reduce | flops 6144 | bytes 49152
  245.9 0.6 constant_dynamic-slice_fusion
  246.5 9.0 %bitcast_multiply_fusion = f32[3,2,256,2048]{3,2,1,0:T(8,128)} fusion(bf16[3,2,192,2048]{3,2,1,0:T(8,128)(2,1)} %all-gather.2.cloned.1.call-done, bf16[1,3,2,192,256]{4,3,2,0,1:T(8,128)(2,1)S(1)} %maximum_bitcast_fusion.8, bf16[1,3,2,192,256]{4,3,2,0,1:T(8,128)(2,1)S(1)} %copy.50), kind=kOutput, calls=%fused_computation.22 | convolution fusion | flops 2419654656 | bytes 18481152 | tf_op jit(solution)/shard_map/psctf,sctg->spfg/dot_general | solution.py:50
  (30 shorter events, 1.5 us)
Async XLA Ops:
  7.2 27.6 %copy-start = (bf16[2,1024,256]{2,1,0:T(8,128)(2,1)S(1)}, bf16[2,1024,256]{2,1,0:T(8,128)(2,1)}, u32[]{:S(2)}) copy-start(bf16[2,1024,256]{2,1,0:T(8,128)(2,1)} %param.5) | copy-start | bytes 3145732
  7.2 27.5 %copy-start.2 = (s32[1024]{0:T(1024)S(1)}, s32[1024]{0:T(1024)}, u32[]{:S(2)}) copy-start(s32[1024]{0:T(1024)} %param.7) | copy-start | bytes 12292
  7.2 162.8 %reduce-scatter.4.cloned.1.call-start = ((), (), s32[]{:S(2)}) async-start(), calls=%async_computation.3 | async-start | bytes 1769472
  27.6 71.6 %collective-permute-start = (bf16[256,6144]{0,1:T(8,128)(2,1)}, bf16[256,6144]{0,1:T(8,128)(2,1)}, u32[]{:S(2)}, u32[]{:S(2)}) collective-permute-start(bf16[256,6144]{0,1:T(8,128)(2,1)} %slice.57), channel_id=1, source_target_pairs={{0,1},{1,2},{2,3},{3,4},{4,5},{5,6},{6,7},{7,8},{8,9},{9,10},{10,1... | collective-permute-start | bytes 9437192 | tf_op jit(solution)/shard_map/ppermute | solution.py:15
  128.1 5.9 %copy-start.3 = (s32[16,3]{0,1:T(4,128)S(1)}, s32[16,3]{0,1:T(4,128)}, u32[]{:S(2)}) copy-start(s32[16,3]{0,1:T(4,128)} %param.6) | copy-start | bytes 580
  128.1 28.0 %copy-start.4 = (u32[128]{0:T(128)S(1)}, u32[128]{0:T(128)}, u32[]{:S(2)}) copy-start(u32[128]{0:T(128)} %constant.97) | copy-start | bytes 1540
  134.0 112.5 %all-gather.2.cloned.1.call-start = ((), (), s32[]{:S(2)}) async-start(), calls=%async_computation.2 | async-start | bytes 5308416 | tf_op jit(solution)/shard_map/all_gather | solution.py:113
  156.1 99.4 %copy-start.1 = (bf16[2,1024,256]{2,1,0:T(8,128)(2,1)S(1)}, bf16[2,1024,256]{2,1,0:T(8,128)(2,1)}, u32[]{:S(2)}) copy-start(bf16[2,1024,256]{2,1,0:T(8,128)(2,1)} %param.5) | copy-start | bytes 3145732
Sparse Core Ops, SparseCore 0:
  134.1 35.8 reduce-scatter.3
  172.2 36.9 all-gather.1
where the time goes:
time: 263 us; the launch traced here: 262 us
  blocking collectives  94.1 us (36%)
  waiting for transfers between devices  68.8 us (26%)
  matrix products  39.5 us (15%)
  local copies, waits for them, and re-layouts  35 us (13%)
  between operations  15.7 us (6%)
  starting transfers between devices  5.65 us (2%)
  other arithmetic  3.75 us (1%)
    unnamed x1, blocking collectives  74.5 us
    ppermute x1, waiting for transfers between devices, from_behind(): return lax.ppermute(x, axis, pairs)  57.4 us
    dot_general x1, matrix products, shards(): lax.dot_general(transform, summed, (((1,), (2,)), ((), ())), precision=la...  28.9 us
    unnamed x16, local copies, waits for them, and re-layouts  21.6 us
    all_to_all x1, blocking collectives, shards(): lax.all_to_all(outgoing, 'freq', split_axis=0, concat_axis=2, tiled=True)  19.6 us
    unnamed x3, waiting for transfers between devices  11.4 us
    dot_general x1, matrix products, accumulate(): jnp.einsum('psctf,sctg->spfg', paired, columns, preferred_element_type=jn...  9.01 us
    ppermute x1, starting transfers between devices, from_behind(): return lax.ppermute(x, axis, pairs)  5.57 us
  transfers between devices with their start and end apart: 3, of which 2 were waited for; matrix products, arithmetic and copies ran while one was open for 5% of the time, Pallas kernels for 0%

commit v1 on v0

v1 whole, which is shorter than its diff:
```python
import functools
import math

import jax
import jax.numpy as jnp
import ml_dtypes
import numpy as np
from jax import lax
from jax.experimental import pallas as pl
from jax.experimental.pallas import tpu as pltpu
from jax.sharding import PartitionSpec as P

NFFT = 2048
TAPS = 4
VMEM = 48 * 1024 * 1024
NT = (((1,), (1,)), ((), ()))


def tap_transform(channels):
    length = TAPS * NFFT
    positions = np.arange(length, dtype=np.float64)
    coeffs = np.sinc((positions - 0.5 * length + 0.5) / NFFT)
    coeffs = coeffs * (0.5 - 0.5 * np.cos(2.0 * math.pi * (positions + 0.5) / length))
    coeffs = coeffs * np.sqrt(NFFT / np.sum(coeffs * coeffs))
    coeffs = coeffs.reshape(TAPS, NFFT)
    angles = (np.arange(channels)[:, None] * np.arange(NFFT)[None, :] % NFFT) * (2.0 * math.pi / NFFT)
    rows = np.stack([np.cos(angles), -np.sin(angles)], axis=1) / math.sqrt(NFFT)
    rows = rows.reshape(2 * channels, NFFT)
    full = (coeffs[:, None, :] * rows[None]).reshape(TAPS * 2 * channels, NFFT)
    high = full.astype(ml_dtypes.bfloat16)
    low = (full - high.astype(np.float64)).astype(ml_dtypes.bfloat16)
    return np.concatenate([high, low], axis=0)


def frame_products(table_ref, volts_ref, rows):
    product = lax.dot_general(
        table_ref[...], volts_ref[...], NT, preferred_element_type=jnp.float32
    )
    half = product.shape[0] // 2
    product = product[:half] + product[half:]
    return [product[tap * rows : (tap + 1) * rows] for tap in range(TAPS)]


def last_frames_kernel(table_ref, volts_ref, total_ref):
    step = pl.program_id(0)
    rows = total_ref.shape[1]

    @pl.when(step == 0)
    def _():
        total_ref[...] = jnp.zeros_like(total_ref)

    parts = frame_products(table_ref, volts_ref, rows)
    for tap in range(TAPS):
        at = step + TAPS - 1 - tap
        total_ref[at] = total_ref[at] + parts[tap]


def first_frames_kernel(table_ref, volts_ref, last_ref, target_ref, total_ref, select_ref):
    step = pl.program_id(0)
    rows = total_ref.shape[1]
    done = total_ref.shape[0] - (TAPS - 1)

    @pl.when(step == 0)
    def _():
        total_ref[:done] = jnp.zeros((done,) + total_ref.shape[1:], jnp.float32)
        total_ref[done:] = last_ref[...]

    parts = frame_products(table_ref, volts_ref, rows)
    for tap in range(TAPS):
        at = step + TAPS - 1 - tap
        total_ref[at] = total_ref[at] + parts[tap]
    place = lax.broadcasted_iota(jnp.int32, select_ref.shape, 1)
    select_ref[...] = jnp.where(place == target_ref[...], 1.0, 0.0).astype(jnp.bfloat16)


def choose_kernel(total_ref, carry_ref, select_ref, out_ref):
    ahead = carry_ref.shape[0]
    head = (total_ref[:ahead] + carry_ref[...]).astype(jnp.bfloat16)
    tail = total_ref[ahead:].astype(jnp.bfloat16)
    spectra = jnp.concatenate([head, tail], axis=0)
    out_ref[...] = jnp.dot(
        select_ref[...], spectra, preferred_element_type=jnp.float32
    ).astype(jnp.bfloat16)


def order_kernel(order_ref, weights_ref, out_ref):
    beams = weights_ref.shape[1]
    share = out_ref.shape[2]
    place = lax.broadcasted_iota(jnp.int32, (share, beams), 1)
    hot = jnp.where(place == order_ref[...], 1.0, 0.0).astype(jnp.bfloat16)
    for part in range(2):
        out_ref[0, part] = jnp.dot(
            hot, weights_ref[part], preferred_element_type=jnp.float32
        ).astype(jnp.bfloat16)


def swap_parts(values, half, sign):
    lanes = values.shape[1]
    lane = lax.broadcasted_iota(jnp.int32, values.shape, 1)
    ahead = pltpu.roll(values, lanes - half, 1)
    behind = pltpu.roll(values, half, 1)
    return jnp.where(lane % (2 * half) < half, sign * ahead, -sign * behind)


def pair_kernel(first, final, half, scale, where_ref, *refs):
    refs = list(refs)
    if first:
        own_ref, other_ref, weight_a_ref, weight_b_ref = refs[:4]
        vis_ref, left_ref, voltage_ref = refs[4:7]
        own = own_ref[0].astype(jnp.float32).T
        left = jnp.concatenate([own, swap_parts(own, half, 1.0)], axis=0).astype(jnp.bfloat16)
        left_ref[0] = left
    else:
        own_ref, other_ref, weight_a_ref, weight_b_ref, left_ref, before_ref, _ = refs[:7]
        vis_ref = refs[7]
        left = left_ref[0]
    core = where_ref[1]
    width = own_ref.shape[2]
    voltage = None
    for ref, weight_ref, at in (
        (own_ref, weight_a_ref, core),
        (other_ref, weight_b_ref, 1 - core),
    ):
        product = jnp.dot(left, ref[0], preferred_element_type=jnp.float32) * scale
        columns = pl.ds(pl.multiple_of(at * width, width), width)
        vis_ref[0, 0, :, columns] = product[: product.shape[0] // 2]
        vis_ref[0, 1, :, columns] = product[product.shape[0] // 2 :]
        beams = weight_ref.shape[1] * weight_ref.shape[2]
        term = lax.dot_general(
            weight_ref[0].reshape(beams, width), ref[0], NT, preferred_element_type=jnp.float32
        )
        voltage = term if voltage is None else voltage + term
    if first:
        voltage_ref[0] = voltage
        return
    voltage = voltage + before_ref[0]
    if not final:
        refs[8][0] = voltage
        return
    power_ref = refs[8]
    share = voltage.shape[0] // 2
    beam = voltage[:share] - swap_parts(voltage[share:], half, 1.0)
    power = jnp.sum(beam * beam, axis=1, keepdims=True) * scale
    slot = lax.broadcasted_iota(jnp.int32, power_ref.shape, 1)
    power_ref[...] = jnp.where(slot == pl.program_id(0), power, power_ref[...])


def params():
    return pltpu.CompilerParams(vmem_limit_bytes=VMEM)


def pair_call(kind, half, scale, where, own, other, weights, left=None, voltage=None, vis=None):
    slots, rows, width = own.shape
    devices, parts, share, _ = weights.shape
    block = lambda shape, at: pl.BlockSpec(shape, at)
    per_slot = lambda *shape: block((1,) + shape, lambda s, w: (s,) + (0,) * len(shape))
    in_specs = [
        per_slot(rows, width),
        per_slot(rows, width),
        block((1, parts, share, width), lambda s, w: (2 * w[0] + w[1], 0, 0, 0)),
        block((1, parts, share, width), lambda s, w: (2 * w[0] + 1 - w[1], 0, 0, 0)),
    ]
    args = [own, other, weights, weights]
    vis_shape = jax.ShapeDtypeStruct((slots, 2, width, devices * width), jnp.float32)
    vis_spec = block((1, 2, width, 2 * width), lambda s, w: (s, 0, 0, w[0]))
    voltage_shape = jax.ShapeDtypeStruct((slots, parts * share, rows), jnp.float32)
    left_shape = jax.ShapeDtypeStruct((slots, 2 * width, rows), jnp.bfloat16)
    power_shape = jax.ShapeDtypeStruct((share, slots), jnp.float32)
    aliases = {}
    if kind == "first":
        out_shape = [vis_shape, left_shape, voltage_shape]
        out_specs = [vis_spec, per_slot(2 * width, rows), per_slot(parts * share, rows)]
    else:
        in_specs += [
            per_slot(2 * width, rows),
            per_slot(parts * share, rows),
            pl.BlockSpec(memory_space=pl.ANY),
        ]
        args += [left, voltage, vis]
        aliases = {7: 0}
        if kind == "final":
            out_shape = [vis_shape, power_shape]
            out_specs = [vis_spec, block((share, slots), lambda s, w: (0, 0))]
        else:
            out_shape = [vis_shape, voltage_shape]
            out_specs = [vis_spec, per_slot(parts * share, rows)]
    flops = 2 * slots * rows * width * 2 * (2 * width + parts * share)
    moved = slots * 2 * width * 2 * width * 4 + 6 * slots * rows * width
    return pl.pallas_call(
        functools.partial(pair_kernel, kind == "first", kind == "final", half, scale),
        out_shape=out_shape,
        grid_spec=pltpu.PrefetchScalarGridSpec(
            num_scalar_prefetch=1, grid=(slots,), in_specs=in_specs, out_specs=out_specs
        ),
        input_output_aliases=aliases,
        compiler_params=params(),
        cost_estimate=pl.CostEstimate(flops=flops, bytes_accessed=moved, transcendentals=0),
    )(where, *args)


def shards(volts, beam_weights, allocation, beam_order):
    feeds_dev = volts.shape[0]
    frames_dev = volts.shape[1] // NFFT
    owners = lax.axis_size("freq")
    devices = lax.axis_size("feed")
    total_frames = frames_dev * owners
    slots_dev = allocation.shape[1]
    channels = (slots_dev - 1) * allocation.shape[0]
    rows = 2 * channels
    late = TAPS - 1
    early = frames_dev - late
    beams = beam_weights.shape[1]
    share = beams // devices
    f32, bf16 = jnp.float32, jnp.bfloat16
    table = jnp.asarray(tap_transform(channels))
    table_spec = pl.BlockSpec(table.shape, lambda i: (0, 0))
    frame_flops = 2 * table.shape[0] * feeds_dev * NFFT

    last = pl.pallas_call(
        last_frames_kernel,
        out_shape=jax.ShapeDtypeStruct((2 * late, rows, feeds_dev), f32),
        grid=(late,),
        in_specs=[table_spec, pl.BlockSpec((feeds_dev, NFFT), lambda i: (0, early + i))],
        out_specs=pl.BlockSpec((2 * late, rows, feeds_dev), lambda i: (0, 0, 0)),
        compiler_params=params(),
        cost_estimate=pl.CostEstimate(
            flops=late * frame_flops, bytes_accessed=late * feeds_dev * NFFT * 2, transcendentals=0
        ),
    )(table, volts)
    carry = lax.ppermute(last[late:], "freq", [(i, i + 1) for i in range(owners - 1)])

    ordered = pl.pallas_call(
        order_kernel,
        out_shape=jax.ShapeDtypeStruct((devices, 2, share, feeds_dev), bf16),
        grid=(devices,),
        in_specs=[
            pl.BlockSpec((share, 1), lambda i: (i, 0)),
            pl.BlockSpec(beam_weights.shape, lambda i: (0, 0, 0)),
        ],
        out_specs=pl.BlockSpec((1, 2, share, feeds_dev), lambda i: (i, 0, 0, 0)),
        compiler_params=params(),
        cost_estimate=pl.CostEstimate(
            flops=4 * beams * beams * feeds_dev, bytes_accessed=4 * beams * feeds_dev, transcendentals=0
        ),
    )(beam_order.reshape(beams, 1), beam_weights)
    weights = lax.all_to_all(ordered, "feed", split_axis=0, concat_axis=0, tiled=True)

    slot_list = allocation.reshape(-1)
    slots = slot_list.shape[0]
    chosen_rows = slots * 2 * frames_dev
    target = (
        jnp.arange(frames_dev, dtype=jnp.int32)[None, None, :] * rows
        + jnp.arange(2, dtype=jnp.int32)[None, :, None]
        + 2 * slot_list[:, None, None]
    )
    target = jnp.where(slot_list[:, None, None] >= 0, target, -1).reshape(chosen_rows, 1)
    per_step = chosen_rows // early
    total, select = pl.pallas_call(
        first_frames_kernel,
        out_shape=[
            jax.ShapeDtypeStruct((frames_dev, rows, feeds_dev), f32),
            jax.ShapeDtypeStruct((chosen_rows, frames_dev * rows), bf16),
        ],
        grid=(early,),
        in_specs=[
            table_spec,
            pl.BlockSpec((feeds_dev, NFFT), lambda i: (0, i)),
            pl.BlockSpec((late, rows, feeds_dev), lambda i: (0, 0, 0)),
            pl.BlockSpec((per_step, 1), lambda i: (i, 0)),
        ],
        out_specs=[
            pl.BlockSpec((frames_dev, rows, feeds_dev), lambda i: (0, 0, 0)),
            pl.BlockSpec((per_step, frames_dev * rows), lambda i: (i, 0)),
        ],
        compiler_params=params(),
        cost_estimate=pl.CostEstimate(
            flops=early * frame_flops, bytes_accessed=early * feeds_dev * NFFT * 2, transcendentals=0
        ),
    )(table, volts, last, target)

    outgoing = pl.pallas_call(
        choose_kernel,
        out_shape=jax.ShapeDtypeStruct((chosen_rows, feeds_dev), bf16),
        compiler_params=params(),
    )(
        total.reshape(frames_dev * rows, feeds_dev), carry.reshape(late * rows, feeds_dev), select
    )
    received = lax.all_to_all(
        outgoing.reshape(owners, slots_dev, 2 * frames_dev, feeds_dev),
        "freq",
        split_axis=0,
        concat_axis=0,
        tiled=True,
    )
    own = received.transpose(1, 0, 2, 3).reshape(slots_dev, 2 * total_frames, feeds_dev)

    def moved(x, by):
        return lax.ppermute(x, "feed", [(i, (i + by) % devices) for i in range(devices)])

    def swapped(x):
        return lax.ppermute(x, "feed", [(i, i ^ 1) for i in range(devices)])

    me = lax.axis_index("feed").astype(jnp.int32)
    chips = devices // 2
    place = lambda behind: jnp.stack([(me // 2 - behind) % chips, me % 2])
    call = functools.partial(pair_call, half=frames_dev, scale=1.0 / total_frames)
    sibling = swapped(own)
    blocks = [moved(own, 2), moved(own, -2), moved(own, 4)]
    others = [swapped(x) for x in blocks]
    vis, left, voltage = call("first", where=place(0), own=own, other=sibling, weights=weights)
    for behind, x, y in ((1, blocks[0], others[0]), (-1, blocks[1], others[1])):
        vis, voltage = call(
            "middle", where=place(behind), own=x, other=y, weights=weights,
            left=left, voltage=voltage, vis=vis,
        )
    vis, power = call(
        "final", where=place(2), own=blocks[2], other=others[2], weights=weights,
        left=left, voltage=voltage, vis=vis,
    )
    return (vis, power)


def solution(mesh):
    in_specs = (P("feed", "freq"), P(None, None, "feed"), P(), P())
    out_specs = (P("freq", None, "feed", None), P("feed", "freq"))
    return jax.shard_map(shards, mesh=mesh, in_specs=in_specs, out_specs=out_specs, check_vma=False)
```

time: 263 us -> 102 us (0.39)
  blocking collectives: 94.1 us -> 19.2 us
  waiting for transfers between devices: 68.8 us -> 24.1 us
  matrix products: 39.5 us -> 0 us
  Pallas kernels: 0 us -> 38.8 us
  local copies, waits for them, and re-layouts: 35 us -> 4.37 us
  between operations: 15.7 us -> 0.79 us
  starting transfers between devices: 5.65 us -> 13.3 us
  other arithmetic: 3.75 us -> 0.48 us
    unnamed x1 -> x0, blocking collectives: 74.5 us -> none
    ppermute x1 -> x8, waiting for transfers between devices: 57.4 us -> 16.1 us  [the longest x3 16.1 us: moved(): lax.ppermute(x, 'feed', [(i, (i + by) % devices) for i in range(devices)])]
    dot_general x5 -> x0, matrix products: 39.5 us -> none  [the longest x1 28.9 us: shards(): lax.dot_general(transform, summed, (((1,), (2,)), ((), ())), precision=la...]
    pallas_call x0 -> x8, Pallas kernels: none -> 38.8 us  [the longest x4 19.6 us: pair_call(): pl.pallas_call(functools.partial(pair_kernel, kind == 'first', kind == 'f...]
    unnamed x16 -> x10, local copies, waits for them, and re-layouts: 21.6 us -> 2.82 us
    unnamed x3 -> x0, waiting for transfers between devices: 11.4 us -> none
    all_to_all x0 -> x1, waiting for transfers between devices: none -> 7.92 us  [shards(): lax.all_to_all(ordered, 'feed', split_axis=0, concat_axis=0, tiled=True)]
    gather x1 -> x0, local copies, waits for them, and re-layouts: 5.28 us -> none  [shards(): weights_ord = jnp.take(beam_weights, beam_order, axis=1)]
  transfers between devices with their start and end apart: 3 -> 9, of which waited for: 2 -> 4; matrix products, arithmetic and copies ran while one was open for 5% -> 1% of each run, Pallas kernels for 0% -> 29%
where the time goes in v1:
time: 102 us; the launch traced here: 101 us
  Pallas kernels  38.8 us (38%)
  waiting for transfers between devices  24.1 us (24%)
  blocking collectives  19.2 us (19%)
  starting transfers between devices  13.3 us (13%)
  local copies, waits for them, and re-layouts  4.37 us (4%)
    pallas_call x4, Pallas kernels, pair_call(): pl.pallas_call(functools.partial(pair_kernel, kind == 'first', kind == 'f...  19.6 us
    all_to_all x1, blocking collectives, shards(): lax.all_to_all(outgoing.reshape(owners, slots_dev, 2 * frames_dev, feeds_...  19.2 us
    ppermute x3, waiting for transfers between devices, moved(): lax.ppermute(x, 'feed', [(i, (i + by) % devices) for i in range(devices)])  16.1 us
    pallas_call x1, Pallas kernels, shards(): pl.pallas_call(first_frames_kernel, out_shape=[jax.ShapeDtypeStruct((fram...  10 us
    all_to_all x1, waiting for transfers between devices, shards(): lax.all_to_all(ordered, 'feed', split_axis=0, concat_axis=0, tiled=True)  7.92 us
    ppermute x3, starting transfers between devices, moved(): lax.ppermute(x, 'feed', [(i, (i + by) % devices) for i in range(devices)])  5.37 us
    pallas_call x1, Pallas kernels, shards(): pl.pallas_call(order_kernel, out_shape=jax.ShapeDtypeStruct((devices, 2,...  4.47 us
    pallas_call x1, Pallas kernels, shards(): pl.pallas_call(last_frames_kernel, out_shape=jax.ShapeDtypeStruct((2 * la...  4.14 us
  transfers between devices with their start and end apart: 9, of which 4 were waited for; matrix products, arithmetic and copies ran while one was open for 1% of the time, Pallas kernels for 29%

profile of v1, /device:TPU:0, one launch (start us, length us, event | category | flops | bytes accessed | tf_op | source)
XLA Modules:
  0.0 101.0 jit_solution(15192719784244743444)
XLA Ops:
  0.6 1.6 %copy-done = bf16[512,2048]{1,0:T(8,128)(2,1)S(1)} copy-done((bf16[512,2048]{1,0:T(8,128)(2,1)S(1)}, bf16[512,2048]{1,0:T(8,128)(2,1)}, u32[]{:S(2)}) %copy-start) | copy-done | bytes 2097176
  2.2 4.1 %shard_map.68.last_ref = f32[6,64,256]{2,1,0:T(8,128)S(1)} custom-call(bf16[512,2048]{1,0:T(8,128)(2,1)S(1)} %copy-done, bf16[256,24576]{1,0:T(8,128)(2,1)} %volts_ref.3), custom_call_target="tpu_custom_call" | custom-call | flops 1610612736 | bytes 3145728 | tf_op jit(solution)/shard_map/pallas_call | solution.py:219
  6.4 3.9 %collective-permute-start = (f32[3,64,256]{2,1,0:T(8,128)S(1)}, f32[3,64,256]{2,1,0:T(8,128)S(1)}, u32[]{:S(2)}, u32[]{:S(2)}) collective-permute-start(f32[3,64,256]{2,1,0:T(8,128)S(1)} %slice.4), channel_id=1, source_target_pairs={{0,1},{1,2},{2,3},{3,4},{4,5},{5,6},{6,7},{7,8},{8,9},{9,10},{10,1... | collective-permute-start | bytes 589832 | tf_op jit(solution)/shard_map/ppermute | solution.py:230
  10.9 0.3 select_n.58.target_ref
  11.2 10.0 %shard_map.69 = (f32[12,64,256]{2,1,0:T(8,128)S(1)}, bf16[1152,768]{1,0:T(8,128)(2,1)S(1)}) custom-call(bf16[512,2048]{1,0:T(8,128)(2,1)S(1)} %copy-done.1, bf16[256,24576]{1,0:T(8,128)(2,1)} %volts_ref.3, f32[6,64,256]{2,1,0:T(8,128)S(1)} %shard_map.68.last_ref, s32[1152,1]{1,0:T(8,128)S(1)} %select_n.58.target_ref), custom_call_target="tpu_custom_call" | custom-call | flops 4831838208 | bytes 9437184 | tf_op jit(solution)/shard_map/pallas_call | solution.py:258
  21.3 0.6 shard_map.70
  21.9 19.2 %all_to_all.10 = bf16[16,3,24,256]{3,2,1,0:T(8,128)(2,1)S(1)} all-to-all(bf16[16,3,24,256]{3,2,1,0:T(8,128)(2,1)S(1)} %bitcast.11), channel_id=1, replica_groups=mesh['feed'=8,'freq'=16] {'freq'}, dimensions={0} | all-to-all | bytes 1179648 | tf_op jit(solution)/shard_map/all_to_all | solution.py:288
  41.1 1.6 %collective-permute-start.6 = (bf16[3,384,256]{2,1,0:T(8,128)(2,1)S(1)}, bf16[3,384,256]{2,1,0:T(8,128)(2,1)S(1)}, u32[]{:S(2)}, u32[]{:S(2)}) collective-permute-start(bf16[3,384,256]{2,1,0:T(8,128)(2,1)S(1)} %bitcast.13), channel_id=1, source_target_pairs={{0,32},{16,48},{32,64},{48,80},{64,96},{80,112},{96,0},{112,16},{1... | collective-permute-start | bytes 1769480 | tf_op jit(solution)/shard_map/ppermute | solution.py:298
  42.8 1.7 %collective-permute-start.4 = (bf16[3,384,256]{2,1,0:T(8,128)(2,1)S(1)}, bf16[3,384,256]{2,1,0:T(8,128)(2,1)S(1)}, u32[]{:S(2)}, u32[]{:S(2)}) collective-permute-start(bf16[3,384,256]{2,1,0:T(8,128)(2,1)S(1)} %bitcast.14), channel_id=1, source_target_pairs={{0,96},{16,112},{32,0},{48,16},{64,32},{80,48},{96,64},{112,80},{1... | collective-permute-start | bytes 1769480 | tf_op jit(solution)/shard_map/ppermute | solution.py:298
  44.4 0.2 copy.24.order_ref
  44.6 2.1 %collective-permute-start.1 = (bf16[3,384,256]{2,1,0:T(8,128)(2,1)S(1)}, bf16[3,384,256]{2,1,0:T(8,128)(2,1)S(1)}, u32[]{:S(2)}, u32[]{:S(2)}) collective-permute-start(bf16[3,384,256]{2,1,0:T(8,128)(2,1)S(1)} %bitcast.15), channel_id=1, source_target_pairs={{0,64},{16,80},{32,96},{48,112},{64,0},{80,16},{96,32},{112,48},{1... | collective-permute-start | bytes 1769480 | tf_op jit(solution)/shard_map/ppermute | solution.py:298
  46.7 1.2 %copy-done.2 = bf16[2,1024,256]{2,1,0:T(8,128)(2,1)S(1)} copy-done((bf16[2,1024,256]{2,1,0:T(8,128)(2,1)S(1)}, bf16[2,1024,256]{2,1,0:T(8,128)(2,1)}, u32[]{:S(2)}) %copy-start.2) | copy-done | bytes 1048600
  47.9 4.5 %shard_map.71 = bf16[8,2,128,256]{3,2,1,0:T(8,128)(2,1)} custom-call(s32[1024,1]{1,0:T(8,128)S(1)} %copy.24.order_ref, bf16[2,1024,256]{2,1,0:T(8,128)(2,1)S(1)} %copy-done.2), custom_call_target="tpu_custom_call" | custom-call | flops 1073741824 | bytes 1048576 | tf_op jit(solution)/shard_map/pallas_call | solution.py:232
  52.4 3.6 %all-to-all-start.1 = ((bf16[8,2,128,256]{3,2,1,0:T(8,128)(2,1)}), bf16[8,2,128,256]{3,2,1,0:T(8,128)(2,1)S(1)}, u32[]{:S(2)}, u32[]{:S(2)}) async-start(bf16[8,2,128,256]{3,2,1,0:T(8,128)(2,1)} %shard_map.71), calls=%async_computation.1 | async-start | bytes 2097152 | tf_op jit(solution)/shard_map/all_to_all | solution.py:246
  56.0 0.4 collective-permute-start.3
  56.4 1.2 %collective-permute-done.6.refs_0_ = bf16[3,384,256]{2,1,0:T(8,128)(2,1)S(1)} collective-permute-done((bf16[3,384,256]{2,1,0:T(8,128)(2,1)S(1)}, bf16[3,384,256]{2,1,0:T(8,128)(2,1)S(1)}, u32[]{:S(2)}, u32[]{:S(2)}) %collective-permute-start.6) | collective-permute-done | bytes 589856 | tf_op jit(solution)/shard_map/ppermute | solution.py:298
  57.5 10.9 %collective-permute-done.4.refs_0_ = bf16[3,384,256]{2,1,0:T(8,128)(2,1)S(1)} collective-permute-done((bf16[3,384,256]{2,1,0:T(8,128)(2,1)S(1)}, bf16[3,384,256]{2,1,0:T(8,128)(2,1)S(1)}, u32[]{:S(2)}, u32[]{:S(2)}) %collective-permute-start.4) | collective-permute-done | bytes 589856 | tf_op jit(solution)/shard_map/ppermute | solution.py:298
  68.5 4.1 %collective-permute-done.1.refs_0_ = bf16[3,384,256]{2,1,0:T(8,128)(2,1)S(1)} collective-permute-done((bf16[3,384,256]{2,1,0:T(8,128)(2,1)S(1)}, bf16[3,384,256]{2,1,0:T(8,128)(2,1)S(1)}, u32[]{:S(2)}, u32[]{:S(2)}) %collective-permute-start.1) | collective-permute-done | bytes 589856 | tf_op jit(solution)/shard_map/ppermute | solution.py:298
  72.8 7.9 %all-to-all-done.1.refs_2_.refs_3_ = bf16[8,2,128,256]{3,2,1,0:T(8,128)(2,1)S(1)} async-done(((bf16[8,2,128,256]{3,2,1,0:T(8,128)(2,1)}), bf16[8,2,128,256]{3,2,1,0:T(8,128)(2,1)S(1)}, u32[]{:S(2)}, u32[]{:S(2)}) %all-to-all-start.1) | async-done | bytes 1048608 | tf_op jit(solution)/shard_map/all_to_all | solution.py:246
  80.7 4.9 %shard_map.72 = (f32[3,2,256,2048]{3,2,1,0:T(8,128)}, bf16[3,512,384]{2,1,0:T(8,128)(2,1)S(1)}, f32[3,256,384]{2,1,0:T(8,128)S(1)}) custom-call(s32[2]{0:T(128)S(1)} %pad_add_fusion.1.where_ref, bf16[3,384,256]{2,1,0:T(8,128)(2,1)S(1)} %bitcast.17, bf16[3,384,256]{2,1,0:T(8,128)(2,1)} %collective-permute-done.3.refs_1_, ...), custom_call_target="tpu_custom_call" | custom-call | flops 905969664 | bytes 4915200 | tf_op jit(solution)/shard_map/pallas_call | solution.py:189
  85.7 4.7 %shard_map.73 = (f32[3,2,256,2048]{3,2,1,0:T(8,128)}, f32[3,256,384]{2,1,0:T(8,128)S(1)}) custom-call(s32[2]{0:T(128)S(1)} %pad_add_fusion.3.where_ref, bf16[3,384,256]{2,1,0:T(8,128)(2,1)S(1)} %collective-permute-done.6.refs_0_, bf16[3,384,256]{2,1,0:T(8,128)(2,1)} %collective-permute-done.7.refs_1_, ...), custom_call_target="tpu_custom_call", output_to_operand_aliasing={{0}: (7, {})} | custom-call | flops 905969664 | bytes 4915200 | tf_op jit(solution)/shard_map/pallas_call | solution.py:189
  90.4 4.7 %shard_map.74 = (f32[3,2,256,2048]{3,2,1,0:T(8,128)}, f32[3,256,384]{2,1,0:T(8,128)S(1)}) custom-call(s32[2]{0:T(128)S(1)} %pad_add_fusion.2.where_ref, bf16[3,384,256]{2,1,0:T(8,128)(2,1)S(1)} %collective-permute-done.4.refs_0_, bf16[3,384,256]{2,1,0:T(8,128)(2,1)} %collective-permute-done.5.refs_1_, ...), custom_call_target="tpu_custom_call", output_to_operand_aliasing={{0}: (7, {})} | custom-call | flops 905969664 | bytes 4915200 | tf_op jit(solution)/shard_map/pallas_call | solution.py:189
  95.1 5.2 %shard_map.75 = (f32[3,2,256,2048]{3,2,1,0:T(8,128)}, f32[128,3]{1,0:T(8,128)S(1)}) custom-call(s32[2]{0:T(128)S(1)} %pad_add_fusion.where_ref, bf16[3,384,256]{2,1,0:T(8,128)(2,1)S(1)} %collective-permute-done.1.refs_0_, bf16[3,384,256]{2,1,0:T(8,128)(2,1)} %collective-permute-done.2.refs_1_, ...), custom_call_target="tpu_custom_call", output_to_operand_aliasing={{0}: (7, {})} | custom-call | flops 905969664 | bytes 4915200 | tf_op jit(solution)/shard_map/pallas_call | solution.py:189
  100.3 0.7 copy.25
  (31 shorter events, 0.9 us)
Async XLA Ops:
  0.6 1.6 %copy-start = (bf16[512,2048]{1,0:T(8,128)(2,1)S(1)}, bf16[512,2048]{1,0:T(8,128)(2,1)}, u32[]{:S(2)}) copy-start(bf16[512,2048]{1,0:T(8,128)(2,1)} %constant.76.clone.table_ref) | copy-start | bytes 6291460
  2.2 8.1 %copy-start.3 = (s32[16,3]{0,1:T(4,128)S(1)}, s32[16,3]{0,1:T(4,128)}, u32[]{:S(2)}) copy-start(s32[16,3]{0,1:T(4,128)} %param.7) | copy-start | bytes 580
  2.2 9.0 %copy-start.1 = (bf16[512,2048]{1,0:T(8,128)(2,1)S(1)}, bf16[512,2048]{1,0:T(8,128)(2,1)}, u32[]{:S(2)}) copy-start(bf16[512,2048]{1,0:T(8,128)(2,1)} %constant.76.clone.table_ref) | copy-start | bytes 6291460
  6.4 14.8 %collective-permute-start = (f32[3,64,256]{2,1,0:T(8,128)S(1)}, f32[3,64,256]{2,1,0:T(8,128)S(1)}, u32[]{:S(2)}, u32[]{:S(2)}) collective-permute-start(f32[3,64,256]{2,1,0:T(8,128)S(1)} %slice.4), channel_id=1, source_target_pairs={{0,1},{1,2},{2,3},{3,4},{4,5},{5,6},{6,7},{7,8},{8,9},{9,10},{10,1... | collective-permute-start | bytes 589832 | tf_op jit(solution)/shard_map/ppermute | solution.py:230
  21.3 23.2 %copy-start.4 = (s32[1024]{0:T(1024)S(1)}, s32[1024]{0:T(1024)}, u32[]{:S(2)}) copy-start(s32[1024]{0:T(1024)} %param.8) | copy-start | bytes 12292
  41.1 16.4 %collective-permute-start.6 = (bf16[3,384,256]{2,1,0:T(8,128)(2,1)S(1)}, bf16[3,384,256]{2,1,0:T(8,128)(2,1)S(1)}, u32[]{:S(2)}, u32[]{:S(2)}) collective-permute-start(bf16[3,384,256]{2,1,0:T(8,128)(2,1)S(1)} %bitcast.13), channel_id=1, source_target_pairs={{0,32},{16,48},{32,64},{48,80},{64,96},{80,112},{96,0},{112,16},{1... | collective-permute-start | bytes 1769480 | tf_op jit(solution)/shard_map/ppermute | solution.py:298
  42.8 25.7 %collective-permute-start.4 = (bf16[3,384,256]{2,1,0:T(8,128)(2,1)S(1)}, bf16[3,384,256]{2,1,0:T(8,128)(2,1)S(1)}, u32[]{:S(2)}, u32[]{:S(2)}) collective-permute-start(bf16[3,384,256]{2,1,0:T(8,128)(2,1)S(1)} %bitcast.14), channel_id=1, source_target_pairs={{0,96},{16,112},{32,0},{48,16},{64,32},{80,48},{96,64},{112,80},{1... | collective-permute-start | bytes 1769480 | tf_op jit(solution)/shard_map/ppermute | solution.py:298
  44.6 27.9 %collective-permute-start.1 = (bf16[3,384,256]{2,1,0:T(8,128)(2,1)S(1)}, bf16[3,384,256]{2,1,0:T(8,128)(2,1)S(1)}, u32[]{:S(2)}, u32[]{:S(2)}) collective-permute-start(bf16[3,384,256]{2,1,0:T(8,128)(2,1)S(1)} %bitcast.15), channel_id=1, source_target_pairs={{0,64},{16,80},{32,96},{48,112},{64,0},{80,16},{96,32},{112,48},{1... | collective-permute-start | bytes 1769480 | tf_op jit(solution)/shard_map/ppermute | solution.py:298
  46.7 1.2 %copy-start.2 = (bf16[2,1024,256]{2,1,0:T(8,128)(2,1)S(1)}, bf16[2,1024,256]{2,1,0:T(8,128)(2,1)}, u32[]{:S(2)}) copy-start(bf16[2,1024,256]{2,1,0:T(8,128)(2,1)} %weights_ref.1) | copy-start | bytes 3145732
  52.4 28.3 %all-to-all-start.1 = ((bf16[8,2,128,256]{3,2,1,0:T(8,128)(2,1)}), bf16[8,2,128,256]{3,2,1,0:T(8,128)(2,1)S(1)}, u32[]{:S(2)}, u32[]{:S(2)}) async-start(bf16[8,2,128,256]{3,2,1,0:T(8,128)(2,1)} %shard_map.71), calls=%async_computation.1 | async-start | bytes 2097152 | tf_op jit(solution)/shard_map/all_to_all | solution.py:246
  56.0 24.8 %collective-permute-start.3 = (bf16[3,384,256]{2,1,0:T(8,128)(2,1)S(1)}, bf16[3,384,256]{2,1,0:T(8,128)(2,1)}, u32[]{:S(2)}, u32[]{:S(2)}) collective-permute-start(bf16[3,384,256]{2,1,0:T(8,128)(2,1)S(1)} %bitcast.16), channel_id=1, source_target_pairs={{0,16},{16,0},{32,48},{48,32},{64,80},{80,64},{96,112},{112,96},{1... | collective-permute-start | bytes 1769480 | tf_op jit(solution)/shard_map/ppermute | solution.py:301
  57.5 28.1 %collective-permute-start.7 = (bf16[3,384,256]{2,1,0:T(8,128)(2,1)S(1)}, bf16[3,384,256]{2,1,0:T(8,128)(2,1)}, u32[]{:S(2)}, u32[]{:S(2)}) collective-permute-start(bf16[3,384,256]{2,1,0:T(8,128)(2,1)S(1)} %collective-permute-done.6.refs_0_), channel_id=1, source_target_pairs={{0,16},{16,0},{32,48},{48,32},{64,80},{80,64},{96,112},{112,96},{1... | collective-permute-start | bytes 1769480 | tf_op jit(solution)/shard_map/ppermute | solution.py:301
  68.4 22.0 %collective-permute-start.5 = (bf16[3,384,256]{2,1,0:T(8,128)(2,1)S(1)}, bf16[3,384,256]{2,1,0:T(8,128)(2,1)}, u32[]{:S(2)}, u32[]{:S(2)}) collective-permute-start(bf16[3,384,256]{2,1,0:T(8,128)(2,1)S(1)} %collective-permute-done.4.refs_0_), channel_id=1, source_target_pairs={{0,16},{16,0},{32,48},{48,32},{64,80},{80,64},{96,112},{112,96},{1... | collective-permute-start | bytes 1769480 | tf_op jit(solution)/shard_map/ppermute | solution.py:301
  72.6 22.5 %collective-permute-start.2 = (bf16[3,384,256]{2,1,0:T(8,128)(2,1)S(1)}, bf16[3,384,256]{2,1,0:T(8,128)(2,1)}, u32[]{:S(2)}, u32[]{:S(2)}) collective-permute-start(bf16[3,384,256]{2,1,0:T(8,128)(2,1)S(1)} %collective-permute-done.1.refs_0_), channel_id=1, source_target_pairs={{0,16},{16,0},{32,48},{48,32},{64,80},{80,64},{96,112},{112,96},{1... | collective-permute-start | bytes 1769480 | tf_op jit(solution)/shard_map/ppermute | solution.py:301

commit v2 on v0

v2 whole, which is shorter than its diff:
```python
import functools
import math

import jax
import jax.numpy as jnp
import ml_dtypes
import numpy as np
from jax import lax
from jax.experimental import pallas as pl
from jax.experimental.pallas import tpu as pltpu
from jax.sharding import PartitionSpec as P

NFFT = 2048
TAPS = 4
AHEAD = 2
COST = {"middle": pl.CostEstimate(flops=1, bytes_accessed=1, transcendentals=0)}
WIDE_VMEM = 62 * 1024 * 1024
NT = (((1,), (1,)), ((), ()))


def tap_transform(channels):
    length = TAPS * NFFT
    positions = np.arange(length, dtype=np.float64)
    coeffs = np.sinc((positions - 0.5 * length + 0.5) / NFFT)
    coeffs = coeffs * (0.5 - 0.5 * np.cos(2.0 * math.pi * (positions + 0.5) / length))
    coeffs = coeffs * np.sqrt(NFFT / np.sum(coeffs * coeffs))
    coeffs = coeffs.reshape(TAPS, NFFT)
    angles = (np.arange(channels)[:, None] * np.arange(NFFT)[None, :] % NFFT) * (2.0 * math.pi / NFFT)
    rows = np.stack([np.cos(angles), -np.sin(angles)], axis=1) / math.sqrt(NFFT)
    rows = rows.reshape(2 * channels, NFFT)
    full = (coeffs[:, None, :] * rows[None]).reshape(TAPS * 2 * channels, NFFT)
    high = full.astype(ml_dtypes.bfloat16)
    low = (full - high.astype(np.float64)).astype(ml_dtypes.bfloat16)
    return np.concatenate([high, low], axis=0)


def frame_loop(table_hbm, volts_hbm, table, frames, table_sem, frame_sems, total_ref, first, extra):
    count = frames.shape[0]
    rows = total_ref.shape[1]

    def table_copy():
        return pltpu.make_async_copy(table_hbm, table, table_sem)

    def frame_copy(i):
        at = pl.multiple_of((first + i) * NFFT, NFFT)
        return pltpu.make_async_copy(
            volts_hbm.at[:, pl.ds(at, NFFT)], frames.at[i], frame_sems.at[i]
        )

    table_copy().start()
    for i in range(AHEAD):
        frame_copy(i).start()
    extra(0)
    table_copy().wait()

    def step(i, _):
        @pl.when(i + AHEAD < count)
        def _():
            frame_copy(i + AHEAD).start()

        frame_copy(i).wait()
        product = lax.dot_general(
            table[...], frames[i], NT, preferred_element_type=jnp.float32
        )
        half = product.shape[0] // 2
        product = product[:half] + product[half:]
        for tap in range(TAPS):
            at = i + TAPS - 1 - tap
            total_ref[at] = total_ref[at] + product[tap * rows : (tap + 1) * rows]
        extra(i)
        return 0

    lax.fori_loop(0, count, step, 0)


def last_frames_kernel(
    first, table_hbm, volts_hbm, own_ref, next_ref, total, table, frames, table_sem, frame_sems
):
    total[...] = jnp.zeros_like(total)
    frame_loop(
        table_hbm, volts_hbm, table, frames, table_sem, frame_sems, total, first, lambda i: None
    )
    own_ref[...] = total[: TAPS - 1]
    next_ref[...] = total[TAPS - 1 :]


def first_frames_kernel(
    allocation_hbm, table_hbm, volts_hbm, last_ref, carry_ref, out_ref,
    total, hot, spectra, allocation_ref, allocation_sem, table, frames, table_sem, frame_sems,
):
    allocation_copy = pltpu.make_async_copy(allocation_hbm, allocation_ref, allocation_sem)
    allocation_copy.start()
    count, rows, width = total.shape
    slots, owners = allocation_ref.shape
    late = last_ref.shape[0]
    done = count - late
    total[:late] = carry_ref[...]
    total[late:done] = jnp.zeros((done - late, rows, width), jnp.float32)
    total[done:] = last_ref[...]
    size = 2 * count
    group = 2 * slots * size
    shape = (size, count * rows)
    row = lax.broadcasted_iota(jnp.int32, shape, 0)
    part = (row >= count).astype(jnp.int32)
    offset = lax.broadcasted_iota(jnp.int32, shape, 1) - (row - part * count) * rows - part

    allocation_copy.wait()

    def choose(i):
        pair = jnp.minimum(i, owners // 2 - 1)
        chosen = []
        for owner in range(2):
            for slot in range(slots):
                channel = allocation_ref[slot, 2 * pair + owner]
                wanted = jnp.where(channel >= 0, 2 * channel, -2 * count * rows)
                chosen.append(jnp.where(offset == wanted, 1.0, 0.0))
        hot[pl.ds(pl.multiple_of(pair * group, group), group)] = jnp.concatenate(
            chosen, axis=0
        ).astype(jnp.bfloat16)

    frame_loop(
        table_hbm, volts_hbm, table, frames, table_sem, frame_sems, total, 0, choose
    )
    for t in range(count):
        spectra[pl.ds(t * rows, rows)] = total[t].astype(jnp.bfloat16)

    def write(i, _):
        at = pl.ds(pl.multiple_of(i * 4 * group, 4 * group), 4 * group)
        out_ref[at] = jnp.dot(hot[at], spectra[...], preferred_element_type=jnp.float32).astype(
            jnp.bfloat16
        )
        return 0

    lax.fori_loop(0, owners // 8, write, 0)


def filter_scratch(table, feeds, count):
    return [
        pltpu.VMEM(table.shape, jnp.bfloat16),
        pltpu.VMEM((count, feeds, NFFT), jnp.bfloat16),
        pltpu.SemaphoreType.DMA,
        pltpu.SemaphoreType.DMA((count,)),
    ]


def order_kernel(order_ref, weights_ref, *out_refs):
    beams = weights_ref.shape[1]
    devices, share = order_ref.shape
    chips = len(out_refs)
    me = lax.axis_index("feed")
    chip, core = me // 2, me % 2
    numbers = order_ref[...].astype(jnp.float32).T
    of_device = lax.broadcasted_iota(jnp.int32, numbers.shape, 1)
    place = lax.broadcasted_iota(jnp.int32, (share, beams), 1)
    for ahead, out_ref in enumerate(out_refs):
        to = lax.rem(chip + ahead, chips)
        hot = []
        for other in range(2):
            device = 2 * to + (core if other == 0 else 1 - core)
            wanted = jnp.sum(jnp.where(of_device == device, numbers, 0.0), axis=1, keepdims=True)
            hot.append(jnp.where(place == wanted.astype(jnp.int32), 1.0, 0.0).astype(jnp.bfloat16))
        hot = jnp.concatenate(hot, axis=0)
        for part in range(2):
            rows = jnp.dot(hot, weights_ref[part], preferred_element_type=jnp.float32)
            rows = rows.astype(jnp.bfloat16)
            out_ref[0, part] = rows[:share]
            out_ref[1, part] = rows[share:]


def swap_parts(values, half, axis):
    count = values.shape[axis]
    place = lax.broadcasted_iota(jnp.int32, values.shape, axis)
    ahead = pltpu.roll(values, count - half, axis)
    behind = pltpu.roll(values, half, axis)
    return jnp.where(place % (2 * half) < half, ahead, -behind)


def pair_kernel(behind, kind, half, scale, *refs):
    refs = list(refs)
    pairs = len(behind)
    block_refs = refs[: 4 * pairs]
    weight_refs = refs[4 * pairs : 6 * pairs]
    refs = refs[6 * pairs :]
    if kind == "first":
        vis_hbm, left_hbm, result_ref = refs[:3]
        refs = refs[3:]
    else:
        left_hbm, voltage_hbm, _, vis_hbm, result_ref = refs[:5]
        refs = refs[5:]
    values, weights, left, voltages, out, sems, weight_sems, out_sems, save_sems = refs
    slots, rows, narrow = values.shape[1:]
    width = 2 * narrow
    chips = vis_hbm.shape[3] // (2 * width)
    me = lax.axis_index("feed")
    chip, core = me // 2, me % 2

    def slot_copies(slot):
        copies = [(ref.at[slot], values.at[i, slot]) for i, ref in enumerate(block_refs)]
        if kind != "first":
            copies += [(left_hbm.at[slot], left.at[slot]), (voltage_hbm.at[slot], voltages.at[slot])]
        return [
            pltpu.make_async_copy(source, target, sems.at[slot, i])
            for i, (source, target) in enumerate(copies)
        ]

    weight_copies = [
        pltpu.make_async_copy(ref.at[0], weights.at[i], weight_sems.at[i])
        for i, ref in enumerate(weight_refs)
    ]

    def save_copies(slot):
        copies = []
        if kind != "last":
            copies.append((voltages.at[slot], result_ref.at[slot]))
        if kind == "first":
            copies.append((left.at[slot], left_hbm.at[slot]))
        return [
            pltpu.make_async_copy(source, target, save_sems.at[slot, i])
            for i, (source, target) in enumerate(copies)
        ]

    def out_copy(slot, pair):
        to = lax.rem(chip + chips - behind[pair], chips)
        at = pl.multiple_of(to * 2 * width, 2 * width)
        return pltpu.make_async_copy(
            out.at[slot, pair],
            vis_hbm.at[slot, :, :, pl.ds(at, 2 * width)],
            out_sems.at[slot, pair],
        )

    for copy in slot_copies(0) + weight_copies + slot_copies(1) + slot_copies(2):
        copy.start()

    def step(slot, _):
        for copy in slot_copies(slot):
            copy.wait()

        def value(i):
            return jnp.concatenate([values[2 * i, slot], values[2 * i + 1, slot]], axis=1)

        if kind == "first":
            own = value(0).astype(jnp.float32).T
            left[slot] = jnp.concatenate([own, swap_parts(own, half, 1)], axis=0).astype(
                jnp.bfloat16
            )
        for pair in range(pairs):
            for side, at in ((0, core), (1, 1 - core)):
                product = jnp.dot(
                    left[slot], value(2 * pair + side), preferred_element_type=jnp.float32
                )
                product = product * scale
                columns = pl.ds(pl.multiple_of(at * width, width), width)
                out[slot, pair, 0, :, columns] = product[:width]
                out[slot, pair, 1, :, columns] = product[width:]
            out_copy(slot, pair).start()

        @pl.when(slot == 0)
        def _():
            for copy in weight_copies:
                copy.wait()

        voltage = None
        for i in range(2 * pairs):
            weight = weights[i]
            weight = weight.reshape(weight.shape[0] * weight.shape[1], width)
            term = lax.dot_general(value(i), weight, NT, preferred_element_type=jnp.float32)
            voltage = term if voltage is None else voltage + term
        share = voltage.shape[1] // 2
        beam = voltage[:, :share] - swap_parts(voltage[:, share:], half, 0)
        if kind != "first":
            beam = voltages[slot] + beam
        if kind == "last":
            result_ref[pl.ds(slot, 1), :] = jnp.sum(beam * beam, axis=0, keepdims=True) * scale
        else:
            voltages[slot] = beam
            for copy in save_copies(slot):
                copy.start()
        return 0

    lax.fori_loop(0, slots, step, 0)
    for slot in range(slots):
        for pair in range(pairs):
            out_copy(slot, pair).wait()
        for copy in save_copies(slot):
            copy.wait()


def params():
    return pltpu.CompilerParams(vmem_limit_bytes=WIDE_VMEM)


def pair_call(
    kind, behind, half, scale, devices, blocks, weights, left=None, voltage=None, vis=None
):
    pairs = len(behind)
    slots, rows, narrow = blocks[0].shape
    width = 2 * narrow
    _, parts, share, _ = weights[0].shape
    anywhere = pl.BlockSpec(memory_space=pl.ANY)
    in_vmem = pl.BlockSpec(memory_space=pltpu.VMEM)
    args = list(blocks) + list(weights)
    vis_shape = jax.ShapeDtypeStruct((slots, 2, width, devices * width), jnp.float32)
    voltage_shape = jax.ShapeDtypeStruct((slots, rows, share), jnp.float32)
    left_shape = jax.ShapeDtypeStruct((slots, 2 * width, rows), jnp.bfloat16)
    power_shape = jax.ShapeDtypeStruct((slots, share), jnp.float32)
    aliases = {}
    if kind == "first":
        out_shape, out_specs = [vis_shape, left_shape, voltage_shape], [anywhere] * 3
    else:
        args += [left, voltage, vis]
        aliases = {len(args) - 1: 0}
        if kind == "middle":
            out_shape, out_specs = [vis_shape, voltage_shape], [anywhere] * 2
        else:
            out_shape, out_specs = [vis_shape, power_shape], [anywhere, in_vmem]
    flops = pairs * 4 * slots * rows * width * (2 * width + parts * share)
    moved = pairs * slots * 2 * width * 2 * width * 4 + 6 * slots * rows * width
    return pl.pallas_call(
        functools.partial(pair_kernel, behind, kind, half, scale),
        out_shape=out_shape,
        in_specs=[anywhere] * len(args),
        out_specs=out_specs,
        scratch_shapes=[
            pltpu.VMEM((4 * pairs, slots, rows, narrow), jnp.bfloat16),
            pltpu.VMEM((2 * pairs, parts, share, width), jnp.bfloat16),
            pltpu.VMEM(left_shape.shape, jnp.bfloat16),
            pltpu.VMEM(voltage_shape.shape, jnp.float32),
            pltpu.VMEM((slots, pairs, 2, width, 2 * width), jnp.float32),
            pltpu.SemaphoreType.DMA((slots, 4 * pairs + 2)),
            pltpu.SemaphoreType.DMA((2 * pairs,)),
            pltpu.SemaphoreType.DMA((slots, pairs)),
            pltpu.SemaphoreType.DMA((slots, 2)),
        ],
        input_output_aliases=aliases,
        compiler_params=params(),
        cost_estimate=COST.get(kind, pl.CostEstimate(flops=flops, bytes_accessed=moved, transcendentals=0)),
        name="pairs_" + kind,
    )(*args)


def shards(volts, beam_weights, allocation, beam_order):
    feeds_dev = volts.shape[0]
    frames_dev = volts.shape[1] // NFFT
    owners = lax.axis_size("freq")
    devices = lax.axis_size("feed")
    total_frames = frames_dev * owners
    slots_dev = allocation.shape[1]
    channels = (slots_dev - 1) * allocation.shape[0]
    rows = 2 * channels
    late = TAPS - 1
    early = frames_dev - late
    beams = beam_weights.shape[1]
    share = beams // devices
    f32, bf16 = jnp.float32, jnp.bfloat16
    table = jnp.asarray(tap_transform(channels))
    frame_flops = 2 * table.shape[0] * feeds_dev * NFFT
    anywhere = pl.BlockSpec(memory_space=pl.ANY)
    in_vmem = pl.BlockSpec(memory_space=pltpu.VMEM)

    def moved(x, by):
        return lax.ppermute(x, "feed", [(i, (i + by) % devices) for i in range(devices)])

    def swapped(x):
        return lax.ppermute(x, "feed", [(i, i ^ 1) for i in range(devices)])

    own_last, next_first = pl.pallas_call(
        functools.partial(last_frames_kernel, early),
        out_shape=[jax.ShapeDtypeStruct((late, rows, feeds_dev), f32)] * 2,
        in_specs=[anywhere, anywhere],
        out_specs=[in_vmem, in_vmem],
        scratch_shapes=[pltpu.VMEM((2 * late, rows, feeds_dev), f32)]
        + filter_scratch(table, feeds_dev, late),
        compiler_params=pltpu.CompilerParams(vmem_limit_bytes=WIDE_VMEM),
        cost_estimate=pl.CostEstimate(
            flops=late * frame_flops, bytes_accessed=late * feeds_dev * NFFT * 2, transcendentals=0
        ),
        name="last_frames",
    )(table, volts)
    carry = lax.ppermute(next_first, "freq", [(i, i + 1) for i in range(owners - 1)])
    ordered = pl.pallas_call(
        order_kernel,
        out_shape=[jax.ShapeDtypeStruct((2, 2, share, feeds_dev), bf16)] * (devices // 2),
        compiler_params=params(),
        cost_estimate=pl.CostEstimate(
            flops=4 * beams * beams * feeds_dev, bytes_accessed=4 * beams * feeds_dev, transcendentals=0
        ),
        name="order_beams",
    )(beam_order.reshape(devices, share), beam_weights)
    own_last, *ordered = lax.optimization_barrier((own_last, *ordered))
    weights = [ordered[0], moved(ordered[1], 2), moved(ordered[3], -2), moved(ordered[2], 4)]
    chosen_rows = owners * slots_dev * 2 * frames_dev
    outgoing = pl.pallas_call(
        first_frames_kernel,
        out_shape=jax.ShapeDtypeStruct((chosen_rows, feeds_dev), bf16),
        in_specs=[anywhere, anywhere, anywhere, in_vmem, in_vmem],
        out_specs=in_vmem,
        scratch_shapes=[
            pltpu.VMEM((frames_dev, rows, feeds_dev), f32),
            pltpu.VMEM((chosen_rows, frames_dev * rows), bf16),
            pltpu.VMEM((frames_dev * rows, feeds_dev), bf16),
            pltpu.SMEM((slots_dev, owners), jnp.int32),
            pltpu.SemaphoreType.DMA,
        ]
        + filter_scratch(table, feeds_dev, early),
        compiler_params=pltpu.CompilerParams(vmem_limit_bytes=WIDE_VMEM),
        cost_estimate=pl.CostEstimate(
            flops=early * frame_flops, bytes_accessed=early * feeds_dev * NFFT * 2, transcendentals=0
        ),
        name="first_frames",
    )(allocation.T, table, volts, own_last, carry)
    outgoing, weights[3] = lax.optimization_barrier((outgoing, weights[3]))
    received = lax.all_to_all(
        outgoing.reshape(owners, slots_dev, 2 * frames_dev, feeds_dev),
        "freq",
        split_axis=0,
        concat_axis=0,
        tiled=True,
    )

    received, weights[1], weights[2] = lax.optimization_barrier(
        (received, weights[1], weights[2])
    )
    weights_other = [swapped(x[1:]) for x in weights]
    by_chip = [[weights[d], weights_other[d]] for d in range(4)]

    own = received.transpose(1, 0, 2, 3).reshape(slots_dev, 2 * total_frames, feeds_dev)
    narrow = feeds_dev // 2
    own = [own[:, :, :narrow], own[:, :, narrow:]]
    up = [moved(own[0], 2)]
    down = [None, moved(own[1], -2)]
    up.append(moved(own[1], 2))
    down[0] = moved(own[0], -2)
    sibling = [swapped(x) for x in own]
    call = functools.partial(pair_call, half=frames_dev, scale=1.0 / total_frames, devices=devices)
    vis, left, voltage = call("first", (0,), blocks=own + sibling, weights=by_chip[0])
    up[0], down[1], voltage = lax.optimization_barrier((up[0], down[1], voltage))
    far = [moved(up[0], 2), moved(down[1], -2)]
    up_other = [swapped(x) for x in up]
    down_other = [swapped(x) for x in down]
    vis, voltage = call(
        "middle", (1, -1), blocks=up + up_other + down + down_other,
        weights=by_chip[1] + by_chip[2], left=left, voltage=voltage, vis=vis,
    )
    *far, voltage = lax.optimization_barrier((*far, voltage))
    far_other = [swapped(x) for x in far]
    vis, power = call(
        "last", (2,), blocks=far + far_other, weights=by_chip[3], left=left, voltage=voltage, vis=vis
    )
    return (vis, power.T)


def solution(mesh):
    in_specs = (P("feed", "freq"), P(None, None, "feed"), P(), P())
    out_specs = (P("freq", None, "feed", None), P("feed", "freq"))
    return jax.shard_map(shards, mesh=mesh, in_specs=in_specs, out_specs=out_specs, check_vma=False)
```

time: 263 us -> 89.2 us (0.34)
  blocking collectives: 94.1 us -> 0 us
  waiting for transfers between devices: 68.8 us -> 12.6 us
  matrix products: 39.5 us -> 0 us
  Pallas kernels: 0 us -> 38.9 us
  local copies, waits for them, and re-layouts: 35 us -> 6.2 us
  starting transfers between devices: 5.65 us -> 29.2 us
  between operations: 15.7 us -> 0.92 us
  other arithmetic: 3.75 us -> 0 us
    unnamed x1 -> x0, blocking collectives: 74.5 us -> none
    ppermute x1 -> x22, waiting for transfers between devices: 57.4 us -> 9.46 us  [the longest x9 5.47 us: moved(): lax.ppermute(x, 'feed', [(i, (i + by) % devices) for i in range(devices)])]
    dot_general x5 -> x0, matrix products: 39.5 us -> none  [the longest x1 28.9 us: shards(): lax.dot_general(transform, summed, (((1,), (2,)), ((), ())), precision=la...]
    pallas_call x0 -> x6, Pallas kernels: none -> 38.9 us  [the longest x3 18.1 us: pair_call(): pl.pallas_call(functools.partial(pair_kernel, behind, kind, half, scale),...]
    all_to_all x1 -> x0, blocking collectives: 19.6 us -> none  [shards(): lax.all_to_all(outgoing, 'freq', split_axis=0, concat_axis=2, tiled=True)]
    unnamed x16 -> x46, local copies, waits for them, and re-layouts: 21.6 us -> 5.12 us
    ppermute x1 -> x22, starting transfers between devices: 5.57 us -> 21.7 us  [the longest x9 15.1 us: moved(): lax.ppermute(x, 'feed', [(i, (i + by) % devices) for i in range(devices)])]
    unnamed x3 -> x0, waiting for transfers between devices: 11.4 us -> none
  transfers between devices with their start and end apart: 3 -> 23, of which waited for: 2 -> 6; matrix products, arithmetic and copies ran while one was open for 5% -> 1% of each run, Pallas kernels for 0% -> 32%
where the time goes in v2:
time: 89.2 us; the launch traced here: 87.8 us
  Pallas kernels  38.9 us (44%)
  starting transfers between devices  29.2 us (33%)
  waiting for transfers between devices  12.6 us (14%)
  local copies, waits for them, and re-layouts  6.2 us (7%)
  between operations  0.92 us (1%)
    pallas_call x3, Pallas kernels, pair_call(): pl.pallas_call(functools.partial(pair_kernel, behind, kind, half, scale),...  18.1 us
    ppermute x9, starting transfers between devices, moved(): lax.ppermute(x, 'feed', [(i, (i + by) % devices) for i in range(devices)])  15.1 us
    pallas_call x1, Pallas kernels, shards(): pl.pallas_call(first_frames_kernel, out_shape=jax.ShapeDtypeStruct((chose...  12.4 us
    all_to_all x1, starting transfers between devices, shards(): lax.all_to_all(outgoing.reshape(owners, slots_dev, 2 * frames_dev, feeds_...  7.43 us
    ppermute x9, waiting for transfers between devices, moved(): lax.ppermute(x, 'feed', [(i, (i + by) % devices) for i in range(devices)])  5.47 us
    unnamed x46, local copies, waits for them, and re-layouts  5.12 us
    pallas_call x1, Pallas kernels, shards(): pl.pallas_call(functools.partial(last_frames_kernel, early), out_shape=[j...  4.94 us
    ppermute x12, waiting for transfers between devices, swapped(): return lax.ppermute(x, 'feed', [(i, i ^ 1) for i in range(devices)])  3.99 us
  transfers between devices with their start and end apart: 23, of which 6 were waited for; matrix products, arithmetic and copies ran while one was open for 1% of the time, Pallas kernels for 32%

profile of v2, /device:TPU:0, one launch (start us, length us, event | category | flops | bytes accessed | tf_op | source)
XLA Modules:
  0.0 87.8 jit_solution(14590487584840778433)
XLA Ops:
  0.6 4.9 %last_frames.1 = (f32[3,64,256]{2,1,0:T(8,128)}, f32[3,64,256]{2,1,0:T(8,128)}) custom-call(bf16[512,2048]{1,0:T(8,128)(2,1)} %constant.2.clone.table_hbm, bf16[256,24576]{1,0:T(8,128)(2,1)} %volts_hbm.3), custom_call_target="tpu_custom_call" | custom-call | flops 1610612736 | bytes 3145728 | tf_op jit(solution)/shard_map/last_frames/pallas_call | solution.py:366
  5.6 3.9 %collective-permute-start = (f32[3,64,256]{2,1,0:T(8,128)}, f32[3,64,256]{2,1,0:T(8,128)S(1)}, u32[]{:S(2)}, u32[]{:S(2)}) collective-permute-start(f32[3,64,256]{2,1,0:T(8,128)} %get-tuple-element.37), channel_id=1, source_target_pairs={{0,1},{1,2},{2,3},{3,4},{4,5},{5,6},{6,7},{7,8},{8,9},{9,10},{10,1... | collective-permute-start | bytes 589832 | tf_op jit(solution)/shard_map/ppermute | solution.py:379
  9.5 3.4 %order_beams.1 = (bf16[2,2,128,256]{3,2,1,0:T(8,128)(2,1)}, bf16[2,2,128,256]{3,2,1,0:T(8,128)(2,1)}, bf16[2,2,128,256]{3,2,1,0:T(8,128)(2,1)}, bf16[2,2,128,256]{3,2,1,0:T(8,128)(2,1)}) custom-call(s32[8,128]{1,0:T(8,128)} %bitcast.9, bf16[2,1024,256]{2,1,0:T(8,128)(2,1)} %weights_ref.1), custom_call_target="tpu_custom_call" | custom-call | flops 1073741824 | bytes 1048576 | tf_op jit(solution)/shard_map/order_beams/pallas_call | solution.py:380
  12.9 3.2 %collective-permute-start.1 = (bf16[2,2,128,256]{3,2,1,0:T(8,128)(2,1)}, bf16[2,2,128,256]{3,2,1,0:T(8,128)(2,1)S(1)}, u32[]{:S(2)}, u32[]{:S(2)}) collective-permute-start(bf16[2,2,128,256]{3,2,1,0:T(8,128)(2,1)} %get-tuple-element.38), channel_id=1, source_target_pairs={{0,64},{16,80},{32,96},{48,112},{64,0},{80,16},{96,32},{112,48},{1... | collective-permute-start | bytes 786440 | tf_op jit(solution)/shard_map/ppermute | solution.py:361
  16.8 12.4 %first_frames.1 = bf16[1152,256]{1,0:T(8,128)(2,1)} custom-call(s32[3,16]{1,0:T(4,128)} %bitcast.10, bf16[512,2048]{1,0:T(8,128)(2,1)} %constant.2.clone.table_hbm, bf16[256,24576]{1,0:T(8,128)(2,1)} %volts_hbm.3, f32[3,64,256]{2,1,0:T(8,128)} %get-tuple-element.36.last_ref, f32[3,64,256]{2,1,0:T(8,128)} %copy-done.21), custom_call_target="tpu_custom_call" | custom-call | flops 4831838208 | bytes 9437184 | tf_op jit(solution)/shard_map/first_frames/pallas_call | solution.py:392
  29.3 7.4 %all-to-all-start = ((bf16[16,3,24,256]{3,2,1,0:T(8,128)(2,1)}), bf16[16,3,24,256]{3,2,1,0:T(8,128)(2,1)S(1)}, u32[]{:S(2)}, u32[]{:S(2)}) async-start(bf16[16,3,24,256]{3,2,1,0:T(8,128)(2,1)} %bitcast.8), calls=%async_computation | async-start | bytes 1179648 | tf_op jit(solution)/shard_map/all_to_all | solution.py:412
  36.7 0.7 collective-permute-start.2
  37.5 2.6 %collective-permute-start.3 = (bf16[2,2,128,256]{3,2,1,0:T(8,128)(2,1)S(1)}, bf16[2,2,128,256]{3,2,1,0:T(8,128)(2,1)S(1)}, u32[]{:S(2)}, u32[]{:S(2)}) collective-permute-start(bf16[2,2,128,256]{3,2,1,0:T(8,128)(2,1)S(1)} %copy-done.19), channel_id=1, source_target_pairs={{0,96},{16,112},{32,0},{48,16},{64,32},{80,48},{96,64},{112,80},{1... | collective-permute-start | bytes 786440 | tf_op jit(solution)/shard_map/ppermute | solution.py:361
  40.0 5.2 %collective-permute-done.2.refs_8_ = bf16[2,2,128,256]{3,2,1,0:T(8,128)(2,1)S(1)} collective-permute-done((bf16[2,2,128,256]{3,2,1,0:T(8,128)(2,1)S(1)}, bf16[2,2,128,256]{3,2,1,0:T(8,128)(2,1)S(1)}, u32[]{:S(2)}, u32[]{:S(2)}) %collective-permute-start.2) | collective-permute-done | bytes 262176 | tf_op jit(solution)/shard_map/ppermute | solution.py:361
  45.2 3.1 %all-to-all-done = bf16[16,3,24,256]{3,2,1,0:T(8,128)(2,1)S(1)} async-done(((bf16[16,3,24,256]{3,2,1,0:T(8,128)(2,1)}), bf16[16,3,24,256]{3,2,1,0:T(8,128)(2,1)S(1)}, u32[]{:S(2)}, u32[]{:S(2)}) %all-to-all-start) | async-done | bytes 589856 | tf_op jit(solution)/shard_map/all_to_all | solution.py:412
  49.8 2.6 %collective-permute-start.5 = (bf16[3,384,128]{2,1,0:T(8,128)(2,1)S(1)}, bf16[3,384,128]{2,1,0:T(8,128)(2,1)S(1)}, u32[]{:S(2)}, u32[]{:S(2)}) collective-permute-start(bf16[3,384,128]{2,1,0:T(8,128)(2,1)S(1)} %get-tuple-element.60.refs_1_), channel_id=1, source_target_pairs={{0,96},{16,112},{32,0},{48,16},{64,32},{80,48},{96,64},{112,80},{1... | collective-permute-start | bytes 884744 | tf_op jit(solution)/shard_map/ppermute | solution.py:361
  52.3 0.9 %slice.20 = bf16[1,2,128,256]{3,2,1,0:T(8,128)(2,1)S(1)} slice(bf16[2,2,128,256]{3,2,1,0:T(8,128)(2,1)} %get-tuple-element.43.refs_4_), slice={[1:2], [0:2], [0:128], [0:256]} | slice | bytes 262144 | tf_op jit(solution)/shard_map/slice | solution.py:423
  53.3 1.3 %collective-permute-done.8.refs_5_ = bf16[1,2,128,256]{3,2,1,0:T(8,128)(2,1)S(1)} collective-permute-done((bf16[1,2,128,256]{3,2,1,0:T(8,128)(2,1)S(1)}, bf16[1,2,128,256]{3,2,1,0:T(8,128)(2,1)S(1)}, u32[]{:S(2)}, u32[]{:S(2)}) %collective-permute-start.8) | collective-permute-done | bytes 131104 | tf_op jit(solution)/shard_map/ppermute | solution.py:364
  54.7 0.7 copy-done.18
  55.4 3.2 %collective-permute-start.14 = (bf16[3,384,128]{2,1,0:T(8,128)(2,1)S(1)}, bf16[3,384,128]{2,1,0:T(8,128)(2,1)}, u32[]{:S(2)}, u32[]{:S(2)}) collective-permute-start(bf16[3,384,128]{2,1,0:T(8,128)(2,1)S(1)} %get-tuple-element.61.refs_0_), channel_id=1, source_target_pairs={{0,96},{16,112},{32,0},{48,16},{64,32},{80,48},{96,64},{112,80},{1... | collective-permute-start | bytes 884744 | tf_op jit(solution)/shard_map/ppermute | solution.py:361
  58.6 5.4 %pairs_first.1 = (f32[3,2,256,2048]{3,2,1,0:T(8,128)}, bf16[3,512,384]{2,1,0:T(8,128)(2,1)}, f32[3,384,128]{2,1,0:T(8,128)}) custom-call(bf16[3,384,128]{2,1,0:T(8,128)(2,1)} %copy-done.3, bf16[3,384,128]{2,1,0:T(8,128)(2,1)} %copy-done.4, bf16[3,384,128]{2,1,0:T(8,128)(2,1)} %copy-done.18, bf16[3,384,128]{2,1,0:T(8,128)(2,1)} %collective-permute-done.7.refs_3_, ...), custom_call_target="tpu_custom_call" | custom-call | flops 905969664 | bytes 4915200 | tf_op jit(solution)/shard_map/pairs_first/pallas_call | solution.py:318
  64.8 1.1 %collective-permute-done.17.refs_9_ = bf16[1,2,128,256]{3,2,1,0:T(8,128)(2,1)S(1)} collective-permute-done((bf16[1,2,128,256]{3,2,1,0:T(8,128)(2,1)S(1)}, bf16[1,2,128,256]{3,2,1,0:T(8,128)(2,1)S(1)}, u32[]{:S(2)}, u32[]{:S(2)}) %collective-permute-start.17) | collective-permute-done | bytes 131104 | tf_op jit(solution)/shard_map/ppermute | solution.py:364
  66.6 2.2 %collective-permute-start.10 = (bf16[3,384,128]{2,1,0:T(8,128)(2,1)S(1)}, bf16[3,384,128]{2,1,0:T(8,128)(2,1)S(1)}, u32[]{:S(2)}, u32[]{:S(2)}) collective-permute-start(bf16[3,384,128]{2,1,0:T(8,128)(2,1)S(1)} %collective-permute-done.5.refs_5_), channel_id=1, source_target_pairs={{0,96},{16,112},{32,0},{48,16},{64,32},{80,48},{96,64},{112,80},{1... | collective-permute-start | bytes 884744 | tf_op jit(solution)/shard_map/ppermute | solution.py:361
  69.5 0.7 copy-done.10
  70.2 0.7 copy-done.11
  70.9 0.7 copy-done.12
  71.7 7.1 %pairs_middle.1 = (f32[3,2,256,2048]{3,2,1,0:T(8,128)}, f32[3,384,128]{2,1,0:T(8,128)}) custom-call(bf16[3,384,128]{2,1,0:T(8,128)(2,1)} %copy-done.5, bf16[3,384,128]{2,1,0:T(8,128)(2,1)} %collective-permute-done.11.refs_1_, bf16[3,384,128]{2,1,0:T(8,128)(2,1)} %copy-done.8, bf16[3,384,128]{2,1,0:T(8,128)(2,1)} %copy-done.11, ...), custom_call_target="tpu_custom_call", output_to_operand_aliasing={{0}: (14, {})} | custom-call | flops 1 | bytes 1 | tf_op jit(solution)/shard_map/pairs_middle/pallas_call | solution.py:318
  79.7 1.6 %collective-permute-done.21.refs_5_ = bf16[1,2,128,256]{3,2,1,0:T(8,128)(2,1)S(1)} collective-permute-done((bf16[1,2,128,256]{3,2,1,0:T(8,128)(2,1)S(1)}, bf16[1,2,128,256]{3,2,1,0:T(8,128)(2,1)S(1)}, u32[]{:S(2)}, u32[]{:S(2)}) %collective-permute-start.21) | collective-permute-done | bytes 131104 | tf_op jit(solution)/shard_map/ppermute | solution.py:364
  82.1 5.6 %pairs_last.1 = (f32[3,2,256,2048]{3,2,1,0:T(8,128)}, f32[3,128]{1,0:T(4,128)}) custom-call(bf16[3,384,128]{2,1,0:T(8,128)(2,1)} %copy-done.9, bf16[3,384,128]{2,1,0:T(8,128)(2,1)} %copy-done.7, bf16[3,384,128]{2,1,0:T(8,128)(2,1)} %copy-done.13, bf16[3,384,128]{2,1,0:T(8,128)(2,1)} %copy-done.14, ...), custom_call_target="tpu_custom_call", output_to_operand_aliasing={{0}: (8, {})} | custom-call | flops 905969664 | bytes 4915200 | tf_op jit(solution)/shard_map/pairs_last/pallas_call | solution.py:318
  (80 shorter events, 6.1 us)
Async XLA Ops:
  5.6 10.5 %collective-permute-start = (f32[3,64,256]{2,1,0:T(8,128)}, f32[3,64,256]{2,1,0:T(8,128)S(1)}, u32[]{:S(2)}, u32[]{:S(2)}) collective-permute-start(f32[3,64,256]{2,1,0:T(8,128)} %get-tuple-element.37), channel_id=1, source_target_pairs={{0,1},{1,2},{2,3},{3,4},{4,5},{5,6},{6,7},{7,8},{8,9},{9,10},{10,1... | collective-permute-start | bytes 589832 | tf_op jit(solution)/shard_map/ppermute | solution.py:379
  12.9 16.3 %collective-permute-start.1 = (bf16[2,2,128,256]{3,2,1,0:T(8,128)(2,1)}, bf16[2,2,128,256]{3,2,1,0:T(8,128)(2,1)S(1)}, u32[]{:S(2)}, u32[]{:S(2)}) collective-permute-start(bf16[2,2,128,256]{3,2,1,0:T(8,128)(2,1)} %get-tuple-element.38), channel_id=1, source_target_pairs={{0,64},{16,80},{32,96},{48,112},{64,0},{80,16},{96,32},{112,48},{1... | collective-permute-start | bytes 786440 | tf_op jit(solution)/shard_map/ppermute | solution.py:361
  29.2 50.4 %copy-start = (bf16[2,2,128,256]{3,2,1,0:T(8,128)(2,1)}, bf16[2,2,128,256]{3,2,1,0:T(8,128)(2,1)S(1)}, u32[]{:S(2)}) copy-start(bf16[2,2,128,256]{3,2,1,0:T(8,128)(2,1)S(1)} %collective-permute-done.1.refs_4_) | copy-start | bytes 786436
  29.3 19.1 %all-to-all-start = ((bf16[16,3,24,256]{3,2,1,0:T(8,128)(2,1)}), bf16[16,3,24,256]{3,2,1,0:T(8,128)(2,1)S(1)}, u32[]{:S(2)}, u32[]{:S(2)}) async-start(bf16[16,3,24,256]{3,2,1,0:T(8,128)(2,1)} %bitcast.8), calls=%async_computation | async-start | bytes 1179648 | tf_op jit(solution)/shard_map/all_to_all | solution.py:412
  36.7 8.5 %collective-permute-start.2 = (bf16[2,2,128,256]{3,2,1,0:T(8,128)(2,1)S(1)}, bf16[2,2,128,256]{3,2,1,0:T(8,128)(2,1)S(1)}, u32[]{:S(2)}, u32[]{:S(2)}) collective-permute-start(bf16[2,2,128,256]{3,2,1,0:T(8,128)(2,1)S(1)} %copy-done.20), channel_id=1, source_target_pairs={{0,32},{16,48},{32,64},{48,80},{64,96},{80,112},{96,0},{112,16},{1... | collective-permute-start | bytes 786440 | tf_op jit(solution)/shard_map/ppermute | solution.py:361
  37.5 7.7 %collective-permute-start.3 = (bf16[2,2,128,256]{3,2,1,0:T(8,128)(2,1)S(1)}, bf16[2,2,128,256]{3,2,1,0:T(8,128)(2,1)S(1)}, u32[]{:S(2)}, u32[]{:S(2)}) collective-permute-start(bf16[2,2,128,256]{3,2,1,0:T(8,128)(2,1)S(1)} %copy-done.19), channel_id=1, source_target_pairs={{0,96},{16,112},{32,0},{48,16},{64,32},{80,48},{96,64},{112,80},{1... | collective-permute-start | bytes 786440 | tf_op jit(solution)/shard_map/ppermute | solution.py:361
  48.5 6.2 %collective-permute-start.6 = (bf16[3,384,128]{2,1,0:T(8,128)(2,1)S(1)}, bf16[3,384,128]{2,1,0:T(8,128)(2,1)S(1)}, u32[]{:S(2)}, u32[]{:S(2)}) collective-permute-start(bf16[3,384,128]{2,1,0:T(8,128)(2,1)S(1)} %get-tuple-element.61.refs_0_), channel_id=1, source_target_pairs={{0,16},{16,0},{32,48},{48,32},{64,80},{80,64},{96,112},{112,96},{1... | collective-permute-start | bytes 884744 | tf_op jit(solution)/shard_map/ppermute | solution.py:364
  48.6 10.0 %collective-permute-start.7 = (bf16[3,384,128]{2,1,0:T(8,128)(2,1)S(1)}, bf16[3,384,128]{2,1,0:T(8,128)(2,1)}, u32[]{:S(2)}, u32[]{:S(2)}) collective-permute-start(bf16[3,384,128]{2,1,0:T(8,128)(2,1)S(1)} %get-tuple-element.60.refs_1_), channel_id=1, source_target_pairs={{0,16},{16,0},{32,48},{48,32},{64,80},{80,64},{96,112},{112,96},{1... | collective-permute-start | bytes 884744 | tf_op jit(solution)/shard_map/ppermute | solution.py:364
  49.1 14.9 %collective-permute-start.4 = (bf16[3,384,128]{2,1,0:T(8,128)(2,1)S(1)}, bf16[3,384,128]{2,1,0:T(8,128)(2,1)S(1)}, u32[]{:S(2)}, u32[]{:S(2)}) collective-permute-start(bf16[3,384,128]{2,1,0:T(8,128)(2,1)S(1)} %get-tuple-element.61.refs_0_), channel_id=1, source_target_pairs={{0,32},{16,48},{32,64},{48,80},{64,96},{80,112},{96,0},{112,16},{1... | collective-permute-start | bytes 884744 | tf_op jit(solution)/shard_map/ppermute | solution.py:361
  49.8 14.3 %collective-permute-start.5 = (bf16[3,384,128]{2,1,0:T(8,128)(2,1)S(1)}, bf16[3,384,128]{2,1,0:T(8,128)(2,1)S(1)}, u32[]{:S(2)}, u32[]{:S(2)}) collective-permute-start(bf16[3,384,128]{2,1,0:T(8,128)(2,1)S(1)} %get-tuple-element.60.refs_1_), channel_id=1, source_target_pairs={{0,96},{16,112},{32,0},{48,16},{64,32},{80,48},{96,64},{112,80},{1... | collective-permute-start | bytes 884744 | tf_op jit(solution)/shard_map/ppermute | solution.py:361
  53.3 1.4 %collective-permute-start.8 = (bf16[1,2,128,256]{3,2,1,0:T(8,128)(2,1)S(1)}, bf16[1,2,128,256]{3,2,1,0:T(8,128)(2,1)S(1)}, u32[]{:S(2)}, u32[]{:S(2)}) collective-permute-start(bf16[1,2,128,256]{3,2,1,0:T(8,128)(2,1)S(1)} %slice.20), channel_id=1, source_target_pairs={{0,16},{16,0},{32,48},{48,32},{64,80},{80,64},{96,112},{112,96},{1... | collective-permute-start | bytes 393224 | tf_op jit(solution)/shard_map/ppermute | solution.py:364
  54.7 11.4 %collective-permute-start.11 = (bf16[3,384,128]{2,1,0:T(8,128)(2,1)S(1)}, bf16[3,384,128]{2,1,0:T(8,128)(2,1)}, u32[]{:S(2)}, u32[]{:S(2)}) collective-permute-start(bf16[3,384,128]{2,1,0:T(8,128)(2,1)S(1)} %get-tuple-element.60.refs_1_), channel_id=1, source_target_pairs={{0,32},{16,48},{32,64},{48,80},{64,96},{80,112},{96,0},{112,16},{1... | collective-permute-start | bytes 884744 | tf_op jit(solution)/shard_map/ppermute | solution.py:361
  55.4 11.0 %collective-permute-start.14 = (bf16[3,384,128]{2,1,0:T(8,128)(2,1)S(1)}, bf16[3,384,128]{2,1,0:T(8,128)(2,1)}, u32[]{:S(2)}, u32[]{:S(2)}) collective-permute-start(bf16[3,384,128]{2,1,0:T(8,128)(2,1)S(1)} %get-tuple-element.61.refs_0_), channel_id=1, source_target_pairs={{0,96},{16,112},{32,0},{48,16},{64,32},{80,48},{96,64},{112,80},{1... | collective-permute-start | bytes 884744 | tf_op jit(solution)/shard_map/ppermute | solution.py:361
  64.1 4.8 %collective-permute-start.12 = (bf16[3,384,128]{2,1,0:T(8,128)(2,1)S(1)}, bf16[3,384,128]{2,1,0:T(8,128)(2,1)S(1)}, u32[]{:S(2)}, u32[]{:S(2)}) collective-permute-start(bf16[3,384,128]{2,1,0:T(8,128)(2,1)S(1)} %collective-permute-done.4.refs_0_), channel_id=1, source_target_pairs={{0,16},{16,0},{32,48},{48,32},{64,80},{80,64},{96,112},{112,96},{1... | collective-permute-start | bytes 884744 | tf_op jit(solution)/shard_map/ppermute | solution.py:364
  64.2 1.7 %collective-permute-start.17 = (bf16[1,2,128,256]{3,2,1,0:T(8,128)(2,1)S(1)}, bf16[1,2,128,256]{3,2,1,0:T(8,128)(2,1)S(1)}, u32[]{:S(2)}, u32[]{:S(2)}) collective-permute-start(bf16[1,2,128,256]{3,2,1,0:T(8,128)(2,1)S(1)} %slice.21), channel_id=1, source_target_pairs={{0,16},{16,0},{32,48},{48,32},{64,80},{80,64},{96,112},{112,96},{1... | collective-permute-start | bytes 393224 | tf_op jit(solution)/shard_map/ppermute | solution.py:364
  64.7 1.9 %collective-permute-start.18 = (bf16[1,2,128,256]{3,2,1,0:T(8,128)(2,1)S(1)}, bf16[1,2,128,256]{3,2,1,0:T(8,128)(2,1)S(1)}, u32[]{:S(2)}, u32[]{:S(2)}) collective-permute-start(bf16[1,2,128,256]{3,2,1,0:T(8,128)(2,1)S(1)} %slice.22), channel_id=1, source_target_pairs={{0,16},{16,0},{32,48},{48,32},{64,80},{80,64},{96,112},{112,96},{1... | collective-permute-start | bytes 393224 | tf_op jit(solution)/shard_map/ppermute | solution.py:364
  65.9 2.9 %collective-permute-start.16 = (bf16[3,384,128]{2,1,0:T(8,128)(2,1)S(1)}, bf16[3,384,128]{2,1,0:T(8,128)(2,1)S(1)}, u32[]{:S(2)}, u32[]{:S(2)}) collective-permute-start(bf16[3,384,128]{2,1,0:T(8,128)(2,1)S(1)} %collective-permute-done.5.refs_5_), channel_id=1, source_target_pairs={{0,16},{16,0},{32,48},{48,32},{64,80},{80,64},{96,112},{112,96},{1... | collective-permute-start | bytes 884744 | tf_op jit(solution)/shard_map/ppermute | solution.py:364
  66.1 3.4 %collective-permute-start.13 = (bf16[3,384,128]{2,1,0:T(8,128)(2,1)}, bf16[3,384,128]{2,1,0:T(8,128)(2,1)S(1)}, u32[]{:S(2)}, u32[]{:S(2)}) collective-permute-start(bf16[3,384,128]{2,1,0:T(8,128)(2,1)} %collective-permute-done.11.refs_1_), channel_id=1, source_target_pairs={{0,16},{16,0},{32,48},{48,32},{64,80},{80,64},{96,112},{112,96},{1... | collective-permute-start | bytes 884744 | tf_op jit(solution)/shard_map/ppermute | solution.py:364
  66.4 3.8 %collective-permute-start.15 = (bf16[3,384,128]{2,1,0:T(8,128)(2,1)}, bf16[3,384,128]{2,1,0:T(8,128)(2,1)S(1)}, u32[]{:S(2)}, u32[]{:S(2)}) collective-permute-start(bf16[3,384,128]{2,1,0:T(8,128)(2,1)} %collective-permute-done.14.refs_4_), channel_id=1, source_target_pairs={{0,16},{16,0},{32,48},{48,32},{64,80},{80,64},{96,112},{112,96},{1... | collective-permute-start | bytes 884744 | tf_op jit(solution)/shard_map/ppermute | solution.py:364
  66.6 12.2 %collective-permute-start.10 = (bf16[3,384,128]{2,1,0:T(8,128)(2,1)S(1)}, bf16[3,384,128]{2,1,0:T(8,128)(2,1)S(1)}, u32[]{:S(2)}, u32[]{:S(2)}) collective-permute-start(bf16[3,384,128]{2,1,0:T(8,128)(2,1)S(1)} %collective-permute-done.5.refs_5_), channel_id=1, source_target_pairs={{0,96},{16,112},{32,0},{48,16},{64,32},{80,48},{96,64},{112,80},{1... | collective-permute-start | bytes 884744 | tf_op jit(solution)/shard_map/ppermute | solution.py:361
  68.8 10.3 %collective-permute-start.9 = (bf16[3,384,128]{2,1,0:T(8,128)(2,1)S(1)}, bf16[3,384,128]{2,1,0:T(8,128)(2,1)S(1)}, u32[]{:S(2)}, u32[]{:S(2)}) collective-permute-start(bf16[3,384,128]{2,1,0:T(8,128)(2,1)S(1)} %collective-permute-done.4.refs_0_), channel_id=1, source_target_pairs={{0,32},{16,48},{32,64},{48,80},{64,96},{80,112},{96,0},{112,16},{1... | collective-permute-start | bytes 884744 | tf_op jit(solution)/shard_map/ppermute | solution.py:361
  79.1 2.2 %collective-permute-start.19 = (bf16[3,384,128]{2,1,0:T(8,128)(2,1)S(1)}, bf16[3,384,128]{2,1,0:T(8,128)(2,1)S(1)}, u32[]{:S(2)}, u32[]{:S(2)}) collective-permute-start(bf16[3,384,128]{2,1,0:T(8,128)(2,1)S(1)} %collective-permute-done.9.refs_0_), channel_id=1, source_target_pairs={{0,16},{16,0},{32,48},{48,32},{64,80},{80,64},{96,112},{112,96},{1... | collective-permute-start | bytes 884744 | tf_op jit(solution)/shard_map/ppermute | solution.py:364
  79.1 2.2 %collective-permute-start.20 = (bf16[3,384,128]{2,1,0:T(8,128)(2,1)S(1)}, bf16[3,384,128]{2,1,0:T(8,128)(2,1)S(1)}, u32[]{:S(2)}, u32[]{:S(2)}) collective-permute-start(bf16[3,384,128]{2,1,0:T(8,128)(2,1)S(1)} %collective-permute-done.10.refs_1_), channel_id=1, source_target_pairs={{0,16},{16,0},{32,48},{48,32},{64,80},{80,64},{96,112},{112,96},{1... | collective-permute-start | bytes 884744 | tf_op jit(solution)/shard_map/ppermute | solution.py:364
  79.6 1.7 %collective-permute-start.21 = (bf16[1,2,128,256]{3,2,1,0:T(8,128)(2,1)S(1)}, bf16[1,2,128,256]{3,2,1,0:T(8,128)(2,1)S(1)}, u32[]{:S(2)}, u32[]{:S(2)}) collective-permute-start(bf16[1,2,128,256]{3,2,1,0:T(8,128)(2,1)S(1)} %slice.23), channel_id=1, source_target_pairs={{0,16},{16,0},{32,48},{48,32},{64,80},{80,64},{96,112},{112,96},{1... | collective-permute-start | bytes 393224 | tf_op jit(solution)/shard_map/ppermute | solution.py:364
  (22 other events, 161.4 us)

commit v3 on v2

v3 whole, which is shorter than its diff:
```python
import functools
import math

import jax
import jax.numpy as jnp
import ml_dtypes
import numpy as np
from jax import lax
from jax.experimental import pallas as pl
from jax.experimental.pallas import tpu as pltpu
from jax.sharding import PartitionSpec as P

NFFT = 2048
TAPS = 4
AHEAD = 2
WIDE_VMEM = 62 * 1024 * 1024
NT = (((1,), (1,)), ((), ()))


def tap_transform(channels):
    length = TAPS * NFFT
    positions = np.arange(length, dtype=np.float64)
    coeffs = np.sinc((positions - 0.5 * length + 0.5) / NFFT)
    coeffs = coeffs * (0.5 - 0.5 * np.cos(2.0 * math.pi * (positions + 0.5) / length))
    coeffs = coeffs * np.sqrt(NFFT / np.sum(coeffs * coeffs))
    coeffs = coeffs.reshape(TAPS, NFFT)
    angles = (np.arange(channels)[:, None] * np.arange(NFFT)[None, :] % NFFT) * (2.0 * math.pi / NFFT)
    rows = np.stack([np.cos(angles), -np.sin(angles)], axis=1) / math.sqrt(NFFT)
    rows = rows.reshape(2 * channels, NFFT)
    full = (coeffs[:, None, :] * rows[None]).reshape(TAPS * 2 * channels, NFFT)
    high = full.astype(ml_dtypes.bfloat16)
    low = (full - high.astype(np.float64)).astype(ml_dtypes.bfloat16)
    return high, low


def frame_loop(
    tables_hbm, volts_hbm, tables, frames, table_sems, frame_sems, total_ref, first, extra
):
    count = frames.shape[0]
    rows = total_ref.shape[1]

    table_copies = [
        pltpu.make_async_copy(source, target, table_sems.at[i])
        for i, (source, target) in enumerate(zip(tables_hbm, tables))
    ]
    high, low = tables

    def frame_copy(i):
        at = pl.multiple_of((first + i) * NFFT, NFFT)
        return pltpu.make_async_copy(
            volts_hbm.at[:, pl.ds(at, NFFT)], frames.at[i], frame_sems.at[i]
        )

    for copy in table_copies:
        copy.start()
    for i in range(AHEAD):
        frame_copy(i).start()
    extra(0)
    for copy in table_copies:
        copy.wait()

    def step(i, _):
        @pl.when(i + AHEAD < count)
        def _():
            frame_copy(i + AHEAD).start()

        frame_copy(i).wait()
        frame = frames[i]
        product = lax.dot_general(high[...], frame, NT, preferred_element_type=jnp.float32)
        product = product + lax.dot_general(
            low[...], frame, NT, preferred_element_type=jnp.float32
        )
        for tap in range(TAPS):
            at = i + TAPS - 1 - tap
            total_ref[at] = total_ref[at] + product[tap * rows : (tap + 1) * rows]
        extra(i)
        return 0

    lax.fori_loop(0, count, step, 0)


def last_frames_kernel(
    first, high_hbm, low_hbm, volts_hbm, own_ref, next_ref,
    total, high, low, frames, table_sems, frame_sems,
):
    total[...] = jnp.zeros_like(total)
    frame_loop(
        (high_hbm, low_hbm), volts_hbm, (high, low), frames, table_sems, frame_sems,
        total, first, lambda i: None,
    )
    own_ref[...] = total[: TAPS - 1]
    next_ref[...] = total[TAPS - 1 :]


def first_frames_kernel(
    allocation_hbm, high_hbm, low_hbm, volts_hbm, last_ref, carry_ref, out_ref,
    total, hot, spectra, allocation_ref, allocation_sem, high, low, frames, table_sems, frame_sems,
):
    allocation_copy = pltpu.make_async_copy(allocation_hbm, allocation_ref, allocation_sem)
    allocation_copy.start()
    count, rows, width = total.shape
    slots, owners = allocation_ref.shape
    late = last_ref.shape[0]
    done = count - late
    total[:late] = carry_ref[...]
    total[late:done] = jnp.zeros((done - late, rows, width), jnp.float32)
    total[done:] = last_ref[...]
    size = 2 * count
    group = 2 * slots * size
    shape = (size, count * rows)
    row = lax.broadcasted_iota(jnp.int32, shape, 0)
    part = (row >= count).astype(jnp.int32)
    offset = lax.broadcasted_iota(jnp.int32, shape, 1) - (row - part * count) * rows - part

    allocation_copy.wait()

    def choose(i):
        pair = jnp.minimum(i, owners // 2 - 1)
        chosen = []
        for owner in range(2):
            for slot in range(slots):
                channel = allocation_ref[slot, 2 * pair + owner]
                wanted = jnp.where(channel >= 0, 2 * channel, -2 * count * rows)
                chosen.append(jnp.where(offset == wanted, 1.0, 0.0))
        hot[pl.ds(pl.multiple_of(pair * group, group), group)] = jnp.concatenate(
            chosen, axis=0
        ).astype(jnp.bfloat16)

    frame_loop(
        (high_hbm, low_hbm), volts_hbm, (high, low), frames, table_sems, frame_sems,
        total, 0, choose,
    )
    for t in range(count):
        spectra[pl.ds(t * rows, rows)] = total[t].astype(jnp.bfloat16)

    def write(i, _):
        at = pl.ds(pl.multiple_of(i * 4 * group, 4 * group), 4 * group)
        out_ref[at] = jnp.dot(hot[at], spectra[...], preferred_element_type=jnp.float32).astype(
            jnp.bfloat16
        )
        return 0

    lax.fori_loop(0, owners // 8, write, 0)


def filter_scratch(tables, feeds, count):
    return [pltpu.VMEM(table.shape, table.dtype) for table in tables] + [
        pltpu.VMEM((count, feeds, NFFT), jnp.bfloat16),
        pltpu.SemaphoreType.DMA((2,)),
        pltpu.SemaphoreType.DMA((count,)),
    ]


def order_kernel(order_ref, weights_ref, *out_refs):
    beams = weights_ref.shape[1]
    devices, share = order_ref.shape
    chips = len(out_refs)
    me = lax.axis_index("feed")
    chip, core = me // 2, me % 2
    numbers = order_ref[...].astype(jnp.float32).T
    of_device = lax.broadcasted_iota(jnp.int32, numbers.shape, 1)
    place = lax.broadcasted_iota(jnp.int32, (share, beams), 1)
    for ahead, out_ref in enumerate(out_refs):
        to = lax.rem(chip + ahead, chips)
        hot = []
        for other in range(2):
            device = 2 * to + (core if other == 0 else 1 - core)
            wanted = jnp.sum(jnp.where(of_device == device, numbers, 0.0), axis=1, keepdims=True)
            hot.append(jnp.where(place == wanted.astype(jnp.int32), 1.0, 0.0).astype(jnp.bfloat16))
        hot = jnp.concatenate(hot, axis=0)
        for part in range(2):
            rows = jnp.dot(hot, weights_ref[part], preferred_element_type=jnp.float32)
            rows = rows.astype(jnp.bfloat16)
            out_ref[0, part] = rows[:share]
            out_ref[1, part] = rows[share:]


def swap_parts(values, half, axis):
    count = values.shape[axis]
    place = lax.broadcasted_iota(jnp.int32, values.shape, axis)
    ahead = pltpu.roll(values, count - half, axis)
    behind = pltpu.roll(values, half, axis)
    return jnp.where(place % (2 * half) < half, ahead, -behind)


def gather_kernel(behind, half, scale, *refs):
    refs = list(refs)
    pairs = len(behind)
    block_refs = refs[: 4 * pairs]
    weight_refs = refs[4 * pairs : 6 * pairs]
    vis_hbm, power_ref, values, weights, left, voltages, out, sems, weight_sems, out_sems = refs[
        6 * pairs :
    ]
    slots, rows, narrow = values.shape[2:]
    width = 2 * narrow
    chips = vis_hbm.shape[3] // (2 * width)
    me = lax.axis_index("feed")
    chip, core = me // 2, me % 2

    copies = []
    for pair in range(pairs):
        copies.append(
            [
                pltpu.make_async_copy(
                    block_refs[4 * pair + i], values.at[pair, i], sems.at[pair, i]
                )
                for i in range(4)
            ]
            + [
                pltpu.make_async_copy(
                    weight_refs[2 * pair + i].at[0], weights.at[pair, i], weight_sems.at[pair, i]
                )
                for i in range(2)
            ]
        )
        for copy in copies[pair]:
            copy.start()

    def out_copy(pair, slot):
        to = lax.rem(chip + chips - behind[pair], chips)
        at = pl.multiple_of(to * 2 * width, 2 * width)
        return pltpu.make_async_copy(
            out.at[pair, slot],
            vis_hbm.at[slot, :, :, pl.ds(at, 2 * width)],
            out_sems.at[pair, slot],
        )

    for pair in range(pairs):
        for copy in copies[pair]:
            copy.wait()
        for slot in range(slots):
            feeds = [
                jnp.concatenate([values[pair, 2 * i, slot], values[pair, 2 * i + 1, slot]], axis=1)
                for i in range(2)
            ]
            if pair == 0:
                own = feeds[0].astype(jnp.float32).T
                left[slot] = jnp.concatenate([own, swap_parts(own, half, 1)], axis=0).astype(
                    jnp.bfloat16
                )
            voltage = None if pair == 0 else voltages[slot]
            for side, at in ((0, core), (1, 1 - core)):
                product = (
                    jnp.dot(left[slot], feeds[side], preferred_element_type=jnp.float32) * scale
                )
                columns = pl.ds(pl.multiple_of(at * width, width), width)
                out[pair, slot, 0, :, columns] = product[:width]
                out[pair, slot, 1, :, columns] = product[width:]
                weight = weights[pair, side]
                weight = weight.reshape(weight.shape[0] * weight.shape[1], width)
                term = lax.dot_general(
                    feeds[side], weight, NT, preferred_element_type=jnp.float32
                )
                voltage = term if voltage is None else voltage + term
            out_copy(pair, slot).start()
            if pair < pairs - 1:
                voltages[slot] = voltage
            else:
                share = voltage.shape[1] // 2
                beam = voltage[:, :share] - swap_parts(voltage[:, share:], half, 0)
                power_ref[pl.ds(slot, 1), :] = jnp.sum(beam * beam, axis=0, keepdims=True) * scale
    for pair in range(pairs):
        for slot in range(slots):
            out_copy(pair, slot).wait()


def params():
    return pltpu.CompilerParams(vmem_limit_bytes=WIDE_VMEM)


def gather_call(behind, half, scale, devices, blocks, weights):
    pairs = len(behind)
    slots, rows, narrow = blocks[0].shape
    width = 2 * narrow
    _, parts, share, _ = weights[0].shape
    anywhere = pl.BlockSpec(memory_space=pl.ANY)
    args = list(blocks) + list(weights)
    flops = pairs * 4 * slots * rows * width * (2 * width + parts * share)
    moved = pairs * slots * 2 * width * 2 * width * 4 + 6 * slots * rows * width
    return pl.pallas_call(
        functools.partial(gather_kernel, behind, half, scale),
        out_shape=[
            jax.ShapeDtypeStruct((slots, 2, width, devices * width), jnp.float32),
            jax.ShapeDtypeStruct((slots, share), jnp.float32),
        ],
        in_specs=[anywhere] * len(args),
        out_specs=[anywhere, pl.BlockSpec(memory_space=pltpu.VMEM)],
        scratch_shapes=[
            pltpu.VMEM((pairs, 4, slots, rows, narrow), jnp.bfloat16),
            pltpu.VMEM((pairs, 2, parts, share, width), jnp.bfloat16),
            pltpu.VMEM((slots, 2 * width, rows), jnp.bfloat16),
            pltpu.VMEM((slots, rows, parts * share), jnp.float32),
            pltpu.VMEM((pairs, slots, 2, width, 2 * width), jnp.float32),
            pltpu.SemaphoreType.DMA((pairs, 4)),
            pltpu.SemaphoreType.DMA((pairs, 2)),
            pltpu.SemaphoreType.DMA((pairs, slots)),
        ],
        compiler_params=params(),
        cost_estimate=pl.CostEstimate(flops=flops, bytes_accessed=moved, transcendentals=0),
        name="gathered",
    )(*args)


def shards(volts, beam_weights, allocation, beam_order):
    feeds_dev = volts.shape[0]
    frames_dev = volts.shape[1] // NFFT
    owners = lax.axis_size("freq")
    devices = lax.axis_size("feed")
    total_frames = frames_dev * owners
    slots_dev = allocation.shape[1]
    channels = (slots_dev - 1) * allocation.shape[0]
    rows = 2 * channels
    late = TAPS - 1
    early = frames_dev - late
    beams = beam_weights.shape[1]
    share = beams // devices
    f32, bf16 = jnp.float32, jnp.bfloat16
    tables = [jnp.asarray(x) for x in tap_transform(channels)]
    frame_flops = 4 * tables[0].shape[0] * feeds_dev * NFFT
    anywhere = pl.BlockSpec(memory_space=pl.ANY)
    in_vmem = pl.BlockSpec(memory_space=pltpu.VMEM)

    def moved(x, by):
        return lax.ppermute(x, "feed", [(i, (i + by) % devices) for i in range(devices)])

    def swapped(x):
        return lax.ppermute(x, "feed", [(i, i ^ 1) for i in range(devices)])

    own_last, next_first = pl.pallas_call(
        functools.partial(last_frames_kernel, early),
        out_shape=[jax.ShapeDtypeStruct((late, rows, feeds_dev), f32)] * 2,
        in_specs=[anywhere] * 3,
        out_specs=[in_vmem, in_vmem],
        scratch_shapes=[pltpu.VMEM((2 * late, rows, feeds_dev), f32)]
        + filter_scratch(tables, feeds_dev, late),
        compiler_params=pltpu.CompilerParams(vmem_limit_bytes=WIDE_VMEM),
        cost_estimate=pl.CostEstimate(
            flops=late * frame_flops, bytes_accessed=late * feeds_dev * NFFT * 2, transcendentals=0
        ),
        name="last_frames",
    )(*tables, volts)
    carry = lax.ppermute(next_first, "freq", [(i, i + 1) for i in range(owners - 1)])
    ordered = pl.pallas_call(
        order_kernel,
        out_shape=[jax.ShapeDtypeStruct((2, 2, share, feeds_dev), bf16)] * (devices // 2),
        compiler_params=params(),
        cost_estimate=pl.CostEstimate(
            flops=4 * beams * beams * feeds_dev, bytes_accessed=4 * beams * feeds_dev, transcendentals=0
        ),
        name="order_beams",
    )(beam_order.reshape(devices, share), beam_weights)
    own_last, *ordered = lax.optimization_barrier((own_last, *ordered))
    weights = [ordered[0], moved(ordered[1], 2), moved(ordered[3], -2), moved(ordered[2], 4)]
    chosen_rows = owners * slots_dev * 2 * frames_dev
    outgoing = pl.pallas_call(
        first_frames_kernel,
        out_shape=jax.ShapeDtypeStruct((chosen_rows, feeds_dev), bf16),
        in_specs=[anywhere] * 4 + [in_vmem] * 2,
        out_specs=in_vmem,
        scratch_shapes=[
            pltpu.VMEM((frames_dev, rows, feeds_dev), f32),
            pltpu.VMEM((chosen_rows, frames_dev * rows), bf16),
            pltpu.VMEM((frames_dev * rows, feeds_dev), bf16),
            pltpu.SMEM((slots_dev, owners), jnp.int32),
            pltpu.SemaphoreType.DMA,
        ]
        + filter_scratch(tables, feeds_dev, early),
        compiler_params=pltpu.CompilerParams(vmem_limit_bytes=WIDE_VMEM),
        cost_estimate=pl.CostEstimate(
            flops=early * frame_flops, bytes_accessed=early * feeds_dev * NFFT * 2, transcendentals=0
        ),
        name="first_frames",
    )(allocation.T, *tables, volts, own_last, carry)
    outgoing, weights[3] = lax.optimization_barrier((outgoing, weights[3]))
    received = lax.all_to_all(
        outgoing.reshape(owners, slots_dev, 2 * frames_dev, feeds_dev),
        "freq",
        split_axis=0,
        concat_axis=0,
        tiled=True,
    )

    weights_other = [swapped(weights[0][1:]), None, None, swapped(weights[3][1:])]
    received, weights[1], weights[2], weights_other[0], weights_other[3] = lax.optimization_barrier(
        (received, weights[1], weights[2], weights_other[0], weights_other[3])
    )

    own = received.transpose(1, 0, 2, 3).reshape(slots_dev, 2 * total_frames, feeds_dev)
    narrow = feeds_dev // 2
    own = [own[:, :, :narrow], own[:, :, narrow:]]
    up = [moved(own[0], 2)]
    down = [None, moved(own[1], -2)]
    up.append(moved(own[1], 2))
    down[0] = moved(own[0], -2)
    far = [moved(up[0], 2), moved(down[1], -2)]
    sibling = [swapped(x) for x in own]
    up_other = [swapped(x) for x in up]
    down_other = [swapped(x) for x in down]
    weights_other[1:3] = [swapped(x[1:]) for x in weights[1:3]]
    far_other = [swapped(x) for x in far]
    by_chip = [[weights[d], weights_other[d]] for d in range(4)]
    vis, power = gather_call(
        (0, 1, -1, 2),
        half=frames_dev,
        scale=1.0 / total_frames,
        devices=devices,
        blocks=own + sibling + up + up_other + down + down_other + far + far_other,
        weights=[x for d in range(4) for x in by_chip[d]],
    )
    return (vis, power.T)


def solution(mesh):
    in_specs = (P("feed", "freq"), P(None, None, "feed"), P(), P())
    out_specs = (P("freq", None, "feed", None), P("feed", "freq"))
    return jax.shard_map(shards, mesh=mesh, in_specs=in_specs, out_specs=out_specs, check_vma=False)
```

time: 89.2 us -> 84.8 us (0.951)
  waiting for transfers between devices: 12.6 us -> 24.1 us
  Pallas kernels: 38.9 us -> 29.7 us
  local copies, waits for them, and re-layouts: 6.2 us -> 2.51 us
  starting transfers between devices: 29.2 us -> 25.7 us
    ppermute x9, waiting for transfers between devices: 5.47 us -> 18 us  [moved(): lax.ppermute(x, 'feed', [(i, (i + by) % devices) for i in range(devices)])]
    pallas_call x3 -> x1, Pallas kernels: 18.1 us -> 9.3 us  [gather_call(): pl.pallas_call(functools.partial(gather_kernel, behind, half, scale), out...]
    ppermute x9, starting transfers between devices: 15.1 us -> 11.9 us  [moved(): lax.ppermute(x, 'feed', [(i, (i + by) % devices) for i in range(devices)])]
    unnamed x46 -> x52, local copies, waits for them, and re-layouts: 5.12 us -> 2.33 us
    ppermute x12, waiting for transfers between devices: 3.99 us -> 3 us  [swapped(): return lax.ppermute(x, 'feed', [(i, i ^ 1) for i in range(devices)])]
    slice x4, local copies, waits for them, and re-layouts: 0.94 us -> 0.04 us  [the longest x2 0.02 us: shards(): weights_other[1:3] = [swapped(x[1:]) for x in weights[1:3]]]
  transfers between devices with their start and end apart: 23 -> 23, of which waited for: 6 -> 9; matrix products, arithmetic and copies ran while one was open for 1% -> 0% of each run, Pallas kernels for 32% -> 19%
where the time goes in v3:
time: 84.8 us; the launch traced here: 83.2 us
  Pallas kernels  29.7 us (35%)
  starting transfers between devices  25.7 us (30%)
  waiting for transfers between devices  24.1 us (28%)
  local copies, waits for them, and re-layouts  2.51 us (3%)
  between operations  1.18 us (1%)
    ppermute x9, waiting for transfers between devices, moved(): lax.ppermute(x, 'feed', [(i, (i + by) % devices) for i in range(devices)])  18 us
    pallas_call x1, Pallas kernels, shards(): pl.pallas_call(first_frames_kernel, out_shape=jax.ShapeDtypeStruct((chose...  12.1 us
    ppermute x9, starting transfers between devices, moved(): lax.ppermute(x, 'feed', [(i, (i + by) % devices) for i in range(devices)])  11.9 us
    pallas_call x1, Pallas kernels, gather_call(): pl.pallas_call(functools.partial(gather_kernel, behind, half, scale), out...  9.3 us
    all_to_all x1, starting transfers between devices, shards(): lax.all_to_all(outgoing.reshape(owners, slots_dev, 2 * frames_dev, feeds_...  7.42 us
    pallas_call x1, Pallas kernels, shards(): pl.pallas_call(functools.partial(last_frames_kernel, early), out_shape=[j...  4.91 us
    ppermute x1, starting transfers between devices, shards(): lax.ppermute(next_first, 'freq', [(i, i + 1) for i in range(owners - 1)])  3.96 us
    pallas_call x1, Pallas kernels, shards(): pl.pallas_call(order_kernel, out_shape=[jax.ShapeDtypeStruct((2, 2, share...  3.37 us
  transfers between devices with their start and end apart: 23, of which 9 were waited for; matrix products, arithmetic and copies ran while one was open for 0% of the time, Pallas kernels for 19%

profile of v3, /device:TPU:0, one launch (start us, length us, event | category | flops | bytes accessed | tf_op | source)
XLA Modules:
  0.0 83.2 jit_solution(9570791116406290785)
XLA Ops:
  0.6 4.9 %last_frames.1 = (f32[3,64,256]{2,1,0:T(8,128)}, f32[3,64,256]{2,1,0:T(8,128)}) custom-call(bf16[256,2048]{1,0:T(8,128)(2,1)} %constant.4.clone.high_hbm, bf16[256,2048]{1,0:T(8,128)(2,1)} %constant.5.clone.low_hbm, bf16[256,24576]{1,0:T(8,128)(2,1)} %volts_hbm.3), custom_call_target="tpu_custom_call" | custom-call | flops 1610612736 | bytes 3145728 | tf_op jit(solution)/shard_map/last_frames/pallas_call | solution.py:329
  5.5 4.0 %collective-permute-start = (f32[3,64,256]{2,1,0:T(8,128)}, f32[3,64,256]{2,1,0:T(8,128)S(1)}, u32[]{:S(2)}, u32[]{:S(2)}) collective-permute-start(f32[3,64,256]{2,1,0:T(8,128)} %get-tuple-element.28), channel_id=1, source_target_pairs={{0,1},{1,2},{2,3},{3,4},{4,5},{5,6},{6,7},{7,8},{8,9},{9,10},{10,1... | collective-permute-start | bytes 589832 | tf_op jit(solution)/shard_map/ppermute | solution.py:342
  9.5 3.4 %order_beams.1 = (bf16[2,2,128,256]{3,2,1,0:T(8,128)(2,1)}, bf16[2,2,128,256]{3,2,1,0:T(8,128)(2,1)}, bf16[2,2,128,256]{3,2,1,0:T(8,128)(2,1)}, bf16[2,2,128,256]{3,2,1,0:T(8,128)(2,1)}) custom-call(s32[8,128]{1,0:T(8,128)} %bitcast.9, bf16[2,1024,256]{2,1,0:T(8,128)(2,1)} %weights_ref.1), custom_call_target="tpu_custom_call" | custom-call | flops 1073741824 | bytes 1048576 | tf_op jit(solution)/shard_map/order_beams/pallas_call | solution.py:343
  12.9 3.2 %collective-permute-start.1 = (bf16[2,2,128,256]{3,2,1,0:T(8,128)(2,1)}, bf16[2,2,128,256]{3,2,1,0:T(8,128)(2,1)S(1)}, u32[]{:S(2)}, u32[]{:S(2)}) collective-permute-start(bf16[2,2,128,256]{3,2,1,0:T(8,128)(2,1)} %get-tuple-element.29), channel_id=1, source_target_pairs={{0,64},{16,80},{32,96},{48,112},{64,0},{80,16},{96,32},{112,48},{1... | collective-permute-start | bytes 786440 | tf_op jit(solution)/shard_map/ppermute | solution.py:324
  16.1 0.7 copy-done.21
  16.8 12.1 %first_frames.1 = bf16[1152,256]{1,0:T(8,128)(2,1)} custom-call(s32[3,16]{1,0:T(4,128)} %bitcast.10, bf16[256,2048]{1,0:T(8,128)(2,1)} %constant.4.clone.high_hbm, bf16[256,2048]{1,0:T(8,128)(2,1)} %constant.5.clone.low_hbm, bf16[256,24576]{1,0:T(8,128)(2,1)} %volts_hbm.3, f32[3,64,256]{2,1,0:T(8,128)} %get-tuple-element.27.last_ref, f32[3,64,256]{2,1,0:T(8,128)} %copy-done.21), custom_call_target="tpu_custom_call" | custom-call | flops 4831838208 | bytes 9437184 | tf_op jit(solution)/shard_map/first_frames/pallas_call | solution.py:355
  29.0 7.4 %all-to-all-start = ((bf16[16,3,24,256]{3,2,1,0:T(8,128)(2,1)}), bf16[16,3,24,256]{3,2,1,0:T(8,128)(2,1)S(1)}, u32[]{:S(2)}, u32[]{:S(2)}) async-start(bf16[16,3,24,256]{3,2,1,0:T(8,128)(2,1)} %bitcast.8), calls=%async_computation | async-start | bytes 1179648 | tf_op jit(solution)/shard_map/all_to_all | solution.py:375
  36.4 0.8 collective-permute-start.2
  37.2 2.6 %collective-permute-start.3 = (bf16[2,2,128,256]{3,2,1,0:T(8,128)(2,1)S(1)}, bf16[2,2,128,256]{3,2,1,0:T(8,128)(2,1)S(1)}, u32[]{:S(2)}, u32[]{:S(2)}) collective-permute-start(bf16[2,2,128,256]{3,2,1,0:T(8,128)(2,1)S(1)} %copy-done.19), channel_id=1, source_target_pairs={{0,96},{16,112},{32,0},{48,16},{64,32},{80,48},{96,64},{112,80},{1... | collective-permute-start | bytes 786440 | tf_op jit(solution)/shard_map/ppermute | solution.py:324
  40.4 0.7 collective-permute-done.4.refs_17_
  41.2 3.7 %collective-permute-done.2.refs_18_ = bf16[2,2,128,256]{3,2,1,0:T(8,128)(2,1)S(1)} collective-permute-done((bf16[2,2,128,256]{3,2,1,0:T(8,128)(2,1)S(1)}, bf16[2,2,128,256]{3,2,1,0:T(8,128)(2,1)S(1)}, u32[]{:S(2)}, u32[]{:S(2)}) %collective-permute-start.2) | collective-permute-done | bytes 262176 | tf_op jit(solution)/shard_map/ppermute | solution.py:324
  45.0 3.1 %all-to-all-done = bf16[16,3,24,256]{3,2,1,0:T(8,128)(2,1)S(1)} async-done(((bf16[16,3,24,256]{3,2,1,0:T(8,128)(2,1)}), bf16[16,3,24,256]{3,2,1,0:T(8,128)(2,1)S(1)}, u32[]{:S(2)}, u32[]{:S(2)}) %all-to-all-start) | async-done | bytes 589856 | tf_op jit(solution)/shard_map/all_to_all | solution.py:375
  48.2 1.5 %collective-permute-start.13 = (bf16[3,384,128]{2,1,0:T(8,128)(2,1)S(1)}, bf16[3,384,128]{2,1,0:T(8,128)(2,1)S(1)}, u32[]{:S(2)}, u32[]{:S(2)}) collective-permute-start(bf16[3,384,128]{2,1,0:T(8,128)(2,1)S(1)} %get-tuple-element.42.refs_1_), channel_id=1, source_target_pairs={{0,96},{16,112},{32,0},{48,16},{64,32},{80,48},{96,64},{112,80},{1... | collective-permute-start | bytes 884744 | tf_op jit(solution)/shard_map/ppermute | solution.py:324
  49.7 0.6 collective-permute-start.9
  50.3 0.7 collective-permute-start.8
  51.4 1.1 %collective-permute-done.21.refs_21_ = bf16[1,2,128,256]{3,2,1,0:T(8,128)(2,1)S(1)} collective-permute-done((bf16[1,2,128,256]{3,2,1,0:T(8,128)(2,1)S(1)}, bf16[1,2,128,256]{3,2,1,0:T(8,128)(2,1)S(1)}, u32[]{:S(2)}, u32[]{:S(2)}) %collective-permute-start.21) | collective-permute-done | bytes 131104 | tf_op jit(solution)/shard_map/ppermute | solution.py:327
  52.7 1.1 %collective-permute-done.20.refs_19_ = bf16[1,2,128,256]{3,2,1,0:T(8,128)(2,1)S(1)} collective-permute-done((bf16[1,2,128,256]{3,2,1,0:T(8,128)(2,1)S(1)}, bf16[1,2,128,256]{3,2,1,0:T(8,128)(2,1)S(1)}, u32[]{:S(2)}, u32[]{:S(2)}) %collective-permute-start.20) | collective-permute-done | bytes 131104 | tf_op jit(solution)/shard_map/ppermute | solution.py:327
  53.8 2.6 %collective-permute-start.12 = (bf16[3,384,128]{2,1,0:T(8,128)(2,1)S(1)}, bf16[3,384,128]{2,1,0:T(8,128)(2,1)S(1)}, u32[]{:S(2)}, u32[]{:S(2)}) collective-permute-start(bf16[3,384,128]{2,1,0:T(8,128)(2,1)S(1)} %get-tuple-element.43.refs_0_), channel_id=1, source_target_pairs={{0,96},{16,112},{32,0},{48,16},{64,32},{80,48},{96,64},{112,80},{1... | collective-permute-start | bytes 884744 | tf_op jit(solution)/shard_map/ppermute | solution.py:324
  56.4 4.3 %collective-permute-done.9.refs_5_ = bf16[3,384,128]{2,1,0:T(8,128)(2,1)S(1)} collective-permute-done((bf16[3,384,128]{2,1,0:T(8,128)(2,1)S(1)}, bf16[3,384,128]{2,1,0:T(8,128)(2,1)S(1)}, u32[]{:S(2)}, u32[]{:S(2)}) %collective-permute-start.9) | collective-permute-done | bytes 294944 | tf_op jit(solution)/shard_map/ppermute | solution.py:324
  60.8 3.2 %collective-permute-done.8.refs_4_ = bf16[3,384,128]{2,1,0:T(8,128)(2,1)S(1)} collective-permute-done((bf16[3,384,128]{2,1,0:T(8,128)(2,1)S(1)}, bf16[3,384,128]{2,1,0:T(8,128)(2,1)S(1)}, u32[]{:S(2)}, u32[]{:S(2)}) %collective-permute-start.8) | collective-permute-done | bytes 294944 | tf_op jit(solution)/shard_map/ppermute | solution.py:324
  64.6 4.8 %collective-permute-done.17.refs_13_ = bf16[3,384,128]{2,1,0:T(8,128)(2,1)S(1)} collective-permute-done((bf16[3,384,128]{2,1,0:T(8,128)(2,1)S(1)}, bf16[3,384,128]{2,1,0:T(8,128)(2,1)S(1)}, u32[]{:S(2)}, u32[]{:S(2)}) %collective-permute-start.17) | collective-permute-done | bytes 294944 | tf_op jit(solution)/shard_map/ppermute | solution.py:324
  70.0 2.0 %collective-permute-done.16.refs_12_ = bf16[3,384,128]{2,1,0:T(8,128)(2,1)S(1)} collective-permute-done((bf16[3,384,128]{2,1,0:T(8,128)(2,1)S(1)}, bf16[3,384,128]{2,1,0:T(8,128)(2,1)S(1)}, u32[]{:S(2)}, u32[]{:S(2)}) %collective-permute-start.16) | collective-permute-done | bytes 294944 | tf_op jit(solution)/shard_map/ppermute | solution.py:324
  72.9 0.7 copy-done.18
  73.7 9.3 %gathered.1 = (f32[3,2,256,2048]{3,2,1,0:T(8,128)}, f32[3,128]{1,0:T(4,128)}) custom-call(bf16[3,384,128]{2,1,0:T(8,128)(2,1)} %copy-done.1, bf16[3,384,128]{2,1,0:T(8,128)(2,1)} %copy-done, bf16[3,384,128]{2,1,0:T(8,128)(2,1)} %copy-done.11, bf16[3,384,128]{2,1,0:T(8,128)(2,1)} %copy-done.8, bf16[3,384,128]{2,1,0:T(8,128)(2,1)} %copy-done.9, ...), custom_call_target="tpu_custom_call" | custom-call | flops 3623878656 | bytes 14352384 | tf_op jit(solution)/shard_map/gathered/pallas_call | solution.py:280
  (84 shorter events, 3.6 us)
Async XLA Ops:
  5.5 10.6 %collective-permute-start = (f32[3,64,256]{2,1,0:T(8,128)}, f32[3,64,256]{2,1,0:T(8,128)S(1)}, u32[]{:S(2)}, u32[]{:S(2)}) collective-permute-start(f32[3,64,256]{2,1,0:T(8,128)} %get-tuple-element.28), channel_id=1, source_target_pairs={{0,1},{1,2},{2,3},{3,4},{4,5},{5,6},{6,7},{7,8},{8,9},{9,10},{10,1... | collective-permute-start | bytes 589832 | tf_op jit(solution)/shard_map/ppermute | solution.py:342
  12.9 16.1 %collective-permute-start.1 = (bf16[2,2,128,256]{3,2,1,0:T(8,128)(2,1)}, bf16[2,2,128,256]{3,2,1,0:T(8,128)(2,1)S(1)}, u32[]{:S(2)}, u32[]{:S(2)}) collective-permute-start(bf16[2,2,128,256]{3,2,1,0:T(8,128)(2,1)} %get-tuple-element.29), channel_id=1, source_target_pairs={{0,64},{16,80},{32,96},{48,112},{64,0},{80,16},{96,32},{112,48},{1... | collective-permute-start | bytes 786440 | tf_op jit(solution)/shard_map/ppermute | solution.py:324
  29.0 44.7 %copy-start.3 = (bf16[2,2,128,256]{3,2,1,0:T(8,128)(2,1)}, bf16[2,2,128,256]{3,2,1,0:T(8,128)(2,1)S(1)}, u32[]{:S(2)}) copy-start(bf16[2,2,128,256]{3,2,1,0:T(8,128)(2,1)S(1)} %collective-permute-done.1.refs_22_) | copy-start | bytes 786436
  29.0 19.1 %all-to-all-start = ((bf16[16,3,24,256]{3,2,1,0:T(8,128)(2,1)}), bf16[16,3,24,256]{3,2,1,0:T(8,128)(2,1)S(1)}, u32[]{:S(2)}, u32[]{:S(2)}) async-start(bf16[16,3,24,256]{3,2,1,0:T(8,128)(2,1)} %bitcast.8), calls=%async_computation | async-start | bytes 1179648 | tf_op jit(solution)/shard_map/all_to_all | solution.py:375
  36.4 8.5 %collective-permute-start.2 = (bf16[2,2,128,256]{3,2,1,0:T(8,128)(2,1)S(1)}, bf16[2,2,128,256]{3,2,1,0:T(8,128)(2,1)S(1)}, u32[]{:S(2)}, u32[]{:S(2)}) collective-permute-start(bf16[2,2,128,256]{3,2,1,0:T(8,128)(2,1)S(1)} %copy-done.20), channel_id=1, source_target_pairs={{0,32},{16,48},{32,64},{48,80},{64,96},{80,112},{96,0},{112,16},{1... | collective-permute-start | bytes 786440 | tf_op jit(solution)/shard_map/ppermute | solution.py:324
  37.2 7.7 %collective-permute-start.3 = (bf16[2,2,128,256]{3,2,1,0:T(8,128)(2,1)S(1)}, bf16[2,2,128,256]{3,2,1,0:T(8,128)(2,1)S(1)}, u32[]{:S(2)}, u32[]{:S(2)}) collective-permute-start(bf16[2,2,128,256]{3,2,1,0:T(8,128)(2,1)S(1)} %copy-done.19), channel_id=1, source_target_pairs={{0,96},{16,112},{32,0},{48,16},{64,32},{80,48},{96,64},{112,80},{1... | collective-permute-start | bytes 786440 | tf_op jit(solution)/shard_map/ppermute | solution.py:324
  39.8 1.4 %collective-permute-start.4 = (bf16[1,2,128,256]{3,2,1,0:T(8,128)(2,1)S(1)}, bf16[1,2,128,256]{3,2,1,0:T(8,128)(2,1)S(1)}, u32[]{:S(2)}, u32[]{:S(2)}) collective-permute-start(bf16[1,2,128,256]{3,2,1,0:T(8,128)(2,1)S(1)} %slice.18), channel_id=1, source_target_pairs={{0,16},{16,0},{32,48},{48,32},{64,80},{80,64},{96,112},{112,96},{1... | collective-permute-start | bytes 393224 | tf_op jit(solution)/shard_map/ppermute | solution.py:327
  39.9 5.1 %collective-permute-start.5 = (bf16[1,2,128,256]{3,2,1,0:T(8,128)(2,1)S(1)}, bf16[1,2,128,256]{3,2,1,0:T(8,128)(2,1)S(1)}, u32[]{:S(2)}, u32[]{:S(2)}) collective-permute-start(bf16[1,2,128,256]{3,2,1,0:T(8,128)(2,1)S(1)} %slice.19), channel_id=1, source_target_pairs={{0,16},{16,0},{32,48},{48,32},{64,80},{80,64},{96,112},{112,96},{1... | collective-permute-start | bytes 393224 | tf_op jit(solution)/shard_map/ppermute | solution.py:327
  48.2 8.1 %collective-permute-start.13 = (bf16[3,384,128]{2,1,0:T(8,128)(2,1)S(1)}, bf16[3,384,128]{2,1,0:T(8,128)(2,1)S(1)}, u32[]{:S(2)}, u32[]{:S(2)}) collective-permute-start(bf16[3,384,128]{2,1,0:T(8,128)(2,1)S(1)} %get-tuple-element.42.refs_1_), channel_id=1, source_target_pairs={{0,96},{16,112},{32,0},{48,16},{64,32},{80,48},{96,64},{112,80},{1... | collective-permute-start | bytes 884744 | tf_op jit(solution)/shard_map/ppermute | solution.py:324
  49.7 10.9 %collective-permute-start.9 = (bf16[3,384,128]{2,1,0:T(8,128)(2,1)S(1)}, bf16[3,384,128]{2,1,0:T(8,128)(2,1)S(1)}, u32[]{:S(2)}, u32[]{:S(2)}) collective-permute-start(bf16[3,384,128]{2,1,0:T(8,128)(2,1)S(1)} %get-tuple-element.42.refs_1_), channel_id=1, source_target_pairs={{0,32},{16,48},{32,64},{48,80},{64,96},{80,112},{96,0},{112,16},{1... | collective-permute-start | bytes 884744 | tf_op jit(solution)/shard_map/ppermute | solution.py:324
  50.3 10.3 %collective-permute-start.7 = (bf16[3,384,128]{2,1,0:T(8,128)(2,1)S(1)}, bf16[3,384,128]{2,1,0:T(8,128)(2,1)S(1)}, u32[]{:S(2)}, u32[]{:S(2)}) collective-permute-start(bf16[3,384,128]{2,1,0:T(8,128)(2,1)S(1)} %get-tuple-element.42.refs_1_), channel_id=1, source_target_pairs={{0,16},{16,0},{32,48},{48,32},{64,80},{80,64},{96,112},{112,96},{1... | collective-permute-start | bytes 884744 | tf_op jit(solution)/shard_map/ppermute | solution.py:327
  50.3 13.6 %collective-permute-start.8 = (bf16[3,384,128]{2,1,0:T(8,128)(2,1)S(1)}, bf16[3,384,128]{2,1,0:T(8,128)(2,1)S(1)}, u32[]{:S(2)}, u32[]{:S(2)}) collective-permute-start(bf16[3,384,128]{2,1,0:T(8,128)(2,1)S(1)} %get-tuple-element.43.refs_0_), channel_id=1, source_target_pairs={{0,32},{16,48},{32,64},{48,80},{64,96},{80,112},{96,0},{112,16},{1... | collective-permute-start | bytes 884744 | tf_op jit(solution)/shard_map/ppermute | solution.py:324
  51.0 1.4 %collective-permute-start.21 = (bf16[1,2,128,256]{3,2,1,0:T(8,128)(2,1)S(1)}, bf16[1,2,128,256]{3,2,1,0:T(8,128)(2,1)S(1)}, u32[]{:S(2)}, u32[]{:S(2)}) collective-permute-start(bf16[1,2,128,256]{3,2,1,0:T(8,128)(2,1)S(1)} %slice.23), channel_id=1, source_target_pairs={{0,16},{16,0},{32,48},{48,32},{64,80},{80,64},{96,112},{112,96},{1... | collective-permute-start | bytes 393224 | tf_op jit(solution)/shard_map/ppermute | solution.py:327
  52.5 1.3 %collective-permute-start.20 = (bf16[1,2,128,256]{3,2,1,0:T(8,128)(2,1)S(1)}, bf16[1,2,128,256]{3,2,1,0:T(8,128)(2,1)S(1)}, u32[]{:S(2)}, u32[]{:S(2)}) collective-permute-start(bf16[1,2,128,256]{3,2,1,0:T(8,128)(2,1)S(1)} %slice.22), channel_id=1, source_target_pairs={{0,16},{16,0},{32,48},{48,32},{64,80},{80,64},{96,112},{112,96},{1... | collective-permute-start | bytes 393224 | tf_op jit(solution)/shard_map/ppermute | solution.py:327
  53.8 10.2 %collective-permute-start.12 = (bf16[3,384,128]{2,1,0:T(8,128)(2,1)S(1)}, bf16[3,384,128]{2,1,0:T(8,128)(2,1)S(1)}, u32[]{:S(2)}, u32[]{:S(2)}) collective-permute-start(bf16[3,384,128]{2,1,0:T(8,128)(2,1)S(1)} %get-tuple-element.43.refs_0_), channel_id=1, source_target_pairs={{0,96},{16,112},{32,0},{48,16},{64,32},{80,48},{96,64},{112,80},{1... | collective-permute-start | bytes 884744 | tf_op jit(solution)/shard_map/ppermute | solution.py:324
  56.4 7.7 %collective-permute-start.6 = (bf16[3,384,128]{2,1,0:T(8,128)(2,1)S(1)}, bf16[3,384,128]{2,1,0:T(8,128)(2,1)S(1)}, u32[]{:S(2)}, u32[]{:S(2)}) collective-permute-start(bf16[3,384,128]{2,1,0:T(8,128)(2,1)S(1)} %get-tuple-element.43.refs_0_), channel_id=1, source_target_pairs={{0,16},{16,0},{32,48},{48,32},{64,80},{80,64},{96,112},{112,96},{1... | collective-permute-start | bytes 884744 | tf_op jit(solution)/shard_map/ppermute | solution.py:327
  60.7 8.7 %collective-permute-start.17 = (bf16[3,384,128]{2,1,0:T(8,128)(2,1)S(1)}, bf16[3,384,128]{2,1,0:T(8,128)(2,1)S(1)}, u32[]{:S(2)}, u32[]{:S(2)}) collective-permute-start(bf16[3,384,128]{2,1,0:T(8,128)(2,1)S(1)} %collective-permute-done.13.refs_9_), channel_id=1, source_target_pairs={{0,96},{16,112},{32,0},{48,16},{64,32},{80,48},{96,64},{112,80},{1... | collective-permute-start | bytes 884744 | tf_op jit(solution)/shard_map/ppermute | solution.py:324
  60.7 8.7 %collective-permute-start.15 = (bf16[3,384,128]{2,1,0:T(8,128)(2,1)S(1)}, bf16[3,384,128]{2,1,0:T(8,128)(2,1)S(1)}, u32[]{:S(2)}, u32[]{:S(2)}) collective-permute-start(bf16[3,384,128]{2,1,0:T(8,128)(2,1)S(1)} %collective-permute-done.13.refs_9_), channel_id=1, source_target_pairs={{0,16},{16,0},{32,48},{48,32},{64,80},{80,64},{96,112},{112,96},{1... | collective-permute-start | bytes 884744 | tf_op jit(solution)/shard_map/ppermute | solution.py:327
  64.0 7.9 %collective-permute-start.16 = (bf16[3,384,128]{2,1,0:T(8,128)(2,1)S(1)}, bf16[3,384,128]{2,1,0:T(8,128)(2,1)S(1)}, u32[]{:S(2)}, u32[]{:S(2)}) collective-permute-start(bf16[3,384,128]{2,1,0:T(8,128)(2,1)S(1)} %collective-permute-done.8.refs_4_), channel_id=1, source_target_pairs={{0,32},{16,48},{32,64},{48,80},{64,96},{80,112},{96,0},{112,16},{1... | collective-permute-start | bytes 884744 | tf_op jit(solution)/shard_map/ppermute | solution.py:324
  64.0 8.0 %collective-permute-start.10 = (bf16[3,384,128]{2,1,0:T(8,128)(2,1)S(1)}, bf16[3,384,128]{2,1,0:T(8,128)(2,1)S(1)}, u32[]{:S(2)}, u32[]{:S(2)}) collective-permute-start(bf16[3,384,128]{2,1,0:T(8,128)(2,1)S(1)} %collective-permute-done.8.refs_4_), channel_id=1, source_target_pairs={{0,16},{16,0},{32,48},{48,32},{64,80},{80,64},{96,112},{112,96},{1... | collective-permute-start | bytes 884744 | tf_op jit(solution)/shard_map/ppermute | solution.py:327
  64.1 7.8 %collective-permute-start.11 = (bf16[3,384,128]{2,1,0:T(8,128)(2,1)S(1)}, bf16[3,384,128]{2,1,0:T(8,128)(2,1)S(1)}, u32[]{:S(2)}, u32[]{:S(2)}) collective-permute-start(bf16[3,384,128]{2,1,0:T(8,128)(2,1)S(1)} %collective-permute-done.9.refs_5_), channel_id=1, source_target_pairs={{0,16},{16,0},{32,48},{48,32},{64,80},{80,64},{96,112},{112,96},{1... | collective-permute-start | bytes 884744 | tf_op jit(solution)/shard_map/ppermute | solution.py:327
  69.4 2.6 %collective-permute-start.14 = (bf16[3,384,128]{2,1,0:T(8,128)(2,1)S(1)}, bf16[3,384,128]{2,1,0:T(8,128)(2,1)S(1)}, u32[]{:S(2)}, u32[]{:S(2)}) collective-permute-start(bf16[3,384,128]{2,1,0:T(8,128)(2,1)S(1)} %collective-permute-done.12.refs_8_), channel_id=1, source_target_pairs={{0,16},{16,0},{32,48},{48,32},{64,80},{80,64},{96,112},{112,96},{1... | collective-permute-start | bytes 884744 | tf_op jit(solution)/shard_map/ppermute | solution.py:327
  69.4 2.6 %collective-permute-start.19 = (bf16[3,384,128]{2,1,0:T(8,128)(2,1)S(1)}, bf16[3,384,128]{2,1,0:T(8,128)(2,1)S(1)}, u32[]{:S(2)}, u32[]{:S(2)}) collective-permute-start(bf16[3,384,128]{2,1,0:T(8,128)(2,1)S(1)} %collective-permute-done.17.refs_13_), channel_id=1, source_target_pairs={{0,16},{16,0},{32,48},{48,32},{64,80},{80,64},{96,112},{112,96},{1... | collective-permute-start | bytes 884744 | tf_op jit(solution)/shard_map/ppermute | solution.py:327
  71.9 1.7 %collective-permute-start.18 = (bf16[3,384,128]{2,1,0:T(8,128)(2,1)S(1)}, bf16[3,384,128]{2,1,0:T(8,128)(2,1)}, u32[]{:S(2)}, u32[]{:S(2)}) collective-permute-start(bf16[3,384,128]{2,1,0:T(8,128)(2,1)S(1)} %collective-permute-done.16.refs_12_), channel_id=1, source_target_pairs={{0,16},{16,0},{32,48},{48,32},{64,80},{80,64},{96,112},{112,96},{1... | collective-permute-start | bytes 884744 | tf_op jit(solution)/shard_map/ppermute | solution.py:327
  (25 other events, 353.3 us)

commit v4 on v3

--- a/solution.py
+++ b/solution.py
@@ -188,33 +188,14 @@
     pairs = len(behind)
     block_refs = refs[: 4 * pairs]
     weight_refs = refs[4 * pairs : 6 * pairs]
-    vis_hbm, power_ref, values, weights, left, voltages, out, sems, weight_sems, out_sems = refs[
+    vis_hbm, power_ref, left, voltages, out, out_sems = refs[
         6 * pairs :
     ]
-    slots, rows, narrow = values.shape[2:]
+    slots, rows, narrow = block_refs[0].shape
     width = 2 * narrow
     chips = vis_hbm.shape[3] // (2 * width)
     me = lax.axis_index("feed")
     chip, core = me // 2, me % 2
-
-    copies = []
-    for pair in range(pairs):
-        copies.append(
-            [
-                pltpu.make_async_copy(
-                    block_refs[4 * pair + i], values.at[pair, i], sems.at[pair, i]
-                )
-                for i in range(4)
-            ]
-            + [
-                pltpu.make_async_copy(
-                    weight_refs[2 * pair + i].at[0], weights.at[pair, i], weight_sems.at[pair, i]
-                )
-                for i in range(2)
-            ]
-        )
-        for copy in copies[pair]:
-            copy.start()
 
     def out_copy(pair, slot):
         to = lax.rem(chip + chips - behind[pair], chips)
@@ -226,11 +207,11 @@
         )
 
     for pair in range(pairs):
-        for copy in copies[pair]:
-            copy.wait()
         for slot in range(slots):
             feeds = [
-                jnp.concatenate([values[pair, 2 * i, slot], values[pair, 2 * i + 1, slot]], axis=1)
+                jnp.concatenate(
+                    [block_refs[4 * pair + 2 * i + j][slot] for j in range(2)], axis=1
+                )
                 for i in range(2)
             ]
             if pair == 0:
@@ -246,7 +227,7 @@
                 columns = pl.ds(pl.multiple_of(at * width, width), width)
                 out[pair, slot, 0, :, columns] = product[:width]
                 out[pair, slot, 1, :, columns] = product[width:]
-                weight = weights[pair, side]
+                weight = weight_refs[2 * pair + side][0]
                 weight = weight.reshape(weight.shape[0] * weight.shape[1], width)
                 term = lax.dot_general(
                     feeds[side], weight, NT, preferred_element_type=jnp.float32
@@ -265,7 +246,7 @@
 
 
 def params():
-    return pltpu.CompilerParams(vmem_limit_bytes=WIDE_VMEM)
+    return pltpu.CompilerParams(vmem_limit_bytes=16 * 1024 * 1024)
 
 
 def gather_call(behind, half, scale, devices, blocks, weights):
@@ -283,19 +264,15 @@
             jax.ShapeDtypeStruct((slots, 2, width, devices * width), jnp.float32),
             jax.ShapeDtypeStruct((slots, share), jnp.float32),
         ],
-        in_specs=[anywhere] * len(args),
+        in_specs=[pl.BlockSpec(memory_space=pltpu.VMEM)] * len(args),
         out_specs=[anywhere, pl.BlockSpec(memory_space=pltpu.VMEM)],
         scratch_shapes=[
-            pltpu.VMEM((pairs, 4, slots, rows, narrow), jnp.bfloat16),
-            pltpu.VMEM((pairs, 2, parts, share, width), jnp.bfloat16),
             pltpu.VMEM((slots, 2 * width, rows), jnp.bfloat16),
             pltpu.VMEM((slots, rows, parts * share), jnp.float32),
             pltpu.VMEM((pairs, slots, 2, width, 2 * width), jnp.float32),
-            pltpu.SemaphoreType.DMA((pairs, 4)),
-            pltpu.SemaphoreType.DMA((pairs, 2)),
             pltpu.SemaphoreType.DMA((pairs, slots)),
         ],
-        compiler_params=params(),
+        compiler_params=pltpu.CompilerParams(vmem_limit_bytes=36 * 1024 * 1024),
         cost_estimate=pl.CostEstimate(flops=flops, bytes_accessed=moved, transcendentals=0),
         name="gathered",
     )(*args)
@@ -393,6 +370,9 @@
     up.append(moved(own[1], 2))
     down[0] = moved(own[0], -2)
     far = [moved(up[0], 2), moved(down[1], -2)]
+    up[1], down[0], weights[1], weights[2] = lax.optimization_barrier(
+        (up[1], down[0], weights[1], weights[2])
+    )
     sibling = [swapped(x) for x in own]
     up_other = [swapped(x) for x in up]
     down_other = [swapped(x) for x in down]

time: 84.8 us -> 79.8 us (0.941)
  Pallas kernels: 29.7 us -> 25.8 us
  local copies, waits for them, and re-layouts: 2.51 us -> 0.19 us
  starting transfers between devices: 25.7 us -> 27.5 us
    pallas_call x1, Pallas kernels: 9.3 us -> 6.69 us  [gather_call(): pl.pallas_call(functools.partial(gather_kernel, behind, half, scale), out...]
    unnamed x52 -> x4, local copies, waits for them, and re-layouts: 2.33 us -> 0.01 us
    pallas_call x1, Pallas kernels: 3.37 us -> 1.92 us  [shards(): pl.pallas_call(order_kernel, out_shape=[jax.ShapeDtypeStruct((2, 2, share...]
    ppermute x9, starting transfers between devices: 11.9 us -> 13.2 us  [moved(): lax.ppermute(x, 'feed', [(i, (i + by) % devices) for i in range(devices)])]
  transfers between devices with their start and end apart: 23 -> 23, of which waited for: 9 -> 11; matrix products, arithmetic and copies ran while one was open for 0% -> 0% of each run, Pallas kernels for 19% -> 18%
where the time goes in v4:
time: 79.8 us; the launch traced here: 78.5 us
  starting transfers between devices  27.5 us (34%)
  Pallas kernels  25.8 us (32%)
  waiting for transfers between devices  24.1 us (30%)
  between operations  0.95 us (1%)
    ppermute x9, waiting for transfers between devices, moved(): lax.ppermute(x, 'feed', [(i, (i + by) % devices) for i in range(devices)])  18 us
    ppermute x9, starting transfers between devices, moved(): lax.ppermute(x, 'feed', [(i, (i + by) % devices) for i in range(devices)])  13.2 us
    pallas_call x1, Pallas kernels, shards(): pl.pallas_call(first_frames_kernel, out_shape=jax.ShapeDtypeStruct((chose...  12.1 us
    all_to_all x1, starting transfers between devices, shards(): lax.all_to_all(outgoing.reshape(owners, slots_dev, 2 * frames_dev, feeds_...  7.12 us
    pallas_call x1, Pallas kernels, gather_call(): pl.pallas_call(functools.partial(gather_kernel, behind, half, scale), out...  6.69 us
    pallas_call x1, Pallas kernels, shards(): pl.pallas_call(functools.partial(last_frames_kernel, early), out_shape=[j...  5.03 us
    ppermute x1, starting transfers between devices, shards(): lax.ppermute(next_first, 'freq', [(i, i + 1) for i in range(owners - 1)])  4.6 us
    ppermute x12, waiting for transfers between devices, swapped(): return lax.ppermute(x, 'feed', [(i, i ^ 1) for i in range(devices)])  3.15 us
  transfers between devices with their start and end apart: 23, of which 11 were waited for; matrix products, arithmetic and copies ran while one was open for 0% of the time, Pallas kernels for 18%

profile of v4, /device:TPU:0, one launch (start us, length us, event | category | flops | bytes accessed | tf_op | source)
XLA Modules:
  0.0 78.5 jit_solution(4534005929984783203)
XLA Ops:
  0.6 5.0 %last_frames.1 = (f32[3,64,256]{2,1,0:T(8,128)}, f32[3,64,256]{2,1,0:T(8,128)}) custom-call(bf16[256,2048]{1,0:T(8,128)(2,1)} %constant.4.clone.high_hbm, bf16[256,2048]{1,0:T(8,128)(2,1)} %constant.5.clone.low_hbm, bf16[256,24576]{1,0:T(8,128)(2,1)} %volts_hbm.3), custom_call_target="tpu_custom_call" | custom-call | flops 1610612736 | bytes 3145728 | tf_op jit(solution)/shard_map/last_frames/pallas_call | solution.py:306
  5.7 4.6 %collective-permute-start = (f32[3,64,256]{2,1,0:T(8,128)}, f32[3,64,256]{2,1,0:T(8,128)}, u32[]{:S(2)}, u32[]{:S(2)}) collective-permute-start(f32[3,64,256]{2,1,0:T(8,128)} %get-tuple-element.32), channel_id=1, source_target_pairs={{0,1},{1,2},{2,3},{3,4},{4,5},{5,6},{6,7},{7,8},{8,9},{9,10},{10,1... | collective-permute-start | bytes 589832 | tf_op jit(solution)/shard_map/ppermute | solution.py:319
  10.3 1.9 %order_beams.1 = (bf16[2,2,128,256]{3,2,1,0:T(8,128)(2,1)S(1)}, bf16[2,2,128,256]{3,2,1,0:T(8,128)(2,1)S(1)}, bf16[2,2,128,256]{3,2,1,0:T(8,128)(2,1)}, bf16[2,2,128,256]{3,2,1,0:T(8,128)(2,1)S(1)}) custom-call(s32[8,128]{1,0:T(8,128)S(1)} %bitcast.6, bf16[2,1024,256]{2,1,0:T(8,128)(2,1)S(1)} %copy-done), custom_call_target="tpu_custom_call" | custom-call | flops 1073741824 | bytes 1048576 | tf_op jit(solution)/shard_map/order_beams/pallas_call | solution.py:320
  12.2 3.2 %collective-permute-start.1 = (bf16[2,2,128,256]{3,2,1,0:T(8,128)(2,1)}, bf16[2,2,128,256]{3,2,1,0:T(8,128)(2,1)S(1)}, u32[]{:S(2)}, u32[]{:S(2)}) collective-permute-start(bf16[2,2,128,256]{3,2,1,0:T(8,128)(2,1)} %get-tuple-element.33), channel_id=1, source_target_pairs={{0,64},{16,80},{32,96},{48,112},{64,0},{80,16},{96,32},{112,48},{1... | collective-permute-start | bytes 786440 | tf_op jit(solution)/shard_map/ppermute | solution.py:301
  15.4 12.1 %first_frames.1 = bf16[1152,256]{1,0:T(8,128)(2,1)} custom-call(s32[3,16]{1,0:T(4,128)} %bitcast.10, bf16[256,2048]{1,0:T(8,128)(2,1)} %constant.4.clone.high_hbm, bf16[256,2048]{1,0:T(8,128)(2,1)} %constant.5.clone.low_hbm, bf16[256,24576]{1,0:T(8,128)(2,1)} %volts_hbm.3, f32[3,64,256]{2,1,0:T(8,128)} %get-tuple-element.31.last_ref, ...), custom_call_target="tpu_custom_call" | custom-call | flops 4831838208 | bytes 9437184 | tf_op jit(solution)/shard_map/first_frames/pallas_call | solution.py:332
  27.6 7.1 %all-to-all-start = ((bf16[16,3,24,256]{3,2,1,0:T(8,128)(2,1)}), bf16[16,3,24,256]{3,2,1,0:T(8,128)(2,1)S(1)}, u32[]{:S(2)}, u32[]{:S(2)}) async-start(bf16[16,3,24,256]{3,2,1,0:T(8,128)(2,1)} %bitcast.9), calls=%async_computation | async-start | bytes 1179648 | tf_op jit(solution)/shard_map/all_to_all | solution.py:352
  34.7 1.8 %collective-permute-start.2 = (bf16[2,2,128,256]{3,2,1,0:T(8,128)(2,1)S(1)}, bf16[2,2,128,256]{3,2,1,0:T(8,128)(2,1)S(1)}, u32[]{:S(2)}, u32[]{:S(2)}) collective-permute-start(bf16[2,2,128,256]{3,2,1,0:T(8,128)(2,1)S(1)} %get-tuple-element.35), channel_id=1, source_target_pairs={{0,32},{16,48},{32,64},{48,80},{64,96},{80,112},{96,0},{112,16},{1... | collective-permute-start | bytes 786440 | tf_op jit(solution)/shard_map/ppermute | solution.py:301
  36.5 1.5 %collective-permute-start.3 = (bf16[2,2,128,256]{3,2,1,0:T(8,128)(2,1)S(1)}, bf16[2,2,128,256]{3,2,1,0:T(8,128)(2,1)S(1)}, u32[]{:S(2)}, u32[]{:S(2)}) collective-permute-start(bf16[2,2,128,256]{3,2,1,0:T(8,128)(2,1)S(1)} %get-tuple-element.36), channel_id=1, source_target_pairs={{0,96},{16,112},{32,0},{48,16},{64,32},{80,48},{96,64},{112,80},{1... | collective-permute-start | bytes 786440 | tf_op jit(solution)/shard_map/ppermute | solution.py:301
  38.1 0.6 collective-permute-start.5
  38.7 0.7 collective-permute-done.4.refs_17_
  39.4 3.6 %collective-permute-done.2.refs_18_ = bf16[2,2,128,256]{3,2,1,0:T(8,128)(2,1)S(1)} collective-permute-done((bf16[2,2,128,256]{3,2,1,0:T(8,128)(2,1)S(1)}, bf16[2,2,128,256]{3,2,1,0:T(8,128)(2,1)S(1)}, u32[]{:S(2)}, u32[]{:S(2)}) %collective-permute-start.2) | collective-permute-done | bytes 262176 | tf_op jit(solution)/shard_map/ppermute | solution.py:301
  43.0 3.0 %all-to-all-done = bf16[16,3,24,256]{3,2,1,0:T(8,128)(2,1)S(1)} async-done(((bf16[16,3,24,256]{3,2,1,0:T(8,128)(2,1)}), bf16[16,3,24,256]{3,2,1,0:T(8,128)(2,1)S(1)}, u32[]{:S(2)}, u32[]{:S(2)}) %all-to-all-start) | async-done | bytes 589856 | tf_op jit(solution)/shard_map/all_to_all | solution.py:352
  46.2 3.1 %collective-permute-start.13 = (bf16[3,384,128]{2,1,0:T(8,128)(2,1)S(1)}, bf16[3,384,128]{2,1,0:T(8,128)(2,1)S(1)}, u32[]{:S(2)}, u32[]{:S(2)}) collective-permute-start(bf16[3,384,128]{2,1,0:T(8,128)(2,1)S(1)} %get-tuple-element.50.refs_1_), channel_id=1, source_target_pairs={{0,96},{16,112},{32,0},{48,16},{64,32},{80,48},{96,64},{112,80},{1... | collective-permute-start | bytes 884744 | tf_op jit(solution)/shard_map/ppermute | solution.py:301
  49.4 3.2 %collective-permute-start.10 = (bf16[3,384,128]{2,1,0:T(8,128)(2,1)S(1)}, bf16[3,384,128]{2,1,0:T(8,128)(2,1)S(1)}, u32[]{:S(2)}, u32[]{:S(2)}) collective-permute-start(bf16[3,384,128]{2,1,0:T(8,128)(2,1)S(1)} %get-tuple-element.51.refs_0_), channel_id=1, source_target_pairs={{0,96},{16,112},{32,0},{48,16},{64,32},{80,48},{96,64},{112,80},{1... | collective-permute-start | bytes 884744 | tf_op jit(solution)/shard_map/ppermute | solution.py:301
  52.6 3.0 %collective-permute-done.13.refs_9_ = bf16[3,384,128]{2,1,0:T(8,128)(2,1)S(1)} collective-permute-done((bf16[3,384,128]{2,1,0:T(8,128)(2,1)S(1)}, bf16[3,384,128]{2,1,0:T(8,128)(2,1)S(1)}, u32[]{:S(2)}, u32[]{:S(2)}) %collective-permute-start.13) | collective-permute-done | bytes 294944 | tf_op jit(solution)/shard_map/ppermute | solution.py:301
  55.6 3.4 %collective-permute-done.9.refs_5_ = bf16[3,384,128]{2,1,0:T(8,128)(2,1)S(1)} collective-permute-done((bf16[3,384,128]{2,1,0:T(8,128)(2,1)S(1)}, bf16[3,384,128]{2,1,0:T(8,128)(2,1)S(1)}, u32[]{:S(2)}, u32[]{:S(2)}) %collective-permute-start.9) | collective-permute-done | bytes 294944 | tf_op jit(solution)/shard_map/ppermute | solution.py:301
  59.5 2.6 %collective-permute-done.8.refs_4_ = bf16[3,384,128]{2,1,0:T(8,128)(2,1)S(1)} collective-permute-done((bf16[3,384,128]{2,1,0:T(8,128)(2,1)S(1)}, bf16[3,384,128]{2,1,0:T(8,128)(2,1)S(1)}, u32[]{:S(2)}, u32[]{:S(2)}) %collective-permute-start.8) | collective-permute-done | bytes 294944 | tf_op jit(solution)/shard_map/ppermute | solution.py:301
  62.3 0.6 collective-permute-start.20
  62.8 0.7 collective-permute-done.21.refs_21_
  64.2 2.0 %collective-permute-done.17.refs_13_ = bf16[3,384,128]{2,1,0:T(8,128)(2,1)S(1)} collective-permute-done((bf16[3,384,128]{2,1,0:T(8,128)(2,1)S(1)}, bf16[3,384,128]{2,1,0:T(8,128)(2,1)S(1)}, u32[]{:S(2)}, u32[]{:S(2)}) %collective-permute-start.17) | collective-permute-done | bytes 294944 | tf_op jit(solution)/shard_map/ppermute | solution.py:301
  66.2 0.5 collective-permute-start.19
  66.7 3.4 %collective-permute-done.16.refs_12_ = bf16[3,384,128]{2,1,0:T(8,128)(2,1)S(1)} collective-permute-done((bf16[3,384,128]{2,1,0:T(8,128)(2,1)S(1)}, bf16[3,384,128]{2,1,0:T(8,128)(2,1)S(1)}, u32[]{:S(2)}, u32[]{:S(2)}) %collective-permute-start.16) | collective-permute-done | bytes 294944 | tf_op jit(solution)/shard_map/ppermute | solution.py:301
  70.1 1.5 %collective-permute-done.18.refs_14_ = bf16[3,384,128]{2,1,0:T(8,128)(2,1)S(1)} collective-permute-done((bf16[3,384,128]{2,1,0:T(8,128)(2,1)S(1)}, bf16[3,384,128]{2,1,0:T(8,128)(2,1)S(1)}, u32[]{:S(2)}, u32[]{:S(2)}) %collective-permute-start.18) | collective-permute-done | bytes 294944 | tf_op jit(solution)/shard_map/ppermute | solution.py:304
  71.7 6.7 %gathered.1 = (f32[3,2,256,2048]{3,2,1,0:T(8,128)}, f32[3,128]{1,0:T(4,128)}) custom-call(bf16[3,384,128]{2,1,0:T(8,128)(2,1)S(1)} %get-tuple-element.51.refs_0_, bf16[3,384,128]{2,1,0:T(8,128)(2,1)S(1)} %get-tuple-element.50.refs_1_, bf16[3,384,128]{2,1,0:T(8,128)(2,1)S(1)} %collective-permute-done.6.refs_2_, ...), custom_call_target="tpu_custom_call" | custom-call | flops 3623878656 | bytes 14352384 | tf_op jit(solution)/shard_map/gathered/pallas_call | solution.py:261
  (36 shorter events, 1.5 us)
Async XLA Ops:
  0.6 9.7 %copy-start.1 = (s32[1024]{0:T(1024)S(1)}, s32[1024]{0:T(1024)}, u32[]{:S(2)}) copy-start(s32[1024]{0:T(1024)} %param.9) | copy-start | bytes 12292
  5.7 9.7 %collective-permute-start = (f32[3,64,256]{2,1,0:T(8,128)}, f32[3,64,256]{2,1,0:T(8,128)}, u32[]{:S(2)}, u32[]{:S(2)}) collective-permute-start(f32[3,64,256]{2,1,0:T(8,128)} %get-tuple-element.32), channel_id=1, source_target_pairs={{0,1},{1,2},{2,3},{3,4},{4,5},{5,6},{6,7},{7,8},{8,9},{9,10},{10,1... | collective-permute-start | bytes 589832 | tf_op jit(solution)/shard_map/ppermute | solution.py:319
  12.2 15.4 %collective-permute-start.1 = (bf16[2,2,128,256]{3,2,1,0:T(8,128)(2,1)}, bf16[2,2,128,256]{3,2,1,0:T(8,128)(2,1)S(1)}, u32[]{:S(2)}, u32[]{:S(2)}) collective-permute-start(bf16[2,2,128,256]{3,2,1,0:T(8,128)(2,1)} %get-tuple-element.33), channel_id=1, source_target_pairs={{0,64},{16,80},{32,96},{48,112},{64,0},{80,16},{96,32},{112,48},{1... | collective-permute-start | bytes 786440 | tf_op jit(solution)/shard_map/ppermute | solution.py:301
  27.6 18.5 %all-to-all-start = ((bf16[16,3,24,256]{3,2,1,0:T(8,128)(2,1)}), bf16[16,3,24,256]{3,2,1,0:T(8,128)(2,1)S(1)}, u32[]{:S(2)}, u32[]{:S(2)}) async-start(bf16[16,3,24,256]{3,2,1,0:T(8,128)(2,1)} %bitcast.9), calls=%async_computation | async-start | bytes 1179648 | tf_op jit(solution)/shard_map/all_to_all | solution.py:352
  34.7 8.3 %collective-permute-start.2 = (bf16[2,2,128,256]{3,2,1,0:T(8,128)(2,1)S(1)}, bf16[2,2,128,256]{3,2,1,0:T(8,128)(2,1)S(1)}, u32[]{:S(2)}, u32[]{:S(2)}) collective-permute-start(bf16[2,2,128,256]{3,2,1,0:T(8,128)(2,1)S(1)} %get-tuple-element.35), channel_id=1, source_target_pairs={{0,32},{16,48},{32,64},{48,80},{64,96},{80,112},{96,0},{112,16},{1... | collective-permute-start | bytes 786440 | tf_op jit(solution)/shard_map/ppermute | solution.py:301
  36.5 6.6 %collective-permute-start.3 = (bf16[2,2,128,256]{3,2,1,0:T(8,128)(2,1)S(1)}, bf16[2,2,128,256]{3,2,1,0:T(8,128)(2,1)S(1)}, u32[]{:S(2)}, u32[]{:S(2)}) collective-permute-start(bf16[2,2,128,256]{3,2,1,0:T(8,128)(2,1)S(1)} %get-tuple-element.36), channel_id=1, source_target_pairs={{0,96},{16,112},{32,0},{48,16},{64,32},{80,48},{96,64},{112,80},{1... | collective-permute-start | bytes 786440 | tf_op jit(solution)/shard_map/ppermute | solution.py:301
  38.0 1.4 %collective-permute-start.4 = (bf16[1,2,128,256]{3,2,1,0:T(8,128)(2,1)S(1)}, bf16[1,2,128,256]{3,2,1,0:T(8,128)(2,1)S(1)}, u32[]{:S(2)}, u32[]{:S(2)}) collective-permute-start(bf16[1,2,128,256]{3,2,1,0:T(8,128)(2,1)S(1)} %slice.18), channel_id=1, source_target_pairs={{0,16},{16,0},{32,48},{48,32},{64,80},{80,64},{96,112},{112,96},{1... | collective-permute-start | bytes 393224 | tf_op jit(solution)/shard_map/ppermute | solution.py:304
  38.1 4.9 %collective-permute-start.5 = (bf16[1,2,128,256]{3,2,1,0:T(8,128)(2,1)S(1)}, bf16[1,2,128,256]{3,2,1,0:T(8,128)(2,1)S(1)}, u32[]{:S(2)}, u32[]{:S(2)}) collective-permute-start(bf16[1,2,128,256]{3,2,1,0:T(8,128)(2,1)S(1)} %slice.19), channel_id=1, source_target_pairs={{0,16},{16,0},{32,48},{48,32},{64,80},{80,64},{96,112},{112,96},{1... | collective-permute-start | bytes 393224 | tf_op jit(solution)/shard_map/ppermute | solution.py:304
  46.2 9.3 %collective-permute-start.13 = (bf16[3,384,128]{2,1,0:T(8,128)(2,1)S(1)}, bf16[3,384,128]{2,1,0:T(8,128)(2,1)S(1)}, u32[]{:S(2)}, u32[]{:S(2)}) collective-permute-start(bf16[3,384,128]{2,1,0:T(8,128)(2,1)S(1)} %get-tuple-element.50.refs_1_), channel_id=1, source_target_pairs={{0,96},{16,112},{32,0},{48,16},{64,32},{80,48},{96,64},{112,80},{1... | collective-permute-start | bytes 884744 | tf_op jit(solution)/shard_map/ppermute | solution.py:301
  49.4 9.6 %collective-permute-start.9 = (bf16[3,384,128]{2,1,0:T(8,128)(2,1)S(1)}, bf16[3,384,128]{2,1,0:T(8,128)(2,1)S(1)}, u32[]{:S(2)}, u32[]{:S(2)}) collective-permute-start(bf16[3,384,128]{2,1,0:T(8,128)(2,1)S(1)} %get-tuple-element.50.refs_1_), channel_id=1, source_target_pairs={{0,32},{16,48},{32,64},{48,80},{64,96},{80,112},{96,0},{112,16},{1... | collective-permute-start | bytes 884744 | tf_op jit(solution)/shard_map/ppermute | solution.py:301
  49.4 9.9 %collective-permute-start.10 = (bf16[3,384,128]{2,1,0:T(8,128)(2,1)S(1)}, bf16[3,384,128]{2,1,0:T(8,128)(2,1)S(1)}, u32[]{:S(2)}, u32[]{:S(2)}) collective-permute-start(bf16[3,384,128]{2,1,0:T(8,128)(2,1)S(1)} %get-tuple-element.51.refs_0_), channel_id=1, source_target_pairs={{0,96},{16,112},{32,0},{48,16},{64,32},{80,48},{96,64},{112,80},{1... | collective-permute-start | bytes 884744 | tf_op jit(solution)/shard_map/ppermute | solution.py:301
  52.6 9.5 %collective-permute-start.8 = (bf16[3,384,128]{2,1,0:T(8,128)(2,1)S(1)}, bf16[3,384,128]{2,1,0:T(8,128)(2,1)S(1)}, u32[]{:S(2)}, u32[]{:S(2)}) collective-permute-start(bf16[3,384,128]{2,1,0:T(8,128)(2,1)S(1)} %get-tuple-element.51.refs_0_), channel_id=1, source_target_pairs={{0,32},{16,48},{32,64},{48,80},{64,96},{80,112},{96,0},{112,16},{1... | collective-permute-start | bytes 884744 | tf_op jit(solution)/shard_map/ppermute | solution.py:301
  52.6 9.5 %collective-permute-start.7 = (bf16[3,384,128]{2,1,0:T(8,128)(2,1)S(1)}, bf16[3,384,128]{2,1,0:T(8,128)(2,1)S(1)}, u32[]{:S(2)}, u32[]{:S(2)}) collective-permute-start(bf16[3,384,128]{2,1,0:T(8,128)(2,1)S(1)} %get-tuple-element.50.refs_1_), channel_id=1, source_target_pairs={{0,16},{16,0},{32,48},{48,32},{64,80},{80,64},{96,112},{112,96},{1... | collective-permute-start | bytes 884744 | tf_op jit(solution)/shard_map/ppermute | solution.py:304
  55.5 6.7 %collective-permute-start.6 = (bf16[3,384,128]{2,1,0:T(8,128)(2,1)S(1)}, bf16[3,384,128]{2,1,0:T(8,128)(2,1)S(1)}, u32[]{:S(2)}, u32[]{:S(2)}) collective-permute-start(bf16[3,384,128]{2,1,0:T(8,128)(2,1)S(1)} %get-tuple-element.51.refs_0_), channel_id=1, source_target_pairs={{0,16},{16,0},{32,48},{48,32},{64,80},{80,64},{96,112},{112,96},{1... | collective-permute-start | bytes 884744 | tf_op jit(solution)/shard_map/ppermute | solution.py:304
  59.0 7.2 %collective-permute-start.17 = (bf16[3,384,128]{2,1,0:T(8,128)(2,1)S(1)}, bf16[3,384,128]{2,1,0:T(8,128)(2,1)S(1)}, u32[]{:S(2)}, u32[]{:S(2)}) collective-permute-start(bf16[3,384,128]{2,1,0:T(8,128)(2,1)S(1)} %collective-permute-done.13.refs_9_), channel_id=1, source_target_pairs={{0,96},{16,112},{32,0},{48,16},{64,32},{80,48},{96,64},{112,80},{1... | collective-permute-start | bytes 884744 | tf_op jit(solution)/shard_map/ppermute | solution.py:301
  59.3 6.9 %collective-permute-start.15 = (bf16[3,384,128]{2,1,0:T(8,128)(2,1)S(1)}, bf16[3,384,128]{2,1,0:T(8,128)(2,1)S(1)}, u32[]{:S(2)}, u32[]{:S(2)}) collective-permute-start(bf16[3,384,128]{2,1,0:T(8,128)(2,1)S(1)} %collective-permute-done.13.refs_9_), channel_id=1, source_target_pairs={{0,16},{16,0},{32,48},{48,32},{64,80},{80,64},{96,112},{112,96},{1... | collective-permute-start | bytes 884744 | tf_op jit(solution)/shard_map/ppermute | solution.py:304
  62.1 8.0 %collective-permute-start.16 = (bf16[3,384,128]{2,1,0:T(8,128)(2,1)S(1)}, bf16[3,384,128]{2,1,0:T(8,128)(2,1)S(1)}, u32[]{:S(2)}, u32[]{:S(2)}) collective-permute-start(bf16[3,384,128]{2,1,0:T(8,128)(2,1)S(1)} %collective-permute-done.8.refs_4_), channel_id=1, source_target_pairs={{0,32},{16,48},{32,64},{48,80},{64,96},{80,112},{96,0},{112,16},{1... | collective-permute-start | bytes 884744 | tf_op jit(solution)/shard_map/ppermute | solution.py:301
  62.1 1.4 %collective-permute-start.21 = (bf16[1,2,128,256]{3,2,1,0:T(8,128)(2,1)S(1)}, bf16[1,2,128,256]{3,2,1,0:T(8,128)(2,1)S(1)}, u32[]{:S(2)}, u32[]{:S(2)}) collective-permute-start(bf16[1,2,128,256]{3,2,1,0:T(8,128)(2,1)S(1)} %slice.23), channel_id=1, source_target_pairs={{0,16},{16,0},{32,48},{48,32},{64,80},{80,64},{96,112},{112,96},{1... | collective-permute-start | bytes 393224 | tf_op jit(solution)/shard_map/ppermute | solution.py:304
  62.3 1.6 %collective-permute-start.20 = (bf16[1,2,128,256]{3,2,1,0:T(8,128)(2,1)S(1)}, bf16[1,2,128,256]{3,2,1,0:T(8,128)(2,1)S(1)}, u32[]{:S(2)}, u32[]{:S(2)}) collective-permute-start(bf16[1,2,128,256]{3,2,1,0:T(8,128)(2,1)S(1)} %slice.22), channel_id=1, source_target_pairs={{0,16},{16,0},{32,48},{48,32},{64,80},{80,64},{96,112},{112,96},{1... | collective-permute-start | bytes 393224 | tf_op jit(solution)/shard_map/ppermute | solution.py:304
  63.6 6.5 %collective-permute-start.12 = (bf16[3,384,128]{2,1,0:T(8,128)(2,1)S(1)}, bf16[3,384,128]{2,1,0:T(8,128)(2,1)S(1)}, u32[]{:S(2)}, u32[]{:S(2)}) collective-permute-start(bf16[3,384,128]{2,1,0:T(8,128)(2,1)S(1)} %collective-permute-done.9.refs_5_), channel_id=1, source_target_pairs={{0,16},{16,0},{32,48},{48,32},{64,80},{80,64},{96,112},{112,96},{1... | collective-permute-start | bytes 884744 | tf_op jit(solution)/shard_map/ppermute | solution.py:304
  63.8 6.3 %collective-permute-start.14 = (bf16[3,384,128]{2,1,0:T(8,128)(2,1)S(1)}, bf16[3,384,128]{2,1,0:T(8,128)(2,1)S(1)}, u32[]{:S(2)}, u32[]{:S(2)}) collective-permute-start(bf16[3,384,128]{2,1,0:T(8,128)(2,1)S(1)} %collective-permute-done.10.refs_8_), channel_id=1, source_target_pairs={{0,16},{16,0},{32,48},{48,32},{64,80},{80,64},{96,112},{112,96},{1... | collective-permute-start | bytes 884744 | tf_op jit(solution)/shard_map/ppermute | solution.py:304
  66.2 3.9 %collective-permute-start.11 = (bf16[3,384,128]{2,1,0:T(8,128)(2,1)S(1)}, bf16[3,384,128]{2,1,0:T(8,128)(2,1)S(1)}, u32[]{:S(2)}, u32[]{:S(2)}) collective-permute-start(bf16[3,384,128]{2,1,0:T(8,128)(2,1)S(1)} %collective-permute-done.8.refs_4_), channel_id=1, source_target_pairs={{0,16},{16,0},{32,48},{48,32},{64,80},{80,64},{96,112},{112,96},{1... | collective-permute-start | bytes 884744 | tf_op jit(solution)/shard_map/ppermute | solution.py:304
  66.2 3.9 %collective-permute-start.19 = (bf16[3,384,128]{2,1,0:T(8,128)(2,1)S(1)}, bf16[3,384,128]{2,1,0:T(8,128)(2,1)S(1)}, u32[]{:S(2)}, u32[]{:S(2)}) collective-permute-start(bf16[3,384,128]{2,1,0:T(8,128)(2,1)S(1)} %collective-permute-done.17.refs_13_), channel_id=1, source_target_pairs={{0,16},{16,0},{32,48},{48,32},{64,80},{80,64},{96,112},{112,96},{1... | collective-permute-start | bytes 884744 | tf_op jit(solution)/shard_map/ppermute | solution.py:304
  70.1 1.6 %collective-permute-start.18 = (bf16[3,384,128]{2,1,0:T(8,128)(2,1)S(1)}, bf16[3,384,128]{2,1,0:T(8,128)(2,1)S(1)}, u32[]{:S(2)}, u32[]{:S(2)}) collective-permute-start(bf16[3,384,128]{2,1,0:T(8,128)(2,1)S(1)} %collective-permute-done.16.refs_12_), channel_id=1, source_target_pairs={{0,16},{16,0},{32,48},{48,32},{64,80},{80,64},{96,112},{112,96},{1... | collective-permute-start | bytes 884744 | tf_op jit(solution)/shard_map/ppermute | solution.py:304
  (1 other events, 9.7 us)

commit v5 on v4

--- a/solution.py
+++ b/solution.py
@@ -13,7 +13,7 @@
 NFFT = 2048
 TAPS = 4
 AHEAD = 2
-WIDE_VMEM = 62 * 1024 * 1024
+FILTER_VMEM = 50 * 1024 * 1024
 NT = (((1,), (1,)), ((), ()))
 
 
@@ -30,20 +30,13 @@
     full = (coeffs[:, None, :] * rows[None]).reshape(TAPS * 2 * channels, NFFT)
     high = full.astype(ml_dtypes.bfloat16)
     low = (full - high.astype(np.float64)).astype(ml_dtypes.bfloat16)
-    return high, low
-
-
-def frame_loop(
-    tables_hbm, volts_hbm, tables, frames, table_sems, frame_sems, total_ref, first, extra
-):
+    return np.concatenate([high, low], axis=0)
+
+
+def frame_loop(table, volts_hbm, frames, frame_sems, total_ref, first, extra):
+    half = table.shape[0] // 2
     count = frames.shape[0]
     rows = total_ref.shape[1]
-
-    table_copies = [
-        pltpu.make_async_copy(source, target, table_sems.at[i])
-        for i, (source, target) in enumerate(zip(tables_hbm, tables))
-    ]
-    high, low = tables
 
     def frame_copy(i):
         at = pl.multiple_of((first + i) * NFFT, NFFT)
@@ -51,14 +44,8 @@
             volts_hbm.at[:, pl.ds(at, NFFT)], frames.at[i], frame_sems.at[i]
         )
 
-    for copy in table_copies:
-        copy.start()
     for i in range(AHEAD):
         frame_copy(i).start()
-    extra(0)
-    for copy in table_copies:
-        copy.wait()
-
     def step(i, _):
         @pl.when(i + AHEAD < count)
         def _():
@@ -66,9 +53,9 @@
 
         frame_copy(i).wait()
         frame = frames[i]
-        product = lax.dot_general(high[...], frame, NT, preferred_element_type=jnp.float32)
+        product = lax.dot_general(table[:half], frame, NT, preferred_element_type=jnp.float32)
         product = product + lax.dot_general(
-            low[...], frame, NT, preferred_element_type=jnp.float32
+            table[half:], frame, NT, preferred_element_type=jnp.float32
         )
         for tap in range(TAPS):
             at = i + TAPS - 1 - tap
@@ -80,21 +67,19 @@
 
 
 def last_frames_kernel(
-    first, high_hbm, low_hbm, volts_hbm, own_ref, next_ref,
-    total, high, low, frames, table_sems, frame_sems,
+    first, table, volts_hbm, own_ref, next_ref, total, frames, frame_sems
 ):
     total[...] = jnp.zeros_like(total)
     frame_loop(
-        (high_hbm, low_hbm), volts_hbm, (high, low), frames, table_sems, frame_sems,
-        total, first, lambda i: None,
+        table, volts_hbm, frames, frame_sems, total, first, lambda i: None
     )
     own_ref[...] = total[: TAPS - 1]
     next_ref[...] = total[TAPS - 1 :]
 
 
 def first_frames_kernel(
-    allocation_hbm, high_hbm, low_hbm, volts_hbm, last_ref, carry_ref, out_ref,
-    total, hot, spectra, allocation_ref, allocation_sem, high, low, frames, table_sems, frame_sems,
+    allocation_hbm, table, volts_hbm, last_ref, carry_ref, out_ref,
+    total, hot, spectra, allocation_ref, allocation_sem, frames, frame_sems,
 ):
     allocation_copy = pltpu.make_async_copy(allocation_hbm, allocation_ref, allocation_sem)
     allocation_copy.start()
@@ -127,8 +112,7 @@
         ).astype(jnp.bfloat16)
 
     frame_loop(
-        (high_hbm, low_hbm), volts_hbm, (high, low), frames, table_sems, frame_sems,
-        total, 0, choose,
+        table, volts_hbm, frames, frame_sems, total, 0, choose
     )
     for t in range(count):
         spectra[pl.ds(t * rows, rows)] = total[t].astype(jnp.bfloat16)
@@ -143,10 +127,9 @@
     lax.fori_loop(0, owners // 8, write, 0)
 
 
-def filter_scratch(tables, feeds, count):
-    return [pltpu.VMEM(table.shape, table.dtype) for table in tables] + [
+def filter_scratch(feeds, count):
+    return [
         pltpu.VMEM((count, feeds, NFFT), jnp.bfloat16),
-        pltpu.SemaphoreType.DMA((2,)),
         pltpu.SemaphoreType.DMA((count,)),
     ]
 
@@ -292,8 +275,8 @@
     beams = beam_weights.shape[1]
     share = beams // devices
     f32, bf16 = jnp.float32, jnp.bfloat16
-    tables = [jnp.asarray(x) for x in tap_transform(channels)]
-    frame_flops = 4 * tables[0].shape[0] * feeds_dev * NFFT
+    table = jnp.asarray(tap_transform(channels))
+    frame_flops = 2 * table.shape[0] * feeds_dev * NFFT
     anywhere = pl.BlockSpec(memory_space=pl.ANY)
     in_vmem = pl.BlockSpec(memory_space=pltpu.VMEM)
 
@@ -306,16 +289,16 @@
     own_last, next_first = pl.pallas_call(
         functools.partial(last_frames_kernel, early),
         out_shape=[jax.ShapeDtypeStruct((late, rows, feeds_dev), f32)] * 2,
-        in_specs=[anywhere] * 3,
+        in_specs=[in_vmem, anywhere],
         out_specs=[in_vmem, in_vmem],
         scratch_shapes=[pltpu.VMEM((2 * late, rows, feeds_dev), f32)]
-        + filter_scratch(tables, feeds_dev, late),
-        compiler_params=pltpu.CompilerParams(vmem_limit_bytes=WIDE_VMEM),
+        + filter_scratch(feeds_dev, late),
+        compiler_params=pltpu.CompilerParams(vmem_limit_bytes=FILTER_VMEM),
         cost_estimate=pl.CostEstimate(
             flops=late * frame_flops, bytes_accessed=late * feeds_dev * NFFT * 2, transcendentals=0
         ),
         name="last_frames",
-    )(*tables, volts)
+    )(table, volts)
     carry = lax.ppermute(next_first, "freq", [(i, i + 1) for i in range(owners - 1)])
     ordered = pl.pallas_call(
         order_kernel,
@@ -332,7 +315,7 @@
     outgoing = pl.pallas_call(
         first_frames_kernel,
         out_shape=jax.ShapeDtypeStruct((chosen_rows, feeds_dev), bf16),
-        in_specs=[anywhere] * 4 + [in_vmem] * 2,
+        in_specs=[anywhere, in_vmem, anywhere, in_vmem, in_vmem],
         out_specs=in_vmem,
         scratch_shapes=[
             pltpu.VMEM((frames_dev, rows, feeds_dev), f32),
@@ -341,13 +324,13 @@
             pltpu.SMEM((slots_dev, owners), jnp.int32),
             pltpu.SemaphoreType.DMA,
         ]
-        + filter_scratch(tables, feeds_dev, early),
-        compiler_params=pltpu.CompilerParams(vmem_limit_bytes=WIDE_VMEM),
+        + filter_scratch(feeds_dev, early),
+        compiler_params=pltpu.CompilerParams(vmem_limit_bytes=FILTER_VMEM),
         cost_estimate=pl.CostEstimate(
             flops=early * frame_flops, bytes_accessed=early * feeds_dev * NFFT * 2, transcendentals=0
         ),
         name="first_frames",
-    )(allocation.T, *tables, volts, own_last, carry)
+    )(allocation.T, table, volts, own_last, carry)
     outgoing, weights[3] = lax.optimization_barrier((outgoing, weights[3]))
     received = lax.all_to_all(
         outgoing.reshape(owners, slots_dev, 2 * frames_dev, feeds_dev),

time: 79.8 us -> 77.8 us (0.975)
  Pallas kernels: 25.8 us -> 22.1 us
  local copies, waits for them, and re-layouts: 0.19 us -> 1.78 us
    pallas_call x1, Pallas kernels: 12.1 us -> 10.3 us  [shards(): pl.pallas_call(first_frames_kernel, out_shape=jax.ShapeDtypeStruct((chose...]
    unnamed x4 -> x8, local copies, waits for them, and re-layouts: 0.01 us -> 1.6 us
    pallas_call x1, Pallas kernels: 5.03 us -> 3.65 us  [shards(): pl.pallas_call(functools.partial(last_frames_kernel, early), out_shape=[j...]
  transfers between devices with their start and end apart: 23 -> 23, of which waited for: 11 -> 11; matrix products, arithmetic and copies ran while one was open for 0% -> 0% of each run, Pallas kernels for 18% -> 15%
where the time goes in v5:
time: 77.8 us; the launch traced here: 76.5 us
  starting transfers between devices  27.5 us (35%)
  waiting for transfers between devices  24.1 us (31%)
  Pallas kernels  22.1 us (28%)
  local copies, waits for them, and re-layouts  1.78 us (2%)
  between operations  0.97 us (1%)
    ppermute x9, waiting for transfers between devices, moved(): lax.ppermute(x, 'feed', [(i, (i + by) % devices) for i in range(devices)])  17.9 us
    ppermute x9, starting transfers between devices, moved(): lax.ppermute(x, 'feed', [(i, (i + by) % devices) for i in range(devices)])  13.1 us
    pallas_call x1, Pallas kernels, shards(): pl.pallas_call(first_frames_kernel, out_shape=jax.ShapeDtypeStruct((chose...  10.3 us
    all_to_all x1, starting transfers between devices, shards(): lax.all_to_all(outgoing.reshape(owners, slots_dev, 2 * frames_dev, feeds_...  7.85 us
    pallas_call x1, Pallas kernels, gather_call(): pl.pallas_call(functools.partial(gather_kernel, behind, half, scale), out...  6.69 us
    ppermute x1, starting transfers between devices, shards(): lax.ppermute(next_first, 'freq', [(i, i + 1) for i in range(owners - 1)])  3.92 us
    pallas_call x1, Pallas kernels, shards(): pl.pallas_call(functools.partial(last_frames_kernel, early), out_shape=[j...  3.65 us
    ppermute x12, waiting for transfers between devices, swapped(): return lax.ppermute(x, 'feed', [(i, i ^ 1) for i in range(devices)])  3.15 us
  transfers between devices with their start and end apart: 23, of which 11 were waited for; matrix products, arithmetic and copies ran while one was open for 0% of the time, Pallas kernels for 15%

profile of v5, /device:TPU:0, one launch (start us, length us, event | category | flops | bytes accessed | tf_op | source)
XLA Modules:
  0.0 76.5 jit_solution(4653970619435083820)
XLA Ops:
  0.6 1.6 %copy-done = bf16[512,2048]{1,0:T(8,128)(2,1)S(1)} copy-done((bf16[512,2048]{1,0:T(8,128)(2,1)S(1)}, bf16[512,2048]{1,0:T(8,128)(2,1)}, u32[]{:S(2)}) %copy-start) | copy-done | bytes 2097176
  2.2 3.6 %last_frames.1 = (f32[3,64,256]{2,1,0:T(8,128)S(1)}, f32[3,64,256]{2,1,0:T(8,128)S(1)}) custom-call(bf16[512,2048]{1,0:T(8,128)(2,1)S(1)} %copy-done, bf16[256,24576]{1,0:T(8,128)(2,1)} %volts_hbm.3), custom_call_target="tpu_custom_call" | custom-call | flops 1610612736 | bytes 3145728 | tf_op jit(solution)/shard_map/last_frames/pallas_call | solution.py:289
  5.9 3.9 %collective-permute-start = (f32[3,64,256]{2,1,0:T(8,128)S(1)}, f32[3,64,256]{2,1,0:T(8,128)S(1)}, u32[]{:S(2)}, u32[]{:S(2)}) collective-permute-start(f32[3,64,256]{2,1,0:T(8,128)S(1)} %get-tuple-element.32), channel_id=1, source_target_pairs={{0,1},{1,2},{2,3},{3,4},{4,5},{5,6},{6,7},{7,8},{8,9},{9,10},{10,1... | collective-permute-start | bytes 589832 | tf_op jit(solution)/shard_map/ppermute | solution.py:302
  9.8 1.4 %order_beams.1 = (bf16[2,2,128,256]{3,2,1,0:T(8,128)(2,1)S(1)}, bf16[2,2,128,256]{3,2,1,0:T(8,128)(2,1)S(1)}, bf16[2,2,128,256]{3,2,1,0:T(8,128)(2,1)S(1)}, bf16[2,2,128,256]{3,2,1,0:T(8,128)(2,1)S(1)}) custom-call(s32[8,128]{1,0:T(8,128)S(1)} %bitcast.6, bf16[2,1024,256]{2,1,0:T(8,128)(2,1)S(1)} %copy-done.1), custom_call_target="tpu_custom_call" | custom-call | flops 1073741824 | bytes 1048576 | tf_op jit(solution)/shard_map/order_beams/pallas_call | solution.py:303
  11.3 3.3 %collective-permute-start.1 = (bf16[2,2,128,256]{3,2,1,0:T(8,128)(2,1)S(1)}, bf16[2,2,128,256]{3,2,1,0:T(8,128)(2,1)S(1)}, u32[]{:S(2)}, u32[]{:S(2)}) collective-permute-start(bf16[2,2,128,256]{3,2,1,0:T(8,128)(2,1)S(1)} %get-tuple-element.33), channel_id=1, source_target_pairs={{0,64},{16,80},{32,96},{48,112},{64,0},{80,16},{96,32},{112,48},{1... | collective-permute-start | bytes 786440 | tf_op jit(solution)/shard_map/ppermute | solution.py:284
  14.6 10.3 %first_frames.1 = bf16[1152,256]{1,0:T(8,128)(2,1)} custom-call(s32[3,16]{1,0:T(4,128)S(1)} %bitcast.7, bf16[512,2048]{1,0:T(8,128)(2,1)S(1)} %copy-done, bf16[256,24576]{1,0:T(8,128)(2,1)} %volts_hbm.3, f32[3,64,256]{2,1,0:T(8,128)S(1)} %get-tuple-element.31.last_ref, f32[3,64,256]{2,1,0:T(8,128)S(1)} %collective-permute-done.carry_ref), custom_call_target="tpu_custom_call" | custom-call | flops 4831838208 | bytes 9437184 | tf_op jit(solution)/shard_map/first_frames/pallas_call | solution.py:315
  24.9 7.8 %all-to-all-start = ((bf16[16,3,24,256]{3,2,1,0:T(8,128)(2,1)}), bf16[16,3,24,256]{3,2,1,0:T(8,128)(2,1)S(1)}, u32[]{:S(2)}, u32[]{:S(2)}) async-start(bf16[16,3,24,256]{3,2,1,0:T(8,128)(2,1)} %bitcast.2), calls=%async_computation | async-start | bytes 1179648 | tf_op jit(solution)/shard_map/all_to_all | solution.py:335
  32.8 1.6 %collective-permute-start.2 = (bf16[2,2,128,256]{3,2,1,0:T(8,128)(2,1)S(1)}, bf16[2,2,128,256]{3,2,1,0:T(8,128)(2,1)S(1)}, u32[]{:S(2)}, u32[]{:S(2)}) collective-permute-start(bf16[2,2,128,256]{3,2,1,0:T(8,128)(2,1)S(1)} %get-tuple-element.35), channel_id=1, source_target_pairs={{0,32},{16,48},{32,64},{48,80},{64,96},{80,112},{96,0},{112,16},{1... | collective-permute-start | bytes 786440 | tf_op jit(solution)/shard_map/ppermute | solution.py:284
  34.4 1.7 %collective-permute-start.3 = (bf16[2,2,128,256]{3,2,1,0:T(8,128)(2,1)S(1)}, bf16[2,2,128,256]{3,2,1,0:T(8,128)(2,1)S(1)}, u32[]{:S(2)}, u32[]{:S(2)}) collective-permute-start(bf16[2,2,128,256]{3,2,1,0:T(8,128)(2,1)S(1)} %get-tuple-element.36), channel_id=1, source_target_pairs={{0,96},{16,112},{32,0},{48,16},{64,32},{80,48},{96,64},{112,80},{1... | collective-permute-start | bytes 786440 | tf_op jit(solution)/shard_map/ppermute | solution.py:284
  36.2 0.6 collective-permute-start.5
  36.8 0.7 collective-permute-done.4.refs_17_
  37.5 3.5 %collective-permute-done.2.refs_18_ = bf16[2,2,128,256]{3,2,1,0:T(8,128)(2,1)S(1)} collective-permute-done((bf16[2,2,128,256]{3,2,1,0:T(8,128)(2,1)S(1)}, bf16[2,2,128,256]{3,2,1,0:T(8,128)(2,1)S(1)}, u32[]{:S(2)}, u32[]{:S(2)}) %collective-permute-start.2) | collective-permute-done | bytes 262176 | tf_op jit(solution)/shard_map/ppermute | solution.py:284
  41.0 3.1 %all-to-all-done = bf16[16,3,24,256]{3,2,1,0:T(8,128)(2,1)S(1)} async-done(((bf16[16,3,24,256]{3,2,1,0:T(8,128)(2,1)}), bf16[16,3,24,256]{3,2,1,0:T(8,128)(2,1)S(1)}, u32[]{:S(2)}, u32[]{:S(2)}) %all-to-all-start) | async-done | bytes 589856 | tf_op jit(solution)/shard_map/all_to_all | solution.py:335
  44.3 3.0 %collective-permute-start.13 = (bf16[3,384,128]{2,1,0:T(8,128)(2,1)S(1)}, bf16[3,384,128]{2,1,0:T(8,128)(2,1)S(1)}, u32[]{:S(2)}, u32[]{:S(2)}) collective-permute-start(bf16[3,384,128]{2,1,0:T(8,128)(2,1)S(1)} %get-tuple-element.50.refs_1_), channel_id=1, source_target_pairs={{0,96},{16,112},{32,0},{48,16},{64,32},{80,48},{96,64},{112,80},{1... | collective-permute-start | bytes 884744 | tf_op jit(solution)/shard_map/ppermute | solution.py:284
  47.3 3.2 %collective-permute-start.10 = (bf16[3,384,128]{2,1,0:T(8,128)(2,1)S(1)}, bf16[3,384,128]{2,1,0:T(8,128)(2,1)S(1)}, u32[]{:S(2)}, u32[]{:S(2)}) collective-permute-start(bf16[3,384,128]{2,1,0:T(8,128)(2,1)S(1)} %get-tuple-element.51.refs_0_), channel_id=1, source_target_pairs={{0,96},{16,112},{32,0},{48,16},{64,32},{80,48},{96,64},{112,80},{1... | collective-permute-start | bytes 884744 | tf_op jit(solution)/shard_map/ppermute | solution.py:284
  50.5 3.0 %collective-permute-done.13.refs_9_ = bf16[3,384,128]{2,1,0:T(8,128)(2,1)S(1)} collective-permute-done((bf16[3,384,128]{2,1,0:T(8,128)(2,1)S(1)}, bf16[3,384,128]{2,1,0:T(8,128)(2,1)S(1)}, u32[]{:S(2)}, u32[]{:S(2)}) %collective-permute-start.13) | collective-permute-done | bytes 294944 | tf_op jit(solution)/shard_map/ppermute | solution.py:284
  53.5 3.4 %collective-permute-done.9.refs_5_ = bf16[3,384,128]{2,1,0:T(8,128)(2,1)S(1)} collective-permute-done((bf16[3,384,128]{2,1,0:T(8,128)(2,1)S(1)}, bf16[3,384,128]{2,1,0:T(8,128)(2,1)S(1)}, u32[]{:S(2)}, u32[]{:S(2)}) %collective-permute-start.9) | collective-permute-done | bytes 294944 | tf_op jit(solution)/shard_map/ppermute | solution.py:284
  57.4 2.6 %collective-permute-done.8.refs_4_ = bf16[3,384,128]{2,1,0:T(8,128)(2,1)S(1)} collective-permute-done((bf16[3,384,128]{2,1,0:T(8,128)(2,1)S(1)}, bf16[3,384,128]{2,1,0:T(8,128)(2,1)S(1)}, u32[]{:S(2)}, u32[]{:S(2)}) %collective-permute-start.8) | collective-permute-done | bytes 294944 | tf_op jit(solution)/shard_map/ppermute | solution.py:284
  60.2 0.6 collective-permute-start.20
  60.8 0.7 collective-permute-done.21.refs_21_
  62.1 2.0 %collective-permute-done.17.refs_13_ = bf16[3,384,128]{2,1,0:T(8,128)(2,1)S(1)} collective-permute-done((bf16[3,384,128]{2,1,0:T(8,128)(2,1)S(1)}, bf16[3,384,128]{2,1,0:T(8,128)(2,1)S(1)}, u32[]{:S(2)}, u32[]{:S(2)}) %collective-permute-start.17) | collective-permute-done | bytes 294944 | tf_op jit(solution)/shard_map/ppermute | solution.py:284
  64.6 3.4 %collective-permute-done.16.refs_12_ = bf16[3,384,128]{2,1,0:T(8,128)(2,1)S(1)} collective-permute-done((bf16[3,384,128]{2,1,0:T(8,128)(2,1)S(1)}, bf16[3,384,128]{2,1,0:T(8,128)(2,1)S(1)}, u32[]{:S(2)}, u32[]{:S(2)}) %collective-permute-start.16) | collective-permute-done | bytes 294944 | tf_op jit(solution)/shard_map/ppermute | solution.py:284
  68.1 1.5 %collective-permute-done.18.refs_14_ = bf16[3,384,128]{2,1,0:T(8,128)(2,1)S(1)} collective-permute-done((bf16[3,384,128]{2,1,0:T(8,128)(2,1)S(1)}, bf16[3,384,128]{2,1,0:T(8,128)(2,1)S(1)}, u32[]{:S(2)}, u32[]{:S(2)}) %collective-permute-start.18) | collective-permute-done | bytes 294944 | tf_op jit(solution)/shard_map/ppermute | solution.py:287
  69.6 6.7 %gathered.1 = (f32[3,2,256,2048]{3,2,1,0:T(8,128)}, f32[3,128]{1,0:T(4,128)}) custom-call(bf16[3,384,128]{2,1,0:T(8,128)(2,1)S(1)} %get-tuple-element.51.refs_0_, bf16[3,384,128]{2,1,0:T(8,128)(2,1)S(1)} %get-tuple-element.50.refs_1_, bf16[3,384,128]{2,1,0:T(8,128)(2,1)S(1)} %collective-permute-done.6.refs_2_, ...), custom_call_target="tpu_custom_call" | custom-call | flops 3623878656 | bytes 14352384 | tf_op jit(solution)/shard_map/gathered/pallas_call | solution.py:244
  (40 shorter events, 2.1 us)
Async XLA Ops:
  2.2 12.3 %copy-start.3 = (s32[16,3]{0,1:T(4,128)S(1)}, s32[16,3]{0,1:T(4,128)}, u32[]{:S(2)}) copy-start(s32[16,3]{0,1:T(4,128)} %param.7) | copy-start | bytes 580
  5.9 8.7 %collective-permute-start = (f32[3,64,256]{2,1,0:T(8,128)S(1)}, f32[3,64,256]{2,1,0:T(8,128)S(1)}, u32[]{:S(2)}, u32[]{:S(2)}) collective-permute-start(f32[3,64,256]{2,1,0:T(8,128)S(1)} %get-tuple-element.32), channel_id=1, source_target_pairs={{0,1},{1,2},{2,3},{3,4},{4,5},{5,6},{6,7},{7,8},{8,9},{9,10},{10,1... | collective-permute-start | bytes 589832 | tf_op jit(solution)/shard_map/ppermute | solution.py:302
  11.3 13.6 %collective-permute-start.1 = (bf16[2,2,128,256]{3,2,1,0:T(8,128)(2,1)S(1)}, bf16[2,2,128,256]{3,2,1,0:T(8,128)(2,1)S(1)}, u32[]{:S(2)}, u32[]{:S(2)}) collective-permute-start(bf16[2,2,128,256]{3,2,1,0:T(8,128)(2,1)S(1)} %get-tuple-element.33), channel_id=1, source_target_pairs={{0,64},{16,80},{32,96},{48,112},{64,0},{80,16},{96,32},{112,48},{1... | collective-permute-start | bytes 786440 | tf_op jit(solution)/shard_map/ppermute | solution.py:284
  24.9 19.2 %all-to-all-start = ((bf16[16,3,24,256]{3,2,1,0:T(8,128)(2,1)}), bf16[16,3,24,256]{3,2,1,0:T(8,128)(2,1)S(1)}, u32[]{:S(2)}, u32[]{:S(2)}) async-start(bf16[16,3,24,256]{3,2,1,0:T(8,128)(2,1)} %bitcast.2), calls=%async_computation | async-start | bytes 1179648 | tf_op jit(solution)/shard_map/all_to_all | solution.py:335
  32.8 8.2 %collective-permute-start.2 = (bf16[2,2,128,256]{3,2,1,0:T(8,128)(2,1)S(1)}, bf16[2,2,128,256]{3,2,1,0:T(8,128)(2,1)S(1)}, u32[]{:S(2)}, u32[]{:S(2)}) collective-permute-start(bf16[2,2,128,256]{3,2,1,0:T(8,128)(2,1)S(1)} %get-tuple-element.35), channel_id=1, source_target_pairs={{0,32},{16,48},{32,64},{48,80},{64,96},{80,112},{96,0},{112,16},{1... | collective-permute-start | bytes 786440 | tf_op jit(solution)/shard_map/ppermute | solution.py:284
  34.4 6.6 %collective-permute-start.3 = (bf16[2,2,128,256]{3,2,1,0:T(8,128)(2,1)S(1)}, bf16[2,2,128,256]{3,2,1,0:T(8,128)(2,1)S(1)}, u32[]{:S(2)}, u32[]{:S(2)}) collective-permute-start(bf16[2,2,128,256]{3,2,1,0:T(8,128)(2,1)S(1)} %get-tuple-element.36), channel_id=1, source_target_pairs={{0,96},{16,112},{32,0},{48,16},{64,32},{80,48},{96,64},{112,80},{1... | collective-permute-start | bytes 786440 | tf_op jit(solution)/shard_map/ppermute | solution.py:284
  36.1 1.4 %collective-permute-start.4 = (bf16[1,2,128,256]{3,2,1,0:T(8,128)(2,1)S(1)}, bf16[1,2,128,256]{3,2,1,0:T(8,128)(2,1)S(1)}, u32[]{:S(2)}, u32[]{:S(2)}) collective-permute-start(bf16[1,2,128,256]{3,2,1,0:T(8,128)(2,1)S(1)} %slice.18), channel_id=1, source_target_pairs={{0,16},{16,0},{32,48},{48,32},{64,80},{80,64},{96,112},{112,96},{1... | collective-permute-start | bytes 393224 | tf_op jit(solution)/shard_map/ppermute | solution.py:287
  36.2 4.8 %collective-permute-start.5 = (bf16[1,2,128,256]{3,2,1,0:T(8,128)(2,1)S(1)}, bf16[1,2,128,256]{3,2,1,0:T(8,128)(2,1)S(1)}, u32[]{:S(2)}, u32[]{:S(2)}) collective-permute-start(bf16[1,2,128,256]{3,2,1,0:T(8,128)(2,1)S(1)} %slice.19), channel_id=1, source_target_pairs={{0,16},{16,0},{32,48},{48,32},{64,80},{80,64},{96,112},{112,96},{1... | collective-permute-start | bytes 393224 | tf_op jit(solution)/shard_map/ppermute | solution.py:287
  44.3 9.2 %collective-permute-start.13 = (bf16[3,384,128]{2,1,0:T(8,128)(2,1)S(1)}, bf16[3,384,128]{2,1,0:T(8,128)(2,1)S(1)}, u32[]{:S(2)}, u32[]{:S(2)}) collective-permute-start(bf16[3,384,128]{2,1,0:T(8,128)(2,1)S(1)} %get-tuple-element.50.refs_1_), channel_id=1, source_target_pairs={{0,96},{16,112},{32,0},{48,16},{64,32},{80,48},{96,64},{112,80},{1... | collective-permute-start | bytes 884744 | tf_op jit(solution)/shard_map/ppermute | solution.py:284
  47.3 9.6 %collective-permute-start.9 = (bf16[3,384,128]{2,1,0:T(8,128)(2,1)S(1)}, bf16[3,384,128]{2,1,0:T(8,128)(2,1)S(1)}, u32[]{:S(2)}, u32[]{:S(2)}) collective-permute-start(bf16[3,384,128]{2,1,0:T(8,128)(2,1)S(1)} %get-tuple-element.50.refs_1_), channel_id=1, source_target_pairs={{0,32},{16,48},{32,64},{48,80},{64,96},{80,112},{96,0},{112,16},{1... | collective-permute-start | bytes 884744 | tf_op jit(solution)/shard_map/ppermute | solution.py:284
  47.3 9.9 %collective-permute-start.10 = (bf16[3,384,128]{2,1,0:T(8,128)(2,1)S(1)}, bf16[3,384,128]{2,1,0:T(8,128)(2,1)S(1)}, u32[]{:S(2)}, u32[]{:S(2)}) collective-permute-start(bf16[3,384,128]{2,1,0:T(8,128)(2,1)S(1)} %get-tuple-element.51.refs_0_), channel_id=1, source_target_pairs={{0,96},{16,112},{32,0},{48,16},{64,32},{80,48},{96,64},{112,80},{1... | collective-permute-start | bytes 884744 | tf_op jit(solution)/shard_map/ppermute | solution.py:284
  50.5 9.5 %collective-permute-start.8 = (bf16[3,384,128]{2,1,0:T(8,128)(2,1)S(1)}, bf16[3,384,128]{2,1,0:T(8,128)(2,1)S(1)}, u32[]{:S(2)}, u32[]{:S(2)}) collective-permute-start(bf16[3,384,128]{2,1,0:T(8,128)(2,1)S(1)} %get-tuple-element.51.refs_0_), channel_id=1, source_target_pairs={{0,32},{16,48},{32,64},{48,80},{64,96},{80,112},{96,0},{112,16},{1... | collective-permute-start | bytes 884744 | tf_op jit(solution)/shard_map/ppermute | solution.py:284
  50.5 9.5 %collective-permute-start.7 = (bf16[3,384,128]{2,1,0:T(8,128)(2,1)S(1)}, bf16[3,384,128]{2,1,0:T(8,128)(2,1)S(1)}, u32[]{:S(2)}, u32[]{:S(2)}) collective-permute-start(bf16[3,384,128]{2,1,0:T(8,128)(2,1)S(1)} %get-tuple-element.50.refs_1_), channel_id=1, source_target_pairs={{0,16},{16,0},{32,48},{48,32},{64,80},{80,64},{96,112},{112,96},{1... | collective-permute-start | bytes 884744 | tf_op jit(solution)/shard_map/ppermute | solution.py:287
  53.5 6.7 %collective-permute-start.6 = (bf16[3,384,128]{2,1,0:T(8,128)(2,1)S(1)}, bf16[3,384,128]{2,1,0:T(8,128)(2,1)S(1)}, u32[]{:S(2)}, u32[]{:S(2)}) collective-permute-start(bf16[3,384,128]{2,1,0:T(8,128)(2,1)S(1)} %get-tuple-element.51.refs_0_), channel_id=1, source_target_pairs={{0,16},{16,0},{32,48},{48,32},{64,80},{80,64},{96,112},{112,96},{1... | collective-permute-start | bytes 884744 | tf_op jit(solution)/shard_map/ppermute | solution.py:287
  56.9 7.2 %collective-permute-start.17 = (bf16[3,384,128]{2,1,0:T(8,128)(2,1)S(1)}, bf16[3,384,128]{2,1,0:T(8,128)(2,1)S(1)}, u32[]{:S(2)}, u32[]{:S(2)}) collective-permute-start(bf16[3,384,128]{2,1,0:T(8,128)(2,1)S(1)} %collective-permute-done.13.refs_9_), channel_id=1, source_target_pairs={{0,96},{16,112},{32,0},{48,16},{64,32},{80,48},{96,64},{112,80},{1... | collective-permute-start | bytes 884744 | tf_op jit(solution)/shard_map/ppermute | solution.py:284
  57.2 6.9 %collective-permute-start.15 = (bf16[3,384,128]{2,1,0:T(8,128)(2,1)S(1)}, bf16[3,384,128]{2,1,0:T(8,128)(2,1)S(1)}, u32[]{:S(2)}, u32[]{:S(2)}) collective-permute-start(bf16[3,384,128]{2,1,0:T(8,128)(2,1)S(1)} %collective-permute-done.13.refs_9_), channel_id=1, source_target_pairs={{0,16},{16,0},{32,48},{48,32},{64,80},{80,64},{96,112},{112,96},{1... | collective-permute-start | bytes 884744 | tf_op jit(solution)/shard_map/ppermute | solution.py:287
  60.1 8.0 %collective-permute-start.16 = (bf16[3,384,128]{2,1,0:T(8,128)(2,1)S(1)}, bf16[3,384,128]{2,1,0:T(8,128)(2,1)S(1)}, u32[]{:S(2)}, u32[]{:S(2)}) collective-permute-start(bf16[3,384,128]{2,1,0:T(8,128)(2,1)S(1)} %collective-permute-done.8.refs_4_), channel_id=1, source_target_pairs={{0,32},{16,48},{32,64},{48,80},{64,96},{80,112},{96,0},{112,16},{1... | collective-permute-start | bytes 884744 | tf_op jit(solution)/shard_map/ppermute | solution.py:284
  60.1 1.4 %collective-permute-start.21 = (bf16[1,2,128,256]{3,2,1,0:T(8,128)(2,1)S(1)}, bf16[1,2,128,256]{3,2,1,0:T(8,128)(2,1)S(1)}, u32[]{:S(2)}, u32[]{:S(2)}) collective-permute-start(bf16[1,2,128,256]{3,2,1,0:T(8,128)(2,1)S(1)} %slice.23), channel_id=1, source_target_pairs={{0,16},{16,0},{32,48},{48,32},{64,80},{80,64},{96,112},{112,96},{1... | collective-permute-start | bytes 393224 | tf_op jit(solution)/shard_map/ppermute | solution.py:287
  60.2 1.6 %collective-permute-start.20 = (bf16[1,2,128,256]{3,2,1,0:T(8,128)(2,1)S(1)}, bf16[1,2,128,256]{3,2,1,0:T(8,128)(2,1)S(1)}, u32[]{:S(2)}, u32[]{:S(2)}) collective-permute-start(bf16[1,2,128,256]{3,2,1,0:T(8,128)(2,1)S(1)} %slice.22), channel_id=1, source_target_pairs={{0,16},{16,0},{32,48},{48,32},{64,80},{80,64},{96,112},{112,96},{1... | collective-permute-start | bytes 393224 | tf_op jit(solution)/shard_map/ppermute | solution.py:287
  61.5 6.5 %collective-permute-start.12 = (bf16[3,384,128]{2,1,0:T(8,128)(2,1)S(1)}, bf16[3,384,128]{2,1,0:T(8,128)(2,1)S(1)}, u32[]{:S(2)}, u32[]{:S(2)}) collective-permute-start(bf16[3,384,128]{2,1,0:T(8,128)(2,1)S(1)} %collective-permute-done.9.refs_5_), channel_id=1, source_target_pairs={{0,16},{16,0},{32,48},{48,32},{64,80},{80,64},{96,112},{112,96},{1... | collective-permute-start | bytes 884744 | tf_op jit(solution)/shard_map/ppermute | solution.py:287
  61.8 6.3 %collective-permute-start.14 = (bf16[3,384,128]{2,1,0:T(8,128)(2,1)S(1)}, bf16[3,384,128]{2,1,0:T(8,128)(2,1)S(1)}, u32[]{:S(2)}, u32[]{:S(2)}) collective-permute-start(bf16[3,384,128]{2,1,0:T(8,128)(2,1)S(1)} %collective-permute-done.10.refs_8_), channel_id=1, source_target_pairs={{0,16},{16,0},{32,48},{48,32},{64,80},{80,64},{96,112},{112,96},{1... | collective-permute-start | bytes 884744 | tf_op jit(solution)/shard_map/ppermute | solution.py:287
  64.1 3.9 %collective-permute-start.11 = (bf16[3,384,128]{2,1,0:T(8,128)(2,1)S(1)}, bf16[3,384,128]{2,1,0:T(8,128)(2,1)S(1)}, u32[]{:S(2)}, u32[]{:S(2)}) collective-permute-start(bf16[3,384,128]{2,1,0:T(8,128)(2,1)S(1)} %collective-permute-done.8.refs_4_), channel_id=1, source_target_pairs={{0,16},{16,0},{32,48},{48,32},{64,80},{80,64},{96,112},{112,96},{1... | collective-permute-start | bytes 884744 | tf_op jit(solution)/shard_map/ppermute | solution.py:287
  64.1 3.9 %collective-permute-start.19 = (bf16[3,384,128]{2,1,0:T(8,128)(2,1)S(1)}, bf16[3,384,128]{2,1,0:T(8,128)(2,1)S(1)}, u32[]{:S(2)}, u32[]{:S(2)}) collective-permute-start(bf16[3,384,128]{2,1,0:T(8,128)(2,1)S(1)} %collective-permute-done.17.refs_13_), channel_id=1, source_target_pairs={{0,16},{16,0},{32,48},{48,32},{64,80},{80,64},{96,112},{112,96},{1... | collective-permute-start | bytes 884744 | tf_op jit(solution)/shard_map/ppermute | solution.py:287
  68.0 1.6 %collective-permute-start.18 = (bf16[3,384,128]{2,1,0:T(8,128)(2,1)S(1)}, bf16[3,384,128]{2,1,0:T(8,128)(2,1)S(1)}, u32[]{:S(2)}, u32[]{:S(2)}) collective-permute-start(bf16[3,384,128]{2,1,0:T(8,128)(2,1)S(1)} %collective-permute-done.16.refs_12_), channel_id=1, source_target_pairs={{0,16},{16,0},{32,48},{48,32},{64,80},{80,64},{96,112},{112,96},{1... | collective-permute-start | bytes 884744 | tf_op jit(solution)/shard_map/ppermute | solution.py:287
  (3 other events, 16.8 us)
